TPU v7x, 128 devices: a whole 4x4x4 slice. The times are simulated.
128 devices in a mesh: ctx: 8 (over x, z_hi), resp: 16 (over z_lo, y, core).
Axes of the slice: x: 4, y: 4, z: 4 (z_hi: 2, z_lo: 2; z = z_hi * 2 + z_lo), core: 2. Of those that a mesh axis runs over, the one named last changes fastest.
Arguments:
- prompt_hidden: bfloat16 [8, 1024, 5120], P('ctx', 'resp'), may hold values from -6 to 6
- prompt_base: bfloat16 [8, 1024, 5120], P('ctx', 'resp'), may hold values from -22 to 22
- reply_hidden: bfloat16 [8, 16, 128, 5120], P('ctx', 'resp'), may hold values from -6 to 6
- reply_base: bfloat16 [8, 16, 128, 5120], P('ctx', 'resp'), may hold values from -22 to 22
- reply_lengths: int32 [8, 16], P('ctx', 'resp'), may hold values from 16 to 128, as said below
- adapter_down: bfloat16 [3, 5120, 16], replicated, may hold values from -0.078125 to 0.078125
- query_up_weight: bfloat16 [16, 4096], replicated, may hold values from -0.75 to 0.75
- key_value_up_weight: bfloat16 [2, 16, 512], replicated, may hold values from -0.75 to 0.75
- output_down: bfloat16 [4096, 16], replicated, may hold values from -0.09375 to 0.09375
- output_up: bfloat16 [16, 5120], replicated, may hold values from -0.75 to 0.75
- prompt_grad_out: bfloat16 [8, 1024, 5120], P('ctx', 'resp'), may hold values from -0.125 to 0.125
- prompt_grad_base: bfloat16 [8, 1024, 4096], P('ctx', 'resp'), may hold values from -0.125 to 0.125
- reply_grad_out: bfloat16 [8, 16, 128, 5120], P('ctx', 'resp'), may hold values from -0.125 to 0.125
- reply_grad_base: bfloat16 [8, 16, 128, 4096], P('ctx', 'resp'), may hold values from -0.125 to 0.125
Outputs:
- prompt_context: bfloat16 [8, 1024, 4096], P('ctx', 'resp')
- reply_context: bfloat16 [8, 16, 128, 4096], P('ctx', 'resp')
- grad_adapter_down: float32 [3, 5120, 16], replicated
- grad_query_up: float32 [16, 4096], replicated
- grad_keyvalue_up: float32 [2, 16, 512], replicated
- grad_output_down: float32 [4096, 16], replicated
- grad_output_up: float32 [16, 5120], replicated
Inputs may be any that keep to these rules, and one draw needn't show every extreme that they name: `reply_lengths`: in each prompt's group one response has all 128 tokens live.
All inputs are finite; a program needn't handle non-finite values.
Results may differ from a plain program's by a relative error of at most 0.023.
Values may be sent and summed in bfloat16 or wider, within the bound.
No kernel may reach another device: no remote copies, remote signals or barrier semaphores. Data moves between devices by JAX's collectives and lax.ppermute only.
A program may use at most 128 MiB of HBM per device.

v0:
```python
import jax
import jax.numpy as jnp
from jax import lax
from jax.sharding import PartitionSpec as P

HEAD_DIM = 128


ADAPTER_SCALE = 2.0
ROPE_BASE = 1000000.0
HIGHEST_ACCURACY = lax.Precision.HIGHEST


def apply_rotary(values, token_positions, sign):
    count = values.shape[0]
    heads = values.shape[1] // HEAD_DIM
    middle = HEAD_DIM // 2
    rates = ROPE_BASE ** (-(jnp.arange(middle, dtype=jnp.float32) * (2.0 / HEAD_DIM)))
    angle = token_positions.astype(jnp.float32)[:, None] * rates[None, :]
    cosine = jnp.cos(angle)
    sine = jnp.sin(angle) * sign
    cosine = jnp.concatenate([cosine, cosine], axis=1)[:, None, :]
    sine = jnp.concatenate([sine, sine], axis=1)[:, None, :]
    shaped = values.reshape(count, heads, HEAD_DIM)
    turned = jnp.concatenate([-shaped[:, :, middle:], shaped[:, :, :middle]], axis=2)
    return (shaped * cosine + turned * sine).reshape(count, heads * HEAD_DIM)


def project(
    hidden_input, base, token_positions, adapter_down, query_up_weight, key_value_up_weight
):
    width_q = query_up_weight.shape[1]
    width_kv = key_value_up_weight.shape[2]
    reduced_product = jnp.einsum(
        "td,jdr->jtr", hidden_input, adapter_down, preferred_element_type=jnp.float32
    ).astype(jnp.bfloat16)
    low_rank_query = reduced_product[0]
    low_rank_key = reduced_product[1]
    low_rank_value = reduced_product[2]
    frozen_query_weight = base[:, :width_q].astype(jnp.float32)
    frozen_key_weight = base[:, width_q : width_q + width_kv].astype(jnp.float32)
    frozen_value_weight = base[:, width_q + width_kv :].astype(jnp.float32)
    query_vectors = apply_rotary(
        frozen_query_weight
        + ADAPTER_SCALE
        * jnp.dot(low_rank_query, query_up_weight, preferred_element_type=jnp.float32),
        token_positions,
        1.0,
    ).astype(jnp.bfloat16)
    key_matrix_rows = apply_rotary(
        frozen_key_weight
        + ADAPTER_SCALE
        * jnp.dot(low_rank_key, key_value_up_weight[0], preferred_element_type=jnp.float32),
        token_positions,
        1.0,
    ).astype(jnp.bfloat16)
    value_matrix_rows = (
        frozen_value_weight
        + ADAPTER_SCALE
        * jnp.dot(low_rank_value, key_value_up_weight[1], preferred_element_type=jnp.float32)
    ).astype(jnp.bfloat16)
    return (
        query_vectors,
        key_matrix_rows,
        value_matrix_rows,
        (low_rank_query, low_rank_key, low_rank_value),
    )


def output_back(grad_out, grad_base, live, output_down, output_up):
    incoming_gradient = jnp.where(live[:, None], grad_out, jnp.zeros_like(grad_out))
    incoming_base_gradient = jnp.where(live[:, None], grad_base, jnp.zeros_like(grad_base))
    reduced_product = jnp.dot(incoming_gradient, output_up.T, preferred_element_type=jnp.float32)
    broadcast_heads = jnp.dot(
        reduced_product, output_down.astype(jnp.float32).T, precision=HIGHEST_ACCURACY
    )
    backward_step = (
        incoming_base_gradient.astype(jnp.float32) + ADAPTER_SCALE * broadcast_heads
    ).astype(jnp.bfloat16)
    return (incoming_gradient, reduced_product, backward_step)


def attend(query_vectors, backward_step, keys, values, allowed, live):
    rows = query_vectors.shape[0]
    count = keys.shape[0]
    groups = keys.shape[1] // HEAD_DIM
    share = query_vectors.shape[1] // keys.shape[1]
    scale = HEAD_DIM ** (-0.5)

    def split_heads(array, width):
        return array.reshape(array.shape[0], groups, width).transpose(1, 0, 2)

    def one_group(inputs):
        query_block, push_block, key_head, value_head = inputs
        query_heads = query_block.reshape(rows, share, HEAD_DIM)
        push_heads = push_block.reshape(rows, share, HEAD_DIM)
        scores = (
            jnp.einsum("rgd,kd->rgk", query_heads, key_head, preferred_element_type=jnp.float32)
            * scale
        )
        scores = jnp.where(allowed[:, None, :], scores, -jnp.inf)
        top = jnp.max(scores, axis=2, keepdims=True)
        weight = jnp.exp(scores - top)
        prob = weight / jnp.sum(weight, axis=2, keepdims=True)
        chosen = prob.astype(jnp.bfloat16)
        mixed = jnp.einsum(
            "rgk,kd->rgd", chosen, value_head, preferred_element_type=jnp.float32
        ).astype(jnp.bfloat16)
        mixed = jnp.where(live[:, None, None], mixed, jnp.zeros_like(mixed))
        delta = jnp.sum(
            mixed.astype(jnp.float32) * push_heads.astype(jnp.float32), axis=2, keepdims=True
        )
        dprob = jnp.einsum(
            "rgd,kd->rgk", push_heads, value_head, preferred_element_type=jnp.float32
        )
        dscore = (prob * (dprob - delta)).astype(jnp.bfloat16)
        dquery = (
            jnp.einsum("rgk,kd->rgd", dscore, key_head, preferred_element_type=jnp.float32) * scale
        )
        dkey = (
            jnp.einsum("rgk,rgd->kd", dscore, query_heads, preferred_element_type=jnp.float32)
            * scale
        )
        dvalue = jnp.einsum("rgk,rgd->kd", chosen, push_heads, preferred_element_type=jnp.float32)
        return (
            mixed.reshape(rows, share * HEAD_DIM),
            dquery.reshape(rows, share * HEAD_DIM),
            dkey,
            dvalue,
        )

    stacked = (
        split_heads(query_vectors, share * HEAD_DIM),
        split_heads(backward_step, share * HEAD_DIM),
        split_heads(keys, HEAD_DIM),
        split_heads(values, HEAD_DIM),
    )
    attended_output, dquery, dkey, dvalue = lax.map(one_group, stacked)

    def merge_heads(array, length):
        return array.transpose(1, 0, 2).reshape(length, -1)

    return (
        merge_heads(attended_output, rows),
        merge_heads(dquery, rows),
        merge_heads(dkey, count),
        merge_heads(dvalue, count),
    )


def fold_back(unrotated_input, adapter_out):
    return jnp.dot(unrotated_input, adapter_out.astype(jnp.float32).T, precision=HIGHEST_ACCURACY)


def low_grad(low_rank_state, unrotated_input):
    return ADAPTER_SCALE * jnp.einsum(
        "sg,su->gu", low_rank_state.astype(jnp.float32), unrotated_input, precision=HIGHEST_ACCURACY
    )


def input_grads(hidden_input, fold_q, fold_k, fold_v):
    folded_gradients = jnp.stack([fold_q, fold_k, fold_v])
    return ADAPTER_SCALE * jnp.einsum(
        "gq,xgs->xqs",
        hidden_input.astype(jnp.float32),
        folded_gradients,
        precision=HIGHEST_ACCURACY,
    )


def output_grads(attended_output, reduced_product, incoming_gradient, output_down):
    down_weight_gradient = ADAPTER_SCALE * jnp.einsum(
        "ym,yp->mp",
        attended_output.astype(jnp.float32),
        reduced_product,
        precision=HIGHEST_ACCURACY,
    )
    raised_product = jnp.dot(attended_output, output_down, preferred_element_type=jnp.float32)
    up_weight_gradient = ADAPTER_SCALE * jnp.einsum(
        "cw,cl->wl",
        raised_product,
        incoming_gradient.astype(jnp.float32),
        precision=HIGHEST_ACCURACY,
    )
    return (down_weight_gradient, up_weight_gradient)


def per_device(
    prompt_hidden,
    prompt_base,
    reply_hidden,
    reply_base,
    reply_lengths,
    adapter_down,
    query_up_weight,
    key_value_up_weight,
    output_down,
    output_up,
    prompt_grad_out,
    prompt_grad_base,
    reply_grad_out,
    reply_grad_base,
):
    resp_count = lax.axis_size("resp")
    prompt_rows = prompt_hidden.shape[1]
    reply_len = reply_hidden.shape[2]
    prompt_len = prompt_rows * resp_count
    prompt_places = lax.axis_index("resp") * prompt_rows + jnp.arange(prompt_rows, dtype=jnp.int32)
    all_places = jnp.arange(prompt_len, dtype=jnp.int32)
    token_index = jnp.arange(reply_len, dtype=jnp.int32)
    reply_places = prompt_len + token_index
    live = token_index < reply_lengths[0, 0]
    every = jnp.ones((prompt_rows,), dtype=bool)
    own_hidden = prompt_hidden[0]
    reply_tokens = reply_hidden[0, 0]
    prompt_query, prompt_key, prompt_value, prompt_low = project(
        own_hidden,
        prompt_base[0],
        prompt_places,
        adapter_down,
        query_up_weight,
        key_value_up_weight,
    )
    reply_query, reply_key, reply_value, reply_low = project(
        reply_tokens,
        reply_base[0, 0],
        reply_places,
        adapter_down,
        query_up_weight,
        key_value_up_weight,
    )
    all_keys, all_values = (
        lax.all_gather(prompt_key, "resp", axis=0, tiled=True),
        lax.all_gather(prompt_value, "resp", axis=0, tiled=True),
    )
    prompt_cot, prompt_lowered, prompt_push = output_back(
        prompt_grad_out[0], prompt_grad_base[0], every, output_down, output_up
    )
    prompt_allowed = all_places[None, :] <= prompt_places[:, None]
    prompt_context, prompt_dquery, prompt_dkey, prompt_dvalue = attend(
        prompt_query, prompt_push, all_keys, all_values, prompt_allowed, every
    )
    reply_cot, reply_lowered, reply_push = output_back(
        reply_grad_out[0, 0], reply_grad_base[0, 0], live, output_down, output_up
    )
    joined_keys = jnp.concatenate([all_keys, reply_key], axis=0)
    joined_values = jnp.concatenate([all_values, reply_value], axis=0)
    reply_allowed = jnp.concatenate(
        [
            jnp.ones((reply_len, prompt_len), dtype=bool),
            token_index[None, :] <= token_index[:, None],
        ],
        axis=1,
    )
    reply_context, reply_dquery, joint_dkey, joint_dvalue = attend(
        reply_query, reply_push, joined_keys, joined_values, reply_allowed, live
    )
    part_dkey = prompt_dkey + joint_dkey[:prompt_len]
    part_dvalue = prompt_dvalue + joint_dvalue[:prompt_len]
    own_dvalue = joint_dvalue[prompt_len:]
    mine_dkey, mine_dvalue = (
        lax.psum_scatter(part_dkey, "resp", scatter_dimension=0, tiled=True),
        lax.psum_scatter(part_dvalue, "resp", scatter_dimension=0, tiled=True),
    )
    raw_key = apply_rotary(mine_dkey, prompt_places, -1.0)
    grad_key_up = low_grad(prompt_low[1], raw_key)
    grad_value_up = low_grad(prompt_low[2], mine_dvalue)
    mine_fold_k = fold_back(raw_key, key_value_up_weight[0])
    mine_fold_v = fold_back(mine_dvalue, key_value_up_weight[1])
    prompt_raw_q = apply_rotary(prompt_dquery, prompt_places, -1.0)
    prompt_down = input_grads(
        own_hidden, fold_back(prompt_raw_q, query_up_weight), mine_fold_k, mine_fold_v
    )
    reply_raw_q = apply_rotary(reply_dquery, reply_places, -1.0)
    reply_raw_k = apply_rotary(joint_dkey[prompt_len:], reply_places, -1.0)
    reply_down = input_grads(
        reply_tokens,
        fold_back(reply_raw_q, query_up_weight),
        fold_back(reply_raw_k, key_value_up_weight[0]),
        fold_back(own_dvalue, key_value_up_weight[1]),
    )
    grad_query = low_grad(prompt_low[0], prompt_raw_q) + low_grad(reply_low[0], reply_raw_q)
    grad_key_up = grad_key_up + low_grad(reply_low[1], reply_raw_k)
    grad_value_up = grad_value_up + low_grad(reply_low[2], own_dvalue)
    prompt_out_down, prompt_out_up = output_grads(
        prompt_context, prompt_lowered, prompt_cot, output_down
    )
    reply_out_down, reply_out_up = output_grads(
        reply_context, reply_lowered, reply_cot, output_down
    )
    summed_down, summed_query, summed_pair, summed_out_down, summed_out_up = lax.psum(
        (
            prompt_down + reply_down,
            grad_query,
            jnp.stack([grad_key_up, grad_value_up]),
            prompt_out_down + reply_out_down,
            prompt_out_up + reply_out_up,
        ),
        ("ctx", "resp"),
    )
    return (
        prompt_context[None],
        reply_context[None, None],
        summed_down,
        summed_query,
        summed_pair,
        summed_out_down,
        summed_out_up,
    )


def solution(mesh):
    return jax.shard_map(
        per_device,
        mesh=mesh,
        in_specs=(
            P("ctx", "resp", None),
            P("ctx", "resp", None),
            P("ctx", "resp", None, None),
            P("ctx", "resp", None, None),
            P("ctx", "resp"),
            P(),
            P(),
            P(),
            P(),
            P(),
            P("ctx", "resp", None),
            P("ctx", "resp", None),
            P("ctx", "resp", None, None),
            P("ctx", "resp", None, None),
        ),
        out_specs=(P("ctx", "resp", None), P("ctx", "resp", None, None), P(), P(), P(), P(), P()),
        check_vma=False,
    )
```

profile of v0, /device:TPU:1, one launch (start us, length us, event | category | flops | bytes accessed | tf_op | source)
XLA Modules:
  0.0 560.8 jit_solution(3884135981981930529)
XLA Ops:
  29.5 3.3 fusion.82
  53.7 28.1 %all-gather.3.cloned.1.call-done = bf16[1024,512]{1,0:T(8,128)(2,1)} async-done(((bf16[64,512]{1,0:T(8,128)(2,1)}), bf16[1024,512]{1,0:T(8,128)(2,1)}) %all-gather.3.cloned.1.call-update) | async-done | bytes 1048592 | tf_op jit(solution)/shard_map/all_gather | solution.py:233
  84.3 87.2 %while.35 = (s32[]{:T(128)}, bf16[4,128,1024]{1,2,0:T(8,128)(2,1)}, f32[4,128,1024]{1,2,0:T(8,128)}, f32[4,1152,128]{1,2,0:T(8,128)}, f32[4,1152,128]{1,2,0:T(8,...) while((s32[]{:T(128)}, bf16[4,128,1024]{1,2,0:T(8,128)(2,1)}, ...), condition=%wide.region_9.10_spmd.clone, body=%wide.region_5.9_spmd.clone.sunk | while | flops 1824801024 | bytes 85106592 | solution.py:138
  85.4 5.0 exponential_reduce_fusion.2
  90.4 3.6 fusion.266
  107.2 5.0 exponential_reduce_fusion.2
  112.2 3.6 fusion.266
  129.0 5.0 exponential_reduce_fusion.2
  134.0 3.6 fusion.266
  150.7 5.0 exponential_reduce_fusion.2
  155.8 3.6 fusion.266
  175.2 85.3 %while.34 = (s32[]{:T(128)}, bf16[4,64,1024]{2,1,0:T(8,128)(2,1)}, f32[4,64,1024]{2,0,1:T(4,128)}, f32[4,1024,128]{1,2,0:T(8,128)}, f32[4,1024,128]{1,2,0:T(8,12...) while((s32[]{:T(128)}, bf16[4,64,1024]{2,1,0:T(8,128)(2,1)}, ...), condition=%wide.region_4.5_spmd.clone, body=%wide.region_0.4_spmd.clone.sunk | while | flops 811139584 | bytes 36905944 | solution.py:138
  188.9 5.9 %dynamic_update_slice.56 = f32[4,64,1024]{2,0,1:T(4,128)} dynamic-update-slice(f32[4,64,1024]{2,0,1:T(4,128)} %get-tuple-element.429, f32[1,64,1024]{2,0,1:T(1,128)S(1)} %bitcast.473, s32[]{:T(128)} %get-tuple-element.427, s32[]{:T(128)} %constant.37.clone.1..sunk, s32[]{:T(128)} %constant.37.clone.1..sunk) | dynamic-update-slice | bytes 524292 | tf_op jit(solution)/shard_map/while/body/jit(dynamic_update_index_in_dim)/dynamic_update_slice | solution.py:138
  197.7 3.2 fusion.251
  210.1 5.9 %dynamic_update_slice.56 = f32[4,64,1024]{2,0,1:T(4,128)} dynamic-update-slice(f32[4,64,1024]{2,0,1:T(4,128)} %get-tuple-element.429, f32[1,64,1024]{2,0,1:T(1,128)S(1)} %bitcast.473, s32[]{:T(128)} %get-tuple-element.427, s32[]{:T(128)} %constant.37.clone.1..sunk, s32[]{:T(128)} %constant.37.clone.1..sunk) | dynamic-update-slice | bytes 524292 | tf_op jit(solution)/shard_map/while/body/jit(dynamic_update_index_in_dim)/dynamic_update_slice | solution.py:138
  219.0 3.2 fusion.251
  231.4 5.9 %dynamic_update_slice.56 = f32[4,64,1024]{2,0,1:T(4,128)} dynamic-update-slice(f32[4,64,1024]{2,0,1:T(4,128)} %get-tuple-element.429, f32[1,64,1024]{2,0,1:T(1,128)S(1)} %bitcast.473, s32[]{:T(128)} %get-tuple-element.427, s32[]{:T(128)} %constant.37.clone.1..sunk, s32[]{:T(128)} %constant.37.clone.1..sunk) | dynamic-update-slice | bytes 524292 | tf_op jit(solution)/shard_map/while/body/jit(dynamic_update_index_in_dim)/dynamic_update_slice | solution.py:138
  252.7 5.9 %dynamic_update_slice.56 = f32[4,64,1024]{2,0,1:T(4,128)} dynamic-update-slice(f32[4,64,1024]{2,0,1:T(4,128)} %get-tuple-element.429, f32[1,64,1024]{2,0,1:T(1,128)S(1)} %bitcast.473, s32[]{:T(128)} %get-tuple-element.427, s32[]{:T(128)} %constant.37.clone.1..sunk, s32[]{:T(128)} %constant.37.clone.1..sunk) | dynamic-update-slice | bytes 524292 | tf_op jit(solution)/shard_map/while/body/jit(dynamic_update_index_in_dim)/dynamic_update_slice | solution.py:138
  268.3 4.1 slice_add_fusion
  281.6 4.2 copy.153
  290.1 3.4 multiply_add_fusion
  322.5 4.6 fusion.104
  331.6 57.0 %reduce-scatter.7.cloned.1.call-done = f32[64,512]{1,0:T(8,128)} async-done(((f32[1024,512]{1,0:T(8,128)}), f32[64,512]{1,0:T(8,128)}) %reduce-scatter.7.cloned.1.call-update) | async-done | bytes 131088
  397.7 151.1 %all-reduce.4.cloned.1.call-done = (f32[3,5120,16]{1,2,0:T(8,128)}, f32[16,4096]{1,0:T(8,128)}, f32[2,16,512]{2,1,0:T(8,128)}, f32[4096,16]{0,1:T(8,128)}, f32[16,5120]{1,0:T(8,128)}) async-done(((f32[3,5120,16]{1,2,0:T(8,128)}, f32[16,4096]{1,0:T(8,128)}, f32[2,16,512]{2,1,0:T(8,128)}, f32[4096,16]{0,1:T(8,128)}, f32[16,5120]{1,0:T(8,128)}), (f32[3,5120,16]{1,2,0:T(8,128)}, f32[16,4096]{1,0:T(8,128)}, ...) | async-done | bytes 1900560 | tf_op jit(solution)/shard_map/psum | solution.py:291
  (470 shorter events, 223.9 us)
Async XLA Ops:
  7.2 7.3 %copy-start = (bf16[1,1,128,5120]{3,2,1,0:T(8,128)(2,1)S(1)}, bf16[1,1,128,5120]{3,2,1,0:T(8,128)(2,1)}, u32[]{:S(2)}) copy-start(bf16[1,1,128,5120]{3,2,1,0:T(8,128)(2,1)} %param.20) | copy-start | bytes 3932164
  7.2 7.3 %copy-start.40 = (bf16[3,5120,16]{1,2,0:T(8,128)(2,1)S(1)}, bf16[3,5120,16]{1,2,0:T(8,128)(2,1)}, u32[]{:S(2)}) copy-start(bf16[3,5120,16]{1,2,0:T(8,128)(2,1)} %param.23) | copy-start | bytes 1474564
  7.2 43.8 %all-gather.5.cloned.1.call-start = ((), (), s32[]{:S(2)}) async-start(), calls=%async_computation.3 | async-start | bytes 1114112 | tf_op jit(solution)/shard_map/all_gather | solution.py:234
  8.9 8.4 %copy-start.71 = (bf16[3,64,16]{1,2,0:T(8,128)(2,1)}, bf16[3,64,16]{1,2,0:T(8,128)(2,1)S(1)}, u32[]{:S(2)}) copy-start(bf16[3,64,16]{1,2,0:T(8,128)(2,1)S(1)} %fusion.100) | copy-start | bytes 18436
  10.6 71.2 %all-gather.3.cloned.1.call-start = ((), (), s32[]{:S(2)}) async-start(), calls=%async_computation.2 | async-start | bytes 1114112 | tf_op jit(solution)/shard_map/all_gather | solution.py:233
  11.8 5.5 copy-start.38
  12.7 5.8 %copy-start.60 = (f32[64,128]{1,0:T(8,128)}, f32[64,128]{1,0:T(8,128)S(1)}, u32[]{:S(2)}) copy-start(f32[64,128]{1,0:T(8,128)S(1)} %get-tuple-element.260) | copy-start | bytes 98308
  12.8 5.8 %copy-start.62 = (f32[64,128]{1,0:T(8,128)}, f32[64,128]{1,0:T(8,128)S(1)}, u32[]{:S(2)}) copy-start(f32[64,128]{1,0:T(8,128)S(1)} %get-tuple-element.259) | copy-start | bytes 98308
  14.4 312.7 %reduce-scatter.5.cloned.1.call-start = ((), (), s32[]{:S(2)}) async-start(), calls=%async_computation.4 | async-start | bytes 2228224 | tf_op jit(solution)/shard_map/reduce_scatter | solution.py:262
  15.1 34.2 %copy-start.73 = (bf16[3,128,16]{1,2,0:T(8,128)(2,1)}, bf16[3,128,16]{1,2,0:T(8,128)(2,1)S(1)}, u32[]{:S(2)}) copy-start(bf16[3,128,16]{1,2,0:T(8,128)(2,1)S(1)} %fusion.101) | copy-start | bytes 36868
  24.8 11.5 %copy-start.86 = (pred[128]{0:T(512)(128)(4,1)}, pred[128]{0:T(512)(128)(4,1)S(1)}, u32[]{:S(2)}) copy-start(pred[128]{0:T(512)(128)(4,1)S(1)} %iota_compare_fusion.3) | copy-start | bytes 388
  36.4 6.0 %copy-start.26 = (bf16[128,4096]{1,0:T(8,128)(2,1)S(1)}, bf16[128,4096]{1,0:T(8,128)(2,1)}, u32[]{:S(2)}) copy-start(bf16[128,4096]{1,0:T(8,128)(2,1)} %fusion.82) | copy-start | bytes 3145732
  264.9 123.7 %reduce-scatter.7.cloned.1.call-start = ((), (), s32[]{:S(2)}) async-start(), calls=%async_computation.5 | async-start | bytes 2228224
  268.3 18.3 %copy-start.59 = (f32[64,128]{1,0:T(8,128)}, f32[64,128]{1,0:T(8,128)S(1)}, u32[]{:S(2)}) copy-start(f32[64,128]{1,0:T(8,128)S(1)} %pad_maximum_fusion.7) | copy-start | bytes 98308
  290.0 258.8 %all-reduce.4.cloned.1.call-start = ((), (), s32[]{:S(2)}) async-start(), calls=%async_computation.6 | async-start | bytes 3801088 | tf_op jit(solution)/shard_map/psum | solution.py:291
  322.5 6.8 %copy-start.36 = (f32[64,4,128]{2,1,0:T(4,128)S(1)}, f32[64,4,128]{2,1,0:T(4,128)}, u32[]{:S(2)}) copy-start(f32[64,4,128]{2,1,0:T(4,128)} %copy-done.35) | copy-start | bytes 393220
  327.1 62.6 %copy-start.34 = (f32[128,4,128]{0,2,1:T(8,128)S(1)}, f32[128,4,128]{0,2,1:T(8,128)}, u32[]{:S(2)}) copy-start(f32[128,4,128]{0,2,1:T(8,128)} %slice.182) | copy-start | bytes 786436
  327.1 64.2 %copy-start.55 = (bf16[2,16,512]{2,1,0:T(8,128)(2,1)S(1)}, bf16[2,16,512]{2,1,0:T(8,128)(2,1)}, u32[]{:S(2)}) copy-start(bf16[2,16,512]{2,1,0:T(8,128)(2,1)} %param.25) | copy-start | bytes 98308
  327.1 65.4 %copy-start.29 = (bf16[1,64,5120]{2,1,0:T(8,128)(2,1)S(1)}, bf16[1,64,5120]{2,1,0:T(8,128)(2,1)}, u32[]{:S(2)}) copy-start(bf16[1,64,5120]{2,1,0:T(8,128)(2,1)} %param.18) | copy-start | bytes 1966084
  327.1 65.4 %copy-start.77 = (f32[1,64,16]{1,2,0:T(8,128)S(1)}, f32[1,64,16]{1,2,0:T(8,128)}, u32[]{:S(2)}) copy-start(f32[1,64,16]{1,2,0:T(8,128)} %convolution_bitcast_fusion.8) | copy-start | bytes 12292
  327.2 64.1 %copy-start.46 = (f32[64,512]{1,0:T(8,128)S(1)}, f32[64,512]{1,0:T(8,128)}, u32[]{:S(2)}) copy-start(f32[64,512]{1,0:T(8,128)} %reduce-scatter.5.cloned.1.call-done) | copy-start | bytes 393220
  328.4 64.8 %copy-start.78 = (f32[1,128,16]{1,2,0:T(8,128)S(1)}, f32[1,128,16]{1,2,0:T(8,128)}, u32[]{:S(2)}) copy-start(f32[1,128,16]{1,2,0:T(8,128)} %fusion.104) | copy-start | bytes 24580
  328.4 64.8 %copy-start.79 = (f32[1,128,16]{1,2,0:T(8,128)S(1)}, f32[1,128,16]{1,2,0:T(8,128)}, u32[]{:S(2)}) copy-start(f32[1,128,16]{1,2,0:T(8,128)} %convolution_bitcast_fusion.5) | copy-start | bytes 24580
  328.4 64.8 %copy-start.80 = (f32[1,128,16]{1,2,0:T(8,128)S(1)}, f32[1,128,16]{1,2,0:T(8,128)}, u32[]{:S(2)}) copy-start(f32[1,128,16]{1,2,0:T(8,128)} %convolution_bitcast_fusion.4) | copy-start | bytes 24580
  (98 other events, 282.8 us)
Sparse Core Ops, SparseCore 0:
  10.7 36.1 all-gather.4
  49.2 32.5 all-gather.2
  265.0 59.3 reduce-scatter.4
  326.6 61.9 reduce-scatter.6
  394.9 153.8 all-reduce.3
where the time goes:
time: 571 us; the launch traced here: 561 us
  waiting for transfers between devices  236 us (41%)
  local copies, waits for them, and re-layouts  125 us (22%)
  matrix products  120 us (21%)
  other arithmetic  61.7 us (11%)
  between operations  15.9 us (3%)
    psum x1, waiting for transfers between devices, per_device(): lax.psum((prompt_down + reply_down, grad_query, jnp.stack([grad_key_up, g...  151 us
    unnamed x6, waiting for transfers between devices  57.1 us
    dynamic_update_slice x32, local copies, waits for them, and re-layouts, attend(): attended_output, dquery, dkey, dvalue = lax.map(one_group, stacked)  45.2 us
    sub x8, matrix products, one_group(): weight = jnp.exp(scores - top)  32.8 us
    all_gather x1, waiting for transfers between devices, per_device(): lax.all_gather(prompt_key, 'resp', axis=0, tiled=True)  28.1 us
    unnamed x174, local copies, waits for them, and re-layouts  27.8 us
    convert_element_type x8, other arithmetic, one_group(): chosen = prob.astype(jnp.bfloat16)  22.3 us
    dot_general x8, matrix products, one_group(): jnp.einsum('rgk,kd->rgd', dscore, key_head, preferred_element_type=jnp.fl...  17.7 us
  transfers between devices with their start and end apart: 5, of which 3 were waited for; matrix products, arithmetic and copies ran while one was open for 19% of the time, Pallas kernels for 0%

commit v1 on v0

v1 whole, which is shorter than its diff:
```python
import functools

import jax
import jax.numpy as jnp
import numpy as np
from jax import lax
from jax.experimental import pallas as pl
from jax.experimental.pallas import tpu as pltpu
from jax.sharding import PartitionSpec as P

HEAD_DIM = 128
HALF = 64
RANK = 16
ROPE_BASE = 1000000.0
LOG2E = 1.4426950408889634
F32 = jnp.float32
BF16 = jnp.bfloat16
BOTH = ("ctx", "resp")
VMEM_LIMIT = 56 * 1024 * 1024

NN = (((1,), (0,)), ((), ()))
NT = (((1,), (1,)), ((), ()))
TN = (((0,), (0,)), ((), ()))


def mm(a, b, dims=NN):
    return lax.dot_general(a, b, dims, preferred_element_type=F32)


def rope_tables(count):
    rates = ROPE_BASE ** (-(np.arange(HALF, dtype=np.float64) * (2.0 / HEAD_DIM)))
    angle = np.arange(count, dtype=np.float64)[:, None] * rates[None, :]
    return np.cos(angle), np.sin(angle)


def rope(x, cos, sin):
    return x * cos + pltpu.roll(x, HALF, 1) * sin


def unrope(x, cos, sin):
    return x * cos - pltpu.roll(x, HALF, 1) * sin


def params(flops=0, nbytes=0):
    return dict(
        compiler_params=pltpu.CompilerParams(vmem_limit_bytes=VMEM_LIMIT),
        cost_estimate=pl.CostEstimate(flops=flops, bytes_accessed=nbytes, transcendentals=0),
    )


def kv_rows(hidden, base, down, kv_up, cos, sin):
    kv_width = kv_up.shape[2]
    low = mm(hidden, down, NT).astype(BF16)
    zero = jnp.zeros((RANK, kv_width), BF16)
    k_lift = jnp.concatenate([zero, kv_up[0], zero], axis=0)
    v_lift = jnp.concatenate([zero, zero, kv_up[1]], axis=0)
    key = base[:, :kv_width].astype(F32) + 2.0 * mm(low, k_lift)
    value = base[:, kv_width:].astype(F32) + 2.0 * mm(low, v_lift)
    heads = [
        rope(key[:, h : h + HEAD_DIM], cos, sin).astype(BF16)
        for h in range(0, kv_width, HEAD_DIM)
    ]
    return low, jnp.concatenate(heads, axis=1), value.astype(BF16)


def pad_low(low):
    return jnp.concatenate([low, jnp.zeros((low.shape[0], HEAD_DIM - 3 * RANK), BF16)], axis=1)


def front_kernel(spot, hidden, base, down, kv_up, cos, sin, out):
    low, key, value = kv_rows(hidden[0], base[0], down[...], kv_up[...], cos[...], sin[...])
    out[...] = jnp.concatenate([key, value, pad_low(low)], axis=1)


def prep_kernel(
    spot, lengths, p_low, p_base, p_out, p_gbase, r_hidden, r_base, r_kvbase, r_out, r_gbase,
    down, q_up, kv_up, out_down, out_up, p_cos, p_sin, r_cos, r_sin,
    query, push, r_kv, low_t, lowered_t,
):
    pr = p_low.shape[0]
    rl = r_hidden.shape[2]
    q_width = q_up.shape[1]
    r_low, r_key, r_value = kv_rows(
        r_hidden[0, 0], r_kvbase[0, 0], down[...], kv_up[...], r_cos[...], r_sin[...]
    )
    r_low = pad_low(r_low)
    r_kv[...] = jnp.concatenate([r_key, r_value, r_low], axis=1)
    lows = (p_low[...], r_low)
    for low, rows in ((lows[0], pl.ds(0, pr)), (lows[1], pl.ds(pr, rl))):
        low_t[:, rows] = jnp.transpose(low.astype(F32))[: 3 * RANK].astype(BF16)
    live = lax.broadcasted_iota(jnp.int32, (rl, HEAD_DIM), 0) < lengths[0, 0]
    p_lowered = mm(p_out[0], out_up[...], NT)
    r_lowered = mm(r_out[0, 0], out_up[...], NT)
    r_lowered = jnp.where(live[:, :RANK], r_lowered, 0.0)
    split = []
    for lowered, at, n in ((p_lowered, 0, pr), (r_lowered, pr, rl)):
        high = lowered.astype(BF16)
        rest = (lowered - high.astype(F32)).astype(BF16)
        zero = jnp.zeros((n, HEAD_DIM - 2 * RANK), BF16)
        both = jnp.concatenate([high, rest, zero], axis=1)
        split.append(both)
        lowered_t[:, pl.ds(at, n)] = jnp.transpose(both.astype(F32))[: 2 * RANK].astype(BF16)
    for c in range(0, q_width, 1024):
        cols = slice(c, c + 1024)
        q_lift = jnp.concatenate(
            [q_up[:, cols], jnp.zeros((HEAD_DIM - RANK, 1024), BF16)], axis=0
        )
        o_lift = jnp.concatenate(
            [out_down[:, cols], out_down[:, cols], jnp.zeros((HEAD_DIM - 2 * RANK, 1024), BF16)],
            axis=0,
        )
        for i, (base, gbase, cos, sin, at, n) in enumerate(
            (
                (p_base[0, :, cols], p_gbase[0, :, cols], p_cos, p_sin, 0, pr),
                (r_base[0, 0, :, cols], r_gbase[0, 0, :, cols], r_cos, r_sin, pr, rl),
            )
        ):
            q = base.astype(F32) + 2.0 * mm(lows[i], q_lift)
            for h in range(0, 1024, HEAD_DIM):
                query[at : at + n, c + h : c + h + HEAD_DIM] = rope(
                    q[:, h : h + HEAD_DIM], cos[...], sin[...]
                ).astype(BF16)
            up = gbase.astype(F32) + 2.0 * mm(split[i], o_lift)
            if i == 1:
                up = jnp.where(live[:, :1], up, 0.0)
            push[at : at + n, c : c + 1024] = up.astype(BF16)


def attend_kernel(
    spot, lengths, query, push, key, value, low, r_key, r_value, r_low, low_t, lowered_t,
    q_up, kv_up, out_down, p_cos, p_sin, r_cos, r_sin, cos_t, sin_t,
    p_context, r_context, grad_q, grad_kv, grad_od, fold_q, lifted, fold_send, fold_reply,
    dk_t, dv_t, raw_q, mixed, keys, values, bias, fold_k, fold_v,
):
    g = pl.program_id(0)
    last = pl.num_programs(0) - 1
    pr = p_context.shape[1]
    rl = r_context.shape[2]
    prompt = key.shape[0]
    scale = HEAD_DIM ** (-0.5)
    step = scale * LOG2E
    share = query.shape[1] // HEAD_DIM
    block = 256

    @pl.when(g == 0)
    def _():
        row = lax.broadcasted_iota(jnp.int32, (pr, prompt), 0) + spot[0] * pr
        col = lax.broadcasted_iota(jnp.int32, (pr, prompt), 1)
        bias[...] = jnp.where(col <= row, 0.0, -jnp.inf)
        fold_q[...] = jnp.zeros_like(fold_q)
        lifted[...] = jnp.zeros_like(lifted)
        fold_k[...] = jnp.zeros_like(fold_k)
        fold_v[...] = jnp.zeros_like(fold_v)
        values[:, HEAD_DIM:] = jnp.ones((prompt + rl, HEAD_DIM), BF16)

    keys[:prompt, :] = key[...]
    keys[prompt:, :] = r_key[...]
    values[:prompt, :HEAD_DIM] = value[...]
    values[prompt:, :HEAD_DIM] = r_value[...]
    dk_t[...] = jnp.zeros_like(dk_t)
    dv_t[...] = jnp.zeros_like(dv_t)

    def one_block(rows, n, at, heads, mask, keep, cos, sin, count):
        def stack(ref):
            return jnp.concatenate(
                [ref[pl.ds(at, n), pl.ds(pl.multiple_of(h * HEAD_DIM, HEAD_DIM), HEAD_DIM)] for h in heads],
                axis=0,
            )

        q = stack(query)
        p = stack(push)
        k = keys[:count, :]
        v = values[:count, :HEAD_DIM]
        score = mask(mm(q, k, NT))
        top = jnp.max(score, axis=1, keepdims=True) * step
        weight = jnp.exp2(score * step - top).astype(BF16)
        summed = mm(weight, values[:count, :])
        share_of = 1.0 / summed[:, HEAD_DIM:]
        context = (summed[:, :HEAD_DIM] * share_of).astype(BF16)
        context = keep(context)
        delta = jnp.sum(context.astype(F32) * p.astype(F32), axis=1, keepdims=True)
        dprob = mm(p, v, NT)
        dscore = (weight.astype(F32) * (dprob - delta)).astype(BF16)
        inverse = share_of * scale
        dq = mm(dscore, k) * inverse
        dk_t[:, :count] += mm((q.astype(F32) * inverse).astype(BF16), dscore, TN)
        dv_t[:, :count] += mm((p.astype(F32) * share_of).astype(BF16), weight, TN)
        for i, h in enumerate(heads):
            part = slice(i * n, (i + 1) * n)
            cols = pl.ds(pl.multiple_of(h * HEAD_DIM, HEAD_DIM), HEAD_DIM)
            raw_q[pl.ds(at, n), cols] = unrope(dq[part], cos[...], sin[...]).astype(BF16)
            mixed[pl.ds(at, n), cols] = context[part]

    p_heads = block // pr
    r_heads = block // rl

    def p_mask(score):
        seen = bias[...]
        return jnp.concatenate(
            [score[i * pr : (i + 1) * pr] + seen for i in range(p_heads)], axis=0
        )

    for b in range(share // p_heads):
        one_block(
            block, pr, 0, [b * p_heads + i for i in range(p_heads)], p_mask,
            lambda c: c, p_cos, p_sin, prompt,
        )

    r_row = lax.broadcasted_iota(jnp.int32, (rl, rl), 0)
    r_col = lax.broadcasted_iota(jnp.int32, (rl, rl), 1)
    r_seen = jnp.concatenate([r_col <= r_row] * r_heads, axis=0)
    live = jnp.concatenate([r_row < lengths[0, 0]] * r_heads, axis=0)

    def r_mask(score):
        own = jnp.where(r_seen, score[:, prompt:], -jnp.inf)
        return jnp.concatenate([score[:, :prompt], own], axis=1)

    for b in range(share // r_heads):
        one_block(
            block, rl, pr, [b * r_heads + i for i in range(r_heads)], r_mask,
            lambda c: jnp.where(live, c, jnp.zeros_like(c)), r_cos, r_sin, prompt + rl,
        )

    context = mixed[...]
    p_context[0] = mixed[:pr, :]
    r_context[0, 0] = mixed[pr:, :]
    raw = raw_q[...]
    grad_q[...] = (2.0 * mm(low_t[:RANK, :], raw)).astype(BF16)
    both = mm(lowered_t[...], context)
    grad_od[...] = (2.0 * (both[:RANK] + both[RANK:])).astype(BF16)
    fold_q[...] += mm(q_up[...], raw, NT)
    lifted[...] += mm(out_down[...], context, NT)
    upper, lower = dk_t[:HALF, :], dk_t[HALF:, :]
    cos, sin = cos_t[...], sin_t[...]
    raw_k = jnp.concatenate(
        [(upper * cos + lower * sin).astype(BF16), (lower * cos - upper * sin).astype(BF16)], axis=0
    )
    raw_v = dv_t[...].astype(BF16)
    fold_k[...] += mm(kv_up[0], raw_k)
    fold_v[...] += mm(kv_up[1], raw_v)
    gk = mm(raw_k[:, :prompt], low[...]) + mm(raw_k[:, prompt:], r_low[...])
    gv = mm(raw_v[:, :prompt], low[...]) + mm(raw_v[:, prompt:], r_low[...])
    gk, gv = jnp.transpose(gk), jnp.transpose(gv)
    grad_kv[...] = (
        2.0 * jnp.concatenate([gk[RANK : 2 * RANK], gv[2 * RANK : 3 * RANK]], axis=0)
    ).astype(BF16)

    @pl.when(g == last)
    def _():
        fk, fv = fold_k[...], fold_v[...]
        for r in range(prompt // pr):
            cols = slice(r * pr, (r + 1) * pr)
            fold_send[r] = jnp.concatenate([fk[:, cols], fv[:, cols]], axis=1).astype(BF16)
        fold_reply[...] = jnp.concatenate([fk[:, prompt:], fv[:, prompt:]], axis=0).astype(BF16)


def grads_kernel(
    fold_q, lifted, fold_reply, fold_recv, p_hidden, r_hidden, p_out, r_out, grad_down, grad_up
):
    pr = p_hidden.shape[1]
    fq = fold_q[...].astype(BF16)
    up = lifted[...].astype(BF16)
    own = jnp.sum(fold_recv[...].astype(F32), axis=0).astype(BF16)
    fp = jnp.concatenate([fq[:, :pr], own[:, :pr], own[:, pr:]], axis=0)
    fr = jnp.concatenate([fq[:, pr:], fold_reply[...]], axis=0)
    d = p_hidden.shape[2]
    down = 2.0 * (mm(fp, p_hidden[0]) + mm(fr, r_hidden[0, 0]))
    grad_down[...] = down.astype(BF16)
    grad_up[...] = (2.0 * (mm(up[:, :pr], p_out[0]) + mm(up[:, pr:], r_out[0, 0]))).astype(BF16)


def whole(shape):
    return pl.BlockSpec(shape, lambda *_: (0,) * len(shape))


def per_device(
    prompt_hidden,
    prompt_base,
    reply_hidden,
    reply_base,
    reply_lengths,
    adapter_down,
    query_up_weight,
    key_value_up_weight,
    output_down,
    output_up,
    prompt_grad_out,
    prompt_grad_base,
    reply_grad_out,
    reply_grad_base,
):
    group = lax.axis_size("resp")
    everyone = group * lax.axis_size("ctx")
    pr = prompt_hidden.shape[1]
    rl = reply_hidden.shape[2]
    d = prompt_hidden.shape[2]
    prompt = pr * group
    q_width = query_up_weight.shape[1]
    kv_width = key_value_up_weight.shape[2]
    heads = kv_width // HEAD_DIM
    qb = q_width // heads
    rows = pr + rl
    wide = 2 * kv_width + HEAD_DIM
    low_at = 2 * kv_width // HEAD_DIM

    spot = lax.axis_index("resp").astype(jnp.int32)[None]
    down = jnp.transpose(adapter_down, (0, 2, 1)).reshape(3 * RANK, d)
    out_down = jnp.transpose(output_down)
    cos, sin = rope_tables(prompt + rl)
    cos_rows = jnp.asarray(np.concatenate([cos, cos], axis=1), F32)
    sin_rows = jnp.asarray(np.concatenate([-sin, sin], axis=1), F32)
    cos_t = jnp.asarray(cos.T, F32)
    sin_t = jnp.asarray(sin.T, F32)
    p_table = pl.BlockSpec((pr, HEAD_DIM), lambda i, s: (s[0], 0))
    r_table = pl.BlockSpec((rl, HEAD_DIM), lambda i, s: (prompt // rl, 0))

    own_kv = pl.pallas_call(
        front_kernel,
        grid_spec=pltpu.PrefetchScalarGridSpec(
            num_scalar_prefetch=1,
            grid=(1,),
            in_specs=[
                whole((1, pr, d)),
                pl.BlockSpec((1, pr, 2 * kv_width), lambda i, s: (0, 0, q_width // (2 * kv_width))),
                whole((3 * RANK, d)),
                whole((2, RANK, kv_width)),
                p_table,
                p_table,
            ],
            out_specs=whole((pr, wide)),
        ),
        out_shape=jax.ShapeDtypeStruct((pr, wide), BF16),
        name="front",
        **params(2 * pr * d * 48, 2_000_000),
    )(spot, prompt_hidden, prompt_base, down, key_value_up_weight, cos_rows, sin_rows)

    all_kv = lax.all_gather(own_kv, "resp", axis=0, tiled=True)

    query, push, reply_kv, low_t, lowered_t = pl.pallas_call(
        prep_kernel,
        grid_spec=pltpu.PrefetchScalarGridSpec(
            num_scalar_prefetch=1,
            grid=(1,),
            in_specs=[
                pl.BlockSpec(memory_space=pltpu.SMEM),
                pl.BlockSpec((pr, HEAD_DIM), lambda i, s: (0, low_at)),
                pl.BlockSpec((1, pr, q_width), lambda i, s: (0, 0, 0)),
                whole((1, pr, d)),
                whole((1, pr, q_width)),
                whole((1, 1, rl, d)),
                pl.BlockSpec((1, 1, rl, q_width), lambda i, s: (0, 0, 0, 0)),
                pl.BlockSpec(
                    (1, 1, rl, 2 * kv_width), lambda i, s: (0, 0, 0, q_width // (2 * kv_width))
                ),
                whole((1, 1, rl, d)),
                whole((1, 1, rl, q_width)),
                whole((3 * RANK, d)),
                whole((RANK, q_width)),
                whole((2, RANK, kv_width)),
                whole((RANK, q_width)),
                whole((RANK, d)),
                p_table,
                p_table,
                r_table,
                r_table,
            ],
            out_specs=[
                whole((rows, q_width)),
                whole((rows, q_width)),
                whole((rl, wide)),
                whole((3 * RANK, rows)),
                whole((2 * RANK, rows)),
            ],
        ),
        out_shape=[
            jax.ShapeDtypeStruct((rows, q_width), BF16),
            jax.ShapeDtypeStruct((rows, q_width), BF16),
            jax.ShapeDtypeStruct((rl, wide), BF16),
            jax.ShapeDtypeStruct((3 * RANK, rows), BF16),
            jax.ShapeDtypeStruct((2 * RANK, rows), BF16),
        ],
        name="prep",
        **params(4 * rows * d * 48, 12_000_000),
    )(
        spot, reply_lengths, own_kv, prompt_base, prompt_grad_out, prompt_grad_base, reply_hidden,
        reply_base, reply_base, reply_grad_out, reply_grad_base, down, query_up_weight,
        key_value_up_weight, out_down, output_up, cos_rows, sin_rows, cos_rows, sin_rows,
    )

    def head_cols(n, width, shift=0):
        return pl.BlockSpec((n, width), lambda i, s: (0, i + shift))

    (
        p_context, r_context, grad_q, grad_kv, grad_od, fold_q, lifted, fold_send, fold_reply,
    ) = pl.pallas_call(
        attend_kernel,
        grid_spec=pltpu.PrefetchScalarGridSpec(
            num_scalar_prefetch=1,
            grid=(heads,),
            in_specs=[
                pl.BlockSpec(memory_space=pltpu.SMEM),
                head_cols(rows, qb),
                head_cols(rows, qb),
                head_cols(prompt, HEAD_DIM),
                head_cols(prompt, HEAD_DIM, heads),
                pl.BlockSpec((prompt, HEAD_DIM), lambda i, s: (0, low_at)),
                head_cols(rl, HEAD_DIM),
                head_cols(rl, HEAD_DIM, heads),
                pl.BlockSpec((rl, HEAD_DIM), lambda i, s: (0, low_at)),
                whole((3 * RANK, rows)),
                whole((2 * RANK, rows)),
                head_cols(RANK, qb),
                pl.BlockSpec((2, RANK, HEAD_DIM), lambda i, s: (0, 0, i)),
                head_cols(RANK, qb),
                p_table,
                p_table,
                r_table,
                r_table,
                whole((HALF, prompt + rl)),
                whole((HALF, prompt + rl)),
            ],
            out_specs=[
                pl.BlockSpec((1, pr, qb), lambda i, s: (0, 0, i)),
                pl.BlockSpec((1, 1, rl, qb), lambda i, s: (0, 0, 0, i)),
                head_cols(RANK, qb),
                head_cols(2 * RANK, HEAD_DIM),
                head_cols(RANK, qb),
                whole((RANK, rows)),
                whole((RANK, rows)),
                whole((group, RANK, 2 * pr)),
                whole((2 * RANK, rl)),
            ],
            scratch_shapes=[
                pltpu.VMEM((HEAD_DIM, prompt + rl), F32),
                pltpu.VMEM((HEAD_DIM, prompt + rl), F32),
                pltpu.VMEM((rows, qb), BF16),
                pltpu.VMEM((rows, qb), BF16),
                pltpu.VMEM((prompt + rl, HEAD_DIM), BF16),
                pltpu.VMEM((prompt + rl, 2 * HEAD_DIM), BF16),
                pltpu.VMEM((pr, prompt), F32),
                pltpu.VMEM((RANK, prompt + rl), F32),
                pltpu.VMEM((RANK, prompt + rl), F32),
            ],
        ),
        out_shape=[
            jax.ShapeDtypeStruct((1, pr, q_width), BF16),
            jax.ShapeDtypeStruct((1, 1, rl, q_width), BF16),
            jax.ShapeDtypeStruct((RANK, q_width), BF16),
            jax.ShapeDtypeStruct((2 * RANK, kv_width), BF16),
            jax.ShapeDtypeStruct((RANK, q_width), BF16),
            jax.ShapeDtypeStruct((RANK, rows), F32),
            jax.ShapeDtypeStruct((RANK, rows), F32),
            jax.ShapeDtypeStruct((group, RANK, 2 * pr), BF16),
            jax.ShapeDtypeStruct((2 * RANK, rl), BF16),
        ],
        name="attend",
        **params(12 * rows * prompt * q_width, 8_000_000),
    )(
        spot, reply_lengths, query, push, all_kv, all_kv, all_kv, reply_kv, reply_kv, reply_kv,
        low_t, lowered_t, query_up_weight, key_value_up_weight, out_down, cos_rows, sin_rows,
        cos_rows, sin_rows, cos_t, sin_t,
    )

    fold_recv = lax.all_to_all(fold_send, "resp", 0, 0, tiled=True)

    grad_down, grad_up = pl.pallas_call(
        grads_kernel,
        out_shape=[
            jax.ShapeDtypeStruct((3 * RANK, d), BF16),
            jax.ShapeDtypeStruct((RANK, d), BF16),
        ],
        name="grads",
        **params(2 * rows * d * 64, 5_000_000),
    )(
        fold_q, lifted, fold_reply, fold_recv, prompt_hidden, reply_hidden, prompt_grad_out,
        reply_grad_out,
    )

    pieces = (grad_down, grad_up, grad_q, grad_od, grad_kv)
    flat = jnp.concatenate([x.reshape(-1) for x in pieces])
    unit = everyone * 8 * HEAD_DIM
    total = -(-flat.size // unit) * unit
    flat = jnp.concatenate([flat, jnp.zeros((total - flat.size,), BF16)])
    spread = lax.all_to_all(flat.reshape(everyone, -1, HEAD_DIM), BOTH, 0, 0, tiled=True)
    mine = jnp.sum(spread.astype(F32), axis=0).astype(BF16)
    full = lax.all_to_all(
        jnp.broadcast_to(mine[None], spread.shape), BOTH, 0, 0, tiled=True
    ).reshape(-1)
    outs = []
    at = 0
    for x in pieces:
        outs.append(full[at : at + x.size].reshape(x.shape).astype(F32))
        at += x.size
    sum_down, sum_up, sum_q, sum_od, sum_kv = outs
    return (
        p_context,
        r_context,
        jnp.transpose(sum_down.reshape(3, RANK, d), (0, 2, 1)),
        sum_q,
        sum_kv.reshape(2, RANK, kv_width),
        jnp.transpose(sum_od),
        sum_up,
    )


def solution(mesh):
    return jax.shard_map(
        per_device,
        mesh=mesh,
        in_specs=(
            P("ctx", "resp", None),
            P("ctx", "resp", None),
            P("ctx", "resp", None, None),
            P("ctx", "resp", None, None),
            P("ctx", "resp"),
            P(),
            P(),
            P(),
            P(),
            P(),
            P("ctx", "resp", None),
            P("ctx", "resp", None),
            P("ctx", "resp", None, None),
            P("ctx", "resp", None, None),
        ),
        out_specs=(P("ctx", "resp", None), P("ctx", "resp", None, None), P(), P(), P(), P(), P()),
        check_vma=False,
    )
```

time: 571 us -> 162 us (0.28); the launches traced: 561 us -> 161 us
  waiting for transfers between devices: 236 us -> 32.9 us
  matrix products: 120 us -> 0 us
  local copies, waits for them, and re-layouts: 125 us -> 9.13 us
  other arithmetic: 61.7 us -> 0.39 us
  Pallas kernels: 0 us -> 49.9 us
  blocking collectives: 0 us -> 49.9 us
    psum x1 -> x0, waiting for transfers between devices: 151 us -> none  [per_device(): lax.psum((prompt_down + reply_down, grad_query, jnp.stack([grad_key_up, g...]
    dot_general x72 -> x0, matrix products: 87.6 us -> none  [the longest x8 17.7 us: one_group(): jnp.einsum('rgk,kd->rgd', dscore, key_head, preferred_element_type=jnp.fl...]
    unnamed x6 -> x1, waiting for transfers between devices: 57.1 us -> 0.02 us
    all_to_all x0 -> x2, blocking collectives: none -> 49.9 us  [the longest x1 26.4 us: per_device(): lax.all_to_all(flat.reshape(everyone, -1, HEAD_DIM), BOTH, 0, 0, tiled=True)]
    pallas_call x0 -> x4, Pallas kernels: none -> 49.9 us  [the longest x1 35.4 us: per_device(): pl.pallas_call(attend_kernel, grid_spec=pltpu.PrefetchScalarGridSpec(num_...]
    dynamic_update_slice x32 -> x0, local copies, waits for them, and re-layouts: 45.2 us -> none  [attend(): attended_output, dquery, dkey, dvalue = lax.map(one_group, stacked)]
    sub x8 -> x0, matrix products: 32.8 us -> none  [one_group(): weight = jnp.exp(scores - top)]
    convert_element_type x14 -> x2, other arithmetic: 28.1 us -> 0.03 us  [per_device(): outs.append(full[at:at + x.size].reshape(x.shape).astype(F32))]
  transfers between devices with their start and end apart: 5 -> 2, of which waited for: 3 -> 2; matrix products, arithmetic and copies ran while one was open for 19% -> 2% of each run, Pallas kernels for 0% -> 5%
where the time goes in v1:
time: 162 us; the launch traced here: 161 us
  Pallas kernels  49.9 us (31%)
  blocking collectives  49.9 us (31%)
  waiting for transfers between devices  32.9 us (20%)
  between operations  14.8 us (9%)
  local copies, waits for them, and re-layouts  9.13 us (6%)
  starting transfers between devices  4.16 us (3%)
    pallas_call x1, Pallas kernels, per_device(): pl.pallas_call(attend_kernel, grid_spec=pltpu.PrefetchScalarGridSpec(num_...  35.4 us
    all_gather x1, waiting for transfers between devices, per_device(): all_kv = lax.all_gather(own_kv, 'resp', axis=0, tiled=True)  29.7 us
    all_to_all x1, blocking collectives, per_device(): lax.all_to_all(flat.reshape(everyone, -1, HEAD_DIM), BOTH, 0, 0, tiled=True)  26.4 us
    all_to_all x1, blocking collectives, per_device(): lax.all_to_all(jnp.broadcast_to(mine[None], spread.shape), BOTH, 0, 0, ti...  23.6 us
    pallas_call x1, Pallas kernels, per_device(): pl.pallas_call(prep_kernel, grid_spec=pltpu.PrefetchScalarGridSpec(num_sc...  8.27 us
    unnamed x12, local copies, waits for them, and re-layouts  5.36 us
    all_to_all x1, starting transfers between devices, per_device(): fold_recv = lax.all_to_all(fold_send, 'resp', 0, 0, tiled=True)  4.12 us
    pallas_call x1, Pallas kernels, per_device(): pl.pallas_call(grads_kernel, out_shape=[jax.ShapeDtypeStruct((3 * RANK, d...  3.66 us
  transfers between devices with their start and end apart: 2, of which 2 were waited for; matrix products, arithmetic and copies ran while one was open for 2% of the time, Pallas kernels for 5%

profile of v1, /device:TPU:1, one launch (start us, length us, event | category | flops | bytes accessed | tf_op | source)
XLA Modules:
  0.0 161.2 jit_solution(15069812206483452355)
XLA Ops:
  7.2 0.0 all-gather.2.cloned.1.call-start
  7.2 2.5 %front.1.p_low = bf16[64,1152]{1,0:T(8,128)(2,1)} custom-call(s32[1]{0:T(128)} %bitcast.spot, bf16[1,64,5120]{2,1,0:T(8,128)(2,1)} %p_hidden.1, bf16[1,64,5120]{2,1,0:T(8,128)(2,1)} %p_base.1, bf16[48,5120]{1,0:T(8,128)(2,1)} %bitcast.26, bf16[2,16,512]{2,1,0:T(8,128)(2,1)} %kv_up.5, f32[1152,128]{1,0:T(8,128)} %constant.16.clone.cos.p_cos.r_cos, ...), custom_call_target="tpu_custom_call" | custom-call | flops 31457280 | bytes 2000000 | tf_op jit(solution)/shard_map/front/pallas_call | solution.py:317
  9.8 0.0 all-gather.2.cloned.1.call-update
  10.4 8.3 %prep.1 = (bf16[192,4096]{1,0:T(8,128)(2,1)}, bf16[192,4096]{1,0:T(8,128)(2,1)}, bf16[128,1152]{1,0:T(8,128)(2,1)}, bf16[48,192]{1,0:T(8,128)(2,1)}, bf16[32,192]{1,0:T(8,128)(2,1)}) custom-call(s32[1]{0:T(128)} %bitcast.spot, s32[1,1]{1,0:T(1,128)S(6)} %copy.39.lengths, bf16[64,1152]{1,0:T(8,128)(2,1)} %front.1.p_low, bf16[1,64,5120]{2,1,0:T(8,128)(2,1)} %p_base.1, ...), custom_call_target="tpu_custom_call" | custom-call | flops 188743680 | bytes 12000000 | tf_op jit(solution)/shard_map/prep/pallas_call | solution.py:339
  18.7 29.7 %all-gather.2.cloned.1.call-done.key.value.low = bf16[1024,1152]{1,0:T(8,128)(2,1)} async-done(((bf16[64,1152]{1,0:T(8,128)(2,1)}), bf16[1024,1152]{1,0:T(8,128)(2,1)}) %all-gather.2.cloned.1.call-update) | async-done | bytes 2359312 | tf_op jit(solution)/shard_map/all_gather | solution.py:337
  48.4 35.4 %attend.1 = (bf16[1,64,4096]{2,1,0:T(8,128)(2,1)}, bf16[1,1,128,4096]{3,2,1,0:T(8,128)(2,1)}, bf16[16,4096]{1,0:T(8,128)(2,1)}, bf16[32,512]{1,0:T(8,128)(2,1)},...) custom-call(s32[1]{0:T(128)} %bitcast.spot, ...), custom_call_target="tpu_custom_call" | custom-call | flops 9663676416 | bytes 8000000 | tf_op jit(solution)/shard_map/attend/pallas_call | solution.py:395
  83.8 4.1 %all-to-all-start = ((bf16[16,16,128]{2,1,0:T(8,128)(2,1)}), bf16[16,16,128]{2,1,0:T(8,128)(2,1)S(1)}, u32[]{:S(2)}, u32[]{:S(2)}) async-start(bf16[16,16,128]{2,1,0:T(8,128)(2,1)} %get-tuple-element.33), calls=%async_computation | async-start | bytes 131072 | tf_op jit(solution)/shard_map/all_to_all | solution.py:464
  87.9 0.8 copy.29
  88.7 0.9 copy.27
  89.6 0.9 copy.28
  90.5 3.2 %all-to-all-done.fold_recv = bf16[16,16,128]{2,1,0:T(8,128)(2,1)S(1)} async-done(((bf16[16,16,128]{2,1,0:T(8,128)(2,1)}), bf16[16,16,128]{2,1,0:T(8,128)(2,1)S(1)}, u32[]{:S(2)}, u32[]{:S(2)}) %all-to-all-start) | async-done | bytes 65568 | tf_op jit(solution)/shard_map/all_to_all | solution.py:464
  93.7 0.6 copy-done
  94.4 3.7 %grads.1 = (bf16[48,5120]{1,0:T(8,128)(2,1)}, bf16[16,5120]{1,0:T(8,128)(2,1)}) custom-call(f32[16,192]{1,0:T(8,128)} %get-tuple-element.30.fold_q, f32[16,192]{1,0:T(8,128)} %get-tuple-element.31.lifted, bf16[32,128]{1,0:T(8,128)(2,1)} %get-tuple-element.32.fold_reply, bf16[16,16,128]{2,1,0:T(8,128)(2,1)} %copy-done, bf16[1,64,5120]{2,1,0:T(8,128)(2,1)} %p_hidden.1, ...), custom_call_target="tpu_custom_call" | custom-call | flops 125829120 | bytes 5000000 | tf_op jit(solution)/shard_map/grads/pallas_call | solution.py:466
  98.0 1.1 copy.25
  99.1 0.9 copy.26
  100.2 26.4 %all_to_all.15 = bf16[128,32,128]{2,1,0:T(8,128)(2,1)S(1)} all-to-all(bf16[128,32,128]{2,1,0:T(8,128)(2,1)S(1)} %bitcast.25), channel_id=1, replica_groups=mesh['ctx'=8,'resp'=16] {'ctx','resp'}, dimensions={0} | all-to-all | bytes 2097152 | tf_op jit(solution)/shard_map/all_to_all | solution.py:484
  126.6 0.2 reduce_sum.12
  126.8 0.1 broadcast_in_dim.14
  126.9 23.6 %all_to_all.16 = bf16[128,32,128]{2,1,0:T(8,128)(2,1)S(1)} all-to-all(bf16[128,32,128]{2,1,0:T(8,128)(2,1)S(1)} %broadcast_in_dim.14), channel_id=1, replica_groups=mesh['ctx'=8,'resp'=16] {'ctx','resp'}, dimensions={0} | all-to-all | bytes 2097152 | tf_op jit(solution)/shard_map/all_to_all | solution.py:486
  150.5 0.6 reshape.74
  151.2 0.8 reshape.75
  152.0 0.1 slice_convert_fusion
  152.1 1.1 reshape.76
  153.2 1.1 bitcast_bitcast_fusion
  (10 shorter events, 0.2 us)
Async XLA Ops:
  7.2 41.2 %all-gather.2.cloned.1.call-start = ((), (), s32[]{:S(2)}) async-start(), calls=%async_computation.3 | async-start | bytes 2506752 | tf_op jit(solution)/shard_map/all_gather | solution.py:337
  83.8 9.9 %all-to-all-start = ((bf16[16,16,128]{2,1,0:T(8,128)(2,1)}), bf16[16,16,128]{2,1,0:T(8,128)(2,1)S(1)}, u32[]{:S(2)}, u32[]{:S(2)}) async-start(bf16[16,16,128]{2,1,0:T(8,128)(2,1)} %get-tuple-element.33), calls=%async_computation | async-start | bytes 131072 | tf_op jit(solution)/shard_map/all_to_all | solution.py:464
  93.7 0.6 copy-start
Sparse Core Ops, SparseCore 0:
  10.3 38.0 all-gather.1

commit v2 on v1

v2 whole, which is shorter than its diff:
```python
import functools

import jax
import jax.numpy as jnp
import numpy as np
from jax import lax
from jax.experimental import pallas as pl
from jax.experimental.pallas import tpu as pltpu
from jax.sharding import Mesh
from jax.sharding import PartitionSpec as P

HEAD_DIM = 128
HALF = 64
RANK = 16
ROPE_BASE = 1000000.0
LOG2E = 1.4426950408889634
F32 = jnp.float32
BF16 = jnp.bfloat16
CTX = ("x", "z_hi")
RESP = ("z_lo", "y", "core")
CHIPS = ("x", "z_hi", "z_lo", "y")
SIZES = (4, 2, 2, 4, 2)
PAIR = [(0, 1), (1, 0)]

NN = (((1,), (0,)), ((), ()))
NT = (((1,), (1,)), ((), ()))
TN = (((0,), (0,)), ((), ()))


def mm(a, b, dims=NN):
    return lax.dot_general(a, b, dims, preferred_element_type=F32)


def rope_tables(count):
    rates = ROPE_BASE ** (-(np.arange(HALF, dtype=np.float64) * (2.0 / HEAD_DIM)))
    angle = np.arange(count, dtype=np.float64)[:, None] * rates[None, :]
    return np.cos(angle), np.sin(angle)


def rope(x, cos, sin):
    return x * cos + pltpu.roll(x, HALF, 1) * sin


def unrope(x, cos, sin):
    return x * cos - pltpu.roll(x, HALF, 1) * sin


def params(flops=0, nbytes=0, mib=36):
    return dict(
        compiler_params=pltpu.CompilerParams(vmem_limit_bytes=mib * 1024 * 1024),
        cost_estimate=pl.CostEstimate(flops=flops, bytes_accessed=nbytes, transcendentals=0),
    )


def kv_rows(hidden, base, down, kv_up, cos, sin):
    kv_width = kv_up.shape[2]
    low = mm(hidden, down, NT).astype(BF16)
    zero = jnp.zeros((RANK, kv_width), BF16)
    k_lift = jnp.concatenate([zero, kv_up[0], zero], axis=0)
    v_lift = jnp.concatenate([zero, zero, kv_up[1]], axis=0)
    key = base[:, :kv_width].astype(F32) + 2.0 * mm(low, k_lift)
    value = base[:, kv_width:].astype(F32) + 2.0 * mm(low, v_lift)
    heads = [
        rope(key[:, h : h + HEAD_DIM], cos, sin).astype(BF16)
        for h in range(0, kv_width, HEAD_DIM)
    ]
    return low, jnp.concatenate(heads, axis=1), value.astype(BF16)


def pad_low(low):
    return jnp.concatenate([low, jnp.zeros((low.shape[0], HEAD_DIM - 3 * RANK), BF16)], axis=1)


def front_kernel(spot, hidden, base, down, kv_up, cos, sin, out):
    low, key, value = kv_rows(hidden[0], base[0], down[...], kv_up[...], cos[...], sin[...])
    half = key.shape[1] // 2
    out[...] = jnp.concatenate(
        [key[:, :half], value[:, :half], pad_low(low), key[:, half:], value[:, half:]], axis=1
    )


def reply_kernel(
    lengths, p_low, p_out, r_hidden, r_base, r_out, down, kv_up, out_up, r_cos, r_sin,
    r_kv, lows, splits, low_t, lowered_t,
):
    pr = p_low.shape[0]
    rl = r_hidden.shape[2]
    r_low, r_key, r_value = kv_rows(
        r_hidden[0, 0], r_base[0, 0], down[...], kv_up[...], r_cos[...], r_sin[...]
    )
    r_low = pad_low(r_low)
    r_kv[...] = jnp.concatenate([r_key, r_value, r_low], axis=1)
    live = lax.broadcasted_iota(jnp.int32, (rl, RANK), 0) < lengths[0, 0]
    p_lowered = mm(p_out[0], out_up[...], NT)
    r_lowered = jnp.where(live, mm(r_out[0, 0], out_up[...], NT), 0.0)
    for low, lowered, at, n in ((p_low[...], p_lowered, 0, pr), (r_low, r_lowered, pr, rl)):
        lows[at : at + n, :] = low
        low_t[:, pl.ds(at, n)] = jnp.transpose(low.astype(F32))[: 3 * RANK].astype(BF16)
        high = lowered.astype(BF16)
        lost = (lowered - high.astype(F32)).astype(BF16)
        zero = jnp.zeros((n, HEAD_DIM - 2 * RANK), BF16)
        both = jnp.concatenate([high, lost, zero], axis=1)
        splits[at : at + n, :] = both
        lowered_t[:, pl.ds(at, n)] = jnp.transpose(both.astype(F32))[: 2 * RANK].astype(BF16)


def query_kernel(
    spot, lengths, lows, splits, p_base, p_gbase, r_base, r_gbase, q_up, out_down,
    p_cos, p_sin, r_cos, r_sin, query, push,
):
    pr = p_base.shape[1]
    rl = r_base.shape[2]
    wide = q_up.shape[1]
    live = lax.broadcasted_iota(jnp.int32, (rl, wide), 0) < lengths[0, 0]
    q_lift = jnp.concatenate([q_up[...], jnp.zeros((HEAD_DIM - RANK, wide), BF16)], axis=0)
    o_lift = jnp.concatenate(
        [out_down[...], out_down[...], jnp.zeros((HEAD_DIM - 2 * RANK, wide), BF16)], axis=0
    )
    for base, gbase, cos, sin, at, n in (
        (p_base[0], p_gbase[0], p_cos, p_sin, 0, pr),
        (r_base[0, 0], r_gbase[0, 0], r_cos, r_sin, pr, rl),
    ):
        q = base.astype(F32) + 2.0 * mm(lows[at : at + n, :], q_lift)
        for h in range(0, wide, HEAD_DIM):
            query[at : at + n, h : h + HEAD_DIM] = rope(
                q[:, h : h + HEAD_DIM], cos[...], sin[...]
            ).astype(BF16)
        up = gbase.astype(F32) + 2.0 * mm(splits[at : at + n, :], o_lift)
        if at:
            up = jnp.where(live, up, 0.0)
        push[at : at + n, :] = up.astype(BF16)


def attend_kernel(
    first, spot, lengths, query, push, key_a, key_b, value_a, value_b, low_a, low_b,
    r_key, r_value, r_low, low_t, lowered_t,
    q_up, kv_up, out_down, p_cos, p_sin, r_cos, r_sin, cos_t, sin_t, *others,
):
    if not first:
        fold_q_in, lifted_in, fold_kv_in, _, _ = others[:5]
        others = others[5:]
    (
        p_context, r_context, tiles, fold_q, lifted, fold_kv, fold_send, fold_reply,
        dk_t, dv_t, raw_q, mixed, keys, values, lows, bias,
    ) = others
    pr = p_context.shape[1]
    rl = r_context.shape[2]
    prompt = bias.shape[1]
    scale = HEAD_DIM ** (-0.5)
    step = scale * LOG2E
    heads = key_a.shape[1] // HEAD_DIM
    wide = query.shape[1] // heads
    share = wide // HEAD_DIM
    block = 512

    me = spot[0]
    places = []
    for other in (0, 1):
        for j in range(8):
            away, far = j // 2, j % 2
            z = jnp.bitwise_xor(me >> 3, far)
            y = jnp.bitwise_and((me >> 1) - away + 4, 3)
            c = jnp.bitwise_xor(jnp.bitwise_and(me, 1), other)
            places.append((other, j, pl.ds(pl.multiple_of((z * 8 + y * 2 + c) * pr, pr), pr)))

    row = lax.broadcasted_iota(jnp.int32, (pr, prompt), 0) + spot[0] * pr
    col = lax.broadcasted_iota(jnp.int32, (pr, prompt), 1)
    bias[...] = jnp.where(col <= row, 0.0, -jnp.inf)
    for other, j, rows in places:
        part = slice(j * pr, (j + 1) * pr)
        lows[rows, :] = (low_a, low_b)[other][part, :]
        for g in range(heads):
            cols = slice(g * HEAD_DIM, (g + 1) * HEAD_DIM)
            keys[g, rows, :] = (key_a, key_b)[other][part, cols]
            values[g, rows, :HEAD_DIM] = (value_a, value_b)[other][part, cols]
    lows[prompt:, :] = r_low[...]
    for g in range(heads):
        cols = slice(g * HEAD_DIM, (g + 1) * HEAD_DIM)
        keys[g, prompt:, :] = r_key[:, cols]
        values[g, prompt:, :HEAD_DIM] = r_value[:, cols]
        values[g, :, HEAD_DIM:] = jnp.ones((prompt + rl, HEAD_DIM), BF16)
    dk_t[...] = jnp.zeros_like(dk_t)
    dv_t[...] = jnp.zeros_like(dv_t)

    def stages(g, n, at, of, mask, keep, cos, sin, count):
        def stack(ref):
            return jnp.concatenate(
                [ref[at : at + n, h * HEAD_DIM : (h + 1) * HEAD_DIM] for h in of], axis=0
            )

        box = {}

        def scores():
            box["q"], box["p"] = stack(query), stack(push)
            box["score"] = mask(mm(box["q"], keys[g, :count, :], NT))

        def softmax():
            score = box.pop("score")
            top = jnp.max(score, axis=1, keepdims=True) * step
            box["weight"] = jnp.exp2(score * step - top).astype(BF16)

        def mix():
            box["summed"] = mm(box["weight"], values[g, :count, :])
            box["dprob"] = mm(box["p"], values[g, :count, :HEAD_DIM], NT)

        def backward():
            summed = box.pop("summed")
            share_of = 1.0 / summed[:, HEAD_DIM:]
            p = box.pop("p").astype(F32)
            context = keep((summed[:, :HEAD_DIM] * share_of).astype(BF16))
            delta = jnp.sum(context.astype(F32) * p, axis=1, keepdims=True)
            box["dscore"] = (box["weight"].astype(F32) * (box.pop("dprob") - delta)).astype(BF16)
            box["inverse"] = share_of * scale
            box["ps"] = (p * share_of).astype(BF16)
            box["qs"] = (box.pop("q").astype(F32) * box["inverse"]).astype(BF16)
            for i, h in enumerate(of):
                part = slice(i * n, (i + 1) * n)
                mixed[at : at + n, h * HEAD_DIM : (h + 1) * HEAD_DIM] = context[part]

        def products():
            dscore = box.pop("dscore")
            dv_t[g, :, :count] += mm(box.pop("ps"), box.pop("weight"), TN)
            dq = mm(dscore, keys[g, :count, :]) * box.pop("inverse")
            dk_t[g, :, :count] += mm(box.pop("qs"), dscore, TN)
            for i, h in enumerate(of):
                part = slice(i * n, (i + 1) * n)
                raw_q[at : at + n, h * HEAD_DIM : (h + 1) * HEAD_DIM] = unrope(
                    dq[part], cos[...], sin[...]
                ).astype(BF16)

        return scores, softmax, mix, backward, products

    p_heads = block // pr
    r_heads = block // rl

    def p_mask(score):
        seen = bias[...]
        return jnp.concatenate(
            [score[i * pr : (i + 1) * pr] + seen for i in range(p_heads)], axis=0
        )

    r_row = lax.broadcasted_iota(jnp.int32, (rl, rl), 0)
    r_col = lax.broadcasted_iota(jnp.int32, (rl, rl), 1)
    r_seen = jnp.concatenate([r_col <= r_row] * r_heads, axis=0)
    live = jnp.concatenate([r_row < lengths[0, 0]] * r_heads, axis=0)

    def r_mask(score):
        own = jnp.where(r_seen, score[:, prompt:], -jnp.inf)
        return jnp.concatenate([score[:, :prompt], own], axis=1)

    def finish(g):
        cols = slice(g * wide, (g + 1) * wide)
        context = mixed[:, cols]
        raw = raw_q[:, cols]
        p_context[0, :, cols] = mixed[:pr, cols]
        r_context[0, 0, :, cols] = mixed[pr:, cols]
        gq = (2.0 * mm(low_t[:RANK, :], raw)).astype(BF16)
        both = mm(lowered_t[...], context)
        god = (2.0 * (both[:RANK] + both[RANK:])).astype(BF16)
        first_tile = g * (2 * share + 2)
        for t in range(share):
            at = slice(t * HEAD_DIM, (t + 1) * HEAD_DIM)
            tiles[first_tile + t] = gq[:, at]
            tiles[first_tile + share + t] = god[:, at]
        upper, lower = dk_t[g, :HALF, :], dk_t[g, HALF:, :]
        cos, sin = cos_t[...], sin_t[...]
        raw_k = jnp.concatenate(
            [(upper * cos + lower * sin).astype(BF16), (lower * cos - upper * sin).astype(BF16)],
            axis=0,
        )
        raw_v = dv_t[g].astype(BF16)
        head = slice(g * HEAD_DIM, (g + 1) * HEAD_DIM)
        gk = jnp.transpose(mm(raw_k, lows[...]))
        gv = jnp.transpose(mm(raw_v, lows[...]))
        tiles[first_tile + 2 * share] = (2.0 * gk[RANK : 2 * RANK]).astype(BF16)
        tiles[first_tile + 2 * share + 1] = (2.0 * gv[2 * RANK : 3 * RANK]).astype(BF16)
        return (
            mm(q_up[:, cols], raw, NT),
            mm(out_down[:, cols], context, NT),
            mm(kv_up[0, :, head], raw_k),
            mm(kv_up[1, :, head], raw_v),
        )

    blocks = []
    for g in range(heads):
        for b in range(share // p_heads):
            of = [g * share + b * p_heads + i for i in range(p_heads)]
            blocks.append(stages(g, pr, 0, of, p_mask, lambda c: c, p_cos, p_sin, prompt))
        for b in range(share // r_heads):
            of = [g * share + b * r_heads + i for i in range(r_heads)]
            blocks.append(
                stages(
                    g, rl, pr, of, r_mask, lambda c: jnp.where(live, c, jnp.zeros_like(c)),
                    r_cos, r_sin, prompt + rl,
                )
            )
    each = len(blocks) // heads
    if first:
        folds = None
    else:
        folds = [fold_q_in[...], lifted_in[...], fold_kv_in[:RANK, :], fold_kv_in[RANK:, :]]
    for at in range(len(blocks) + 1):
        if at < len(blocks):
            blocks[at][0]()
        if at:
            blocks[at - 1][3]()
            blocks[at - 1][4]()
        if at < len(blocks):
            blocks[at][1]()
            blocks[at][2]()
        if at and at % each == 0:
            new = finish(at // each - 1)
            folds = new if folds is None else [x + y for x, y in zip(folds, new)]
    fold_q[...] = folds[0]
    lifted[...] = folds[1]
    fk, fv = folds[2], folds[3]
    fold_kv[:RANK, :] = fk
    fold_kv[RANK:, :] = fv
    for r in range(prompt // pr):
        cols = slice(r * pr, (r + 1) * pr)
        fold_send[r] = jnp.concatenate([fk[:, cols], fv[:, cols]], axis=1).astype(BF16)
    fold_reply[...] = jnp.concatenate([fk[:, prompt:], fv[:, prompt:]], axis=0).astype(BF16)


def grads_kernel(
    spot, fold_q, lifted, fold_reply, fold_recv, p_hidden, r_hidden, p_out, r_out, tiles_a, tiles_b,
    keep, give, held,
):
    pr = p_hidden.shape[1]
    fq = fold_q[...].astype(BF16)
    up = lifted[...].astype(BF16)
    own = jnp.sum(fold_recv[...].astype(F32), axis=0).astype(BF16)
    fp = jnp.concatenate([fq[:, :pr], own[:, :pr], own[:, pr:]], axis=0)
    fr = jnp.concatenate([fq[:, pr:], fold_reply[...]], axis=0)
    wide = p_hidden.shape[2] // HEAD_DIM
    down = (2.0 * (mm(fp, p_hidden[0]) + mm(fr, r_hidden[0, 0]))).astype(BF16)
    grad_up = (2.0 * (mm(up[:, :pr], p_out[0]) + mm(up[:, pr:], r_out[0, 0]))).astype(BF16)
    for t in range(wide):
        cols = slice(t * HEAD_DIM, (t + 1) * HEAD_DIM)
        for j in range(3):
            held[j * wide + t] = down[j * RANK : (j + 1) * RANK, cols]
        held[3 * wide + t] = grad_up[:, cols]
    at = 4 * wide
    small = tiles_a.shape[0]
    held[at : at + small] = tiles_a[...]
    held[at + small : at + 2 * small] = tiles_b[...]
    left = held.shape[0] - at - 2 * small
    held[at + 2 * small :] = jnp.zeros((left, RANK, HEAD_DIM), BF16)
    half = held.shape[0] // 2
    core = jnp.bitwise_and(spot[0], 1)

    @pl.when(core == 0)
    def _():
        keep[...] = held[:half]
        give[...] = held[half:]

    @pl.when(core == 1)
    def _():
        keep[...] = held[half:]
        give[...] = held[:half]


def unpack_kernel(spot, mine, theirs, down, gq, gkv, god, up, held):
    half = mine.shape[0]
    core = jnp.bitwise_and(spot[0], 1)

    @pl.when(core == 0)
    def _():
        held[:half] = mine[...]
        held[half:] = theirs[...]

    @pl.when(core == 1)
    def _():
        held[half:] = mine[...]
        held[:half] = theirs[...]

    def cols(t):
        return slice(t * HEAD_DIM, (t + 1) * HEAD_DIM)

    wide = down.shape[1] // HEAD_DIM
    for t in range(wide):
        for j in range(3):
            down[j * RANK : (j + 1) * RANK, cols(t)] = held[j * wide + t].astype(F32)
        up[:, cols(t)] = held[3 * wide + t].astype(F32)
    at = 4 * wide
    heads = gkv.shape[1] // HEAD_DIM
    share = gq.shape[1] // HEAD_DIM // heads
    for g in range(heads):
        for t in range(share):
            gq[:, cols(g * share + t)] = held[at + t].astype(F32)
            god[:, cols(g * share + t)] = held[at + share + t].astype(F32)
        gkv[:RANK, cols(g)] = held[at + 2 * share].astype(F32)
        gkv[RANK:, cols(g)] = held[at + 2 * share + 1].astype(F32)
        at += 2 * share + 2


def whole(shape):
    return pl.BlockSpec(shape, lambda *_: (0,) * len(shape))


def shifted(x, axis, by):
    n = lax.axis_size(axis)
    return lax.ppermute(x, axis, [(i, (i + by) % n) for i in range(n)])


def chips_of(pair):
    return [pair] + [shifted(pair, "y", k) for k in (1, 2, 3)]


def per_device(
    prompt_hidden,
    prompt_base,
    reply_hidden,
    reply_base,
    reply_lengths,
    adapter_down,
    query_up_weight,
    key_value_up_weight,
    output_down,
    output_up,
    prompt_grad_out,
    prompt_grad_base,
    reply_grad_out,
    reply_grad_base,
):
    group = lax.axis_size(RESP)
    pr = prompt_hidden.shape[1]
    rl = reply_hidden.shape[2]
    d = prompt_hidden.shape[2]
    prompt = pr * group
    q_width = query_up_weight.shape[1]
    kv_width = key_value_up_weight.shape[2]
    heads = kv_width // HEAD_DIM
    each = heads // 2
    qb = q_width // heads
    share = qb // HEAD_DIM
    rows = pr + rl
    wide = 2 * kv_width + HEAD_DIM
    low_at = 2 * kv_width // HEAD_DIM

    spot = lax.axis_index(RESP).astype(jnp.int32)[None]
    down = jnp.transpose(adapter_down, (0, 2, 1)).reshape(3 * RANK, d)
    out_down = jnp.transpose(output_down)
    cos, sin = rope_tables(prompt + rl)
    cos_rows = jnp.asarray(np.concatenate([cos, cos], axis=1), F32)
    sin_rows = jnp.asarray(np.concatenate([-sin, sin], axis=1), F32)
    cos_t = jnp.asarray(cos.T, F32)
    sin_t = jnp.asarray(sin.T, F32)
    p_table = pl.BlockSpec((pr, HEAD_DIM), lambda i, s: (s[0], 0))
    r_table = pl.BlockSpec((rl, HEAD_DIM), lambda i, *_: (prompt // rl, 0))

    own_kv = pl.pallas_call(
        front_kernel,
        grid_spec=pltpu.PrefetchScalarGridSpec(
            num_scalar_prefetch=1,
            grid=(1,),
            in_specs=[
                whole((1, pr, d)),
                pl.BlockSpec((1, pr, 2 * kv_width), lambda i, s: (0, 0, q_width // (2 * kv_width))),
                whole((3 * RANK, d)),
                whole((2, RANK, kv_width)),
                p_table,
                p_table,
            ],
            out_specs=whole((pr, wide)),
        ),
        out_shape=jax.ShapeDtypeStruct((pr, wide), BF16),
        name="front",
        **params(2 * pr * d * 48, 2_000_000, 56),
    )(spot, prompt_hidden, prompt_base, down, key_value_up_weight, cos_rows, sin_rows)

    far_kv = lax.ppermute(own_kv, "z_lo", PAIR)

    reply_kv, lows, splits, low_t, lowered_t = pl.pallas_call(
        reply_kernel,
        grid=(1,),
        in_specs=[
            pl.BlockSpec(memory_space=pltpu.SMEM),
            pl.BlockSpec((pr, HEAD_DIM), lambda i: (0, kv_width // HEAD_DIM)),
            whole((1, pr, d)),
            whole((1, 1, rl, d)),
            pl.BlockSpec(
                (1, 1, rl, 2 * kv_width), lambda i: (0, 0, 0, q_width // (2 * kv_width))
            ),
            whole((1, 1, rl, d)),
            whole((3 * RANK, d)),
            whole((2, RANK, kv_width)),
            whole((RANK, d)),
            r_table,
            r_table,
        ],
        out_specs=[
            whole((rl, wide)),
            whole((rows, HEAD_DIM)),
            whole((rows, HEAD_DIM)),
            whole((3 * RANK, rows)),
            whole((2 * RANK, rows)),
        ],
        out_shape=[
            jax.ShapeDtypeStruct((rl, wide), BF16),
            jax.ShapeDtypeStruct((rows, HEAD_DIM), BF16),
            jax.ShapeDtypeStruct((rows, HEAD_DIM), BF16),
            jax.ShapeDtypeStruct((3 * RANK, rows), BF16),
            jax.ShapeDtypeStruct((2 * RANK, rows), BF16),
        ],
        name="reply",
        **params(4 * rows * d * 48, 6_000_000, 56),
    )(
        reply_lengths, own_kv, prompt_grad_out, reply_hidden, reply_base, reply_grad_out, down,
        key_value_up_weight, output_up, cos_rows, sin_rows,
    )

    own_kv, far_kv, lows, splits = lax.optimization_barrier((own_kv, far_kv, lows, splits))
    cut = kv_width + HEAD_DIM
    first_pair = jnp.concatenate([own_kv[:, :cut], far_kv[:, :cut]], axis=0)
    second_pair = jnp.concatenate([own_kv[:, cut:], far_kv[:, cut:]], axis=0)
    first_parts = chips_of(first_pair)

    def head_cols(n, width, shift=0):
        return pl.BlockSpec((n, width), lambda i, s: (0, i + shift))

    def cols3(shift=0):
        return pl.BlockSpec((1, pr, qb), lambda i, s: (0, 0, i + shift))

    def cols4(shift=0):
        return pl.BlockSpec((1, 1, rl, qb), lambda i, s: (0, 0, 0, i + shift))

    query, push = pl.pallas_call(
        query_kernel,
        grid_spec=pltpu.PrefetchScalarGridSpec(
            num_scalar_prefetch=1,
            grid=(heads,),
            in_specs=[
                pl.BlockSpec(memory_space=pltpu.SMEM),
                whole((rows, HEAD_DIM)),
                whole((rows, HEAD_DIM)),
                cols3(),
                cols3(),
                cols4(),
                cols4(),
                head_cols(RANK, qb),
                head_cols(RANK, qb),
                p_table,
                p_table,
                r_table,
                r_table,
            ],
            out_specs=[head_cols(rows, qb), head_cols(rows, qb)],
        ),
        out_shape=[
            jax.ShapeDtypeStruct((rows, q_width), BF16),
            jax.ShapeDtypeStruct((rows, q_width), BF16),
        ],
        name="query",
        **params(4 * rows * q_width * 128, 8_000_000, 48),
    )(
        spot, reply_lengths, lows, splits, prompt_base, prompt_grad_base, reply_base,
        reply_grad_base, query_up_weight, out_down, cos_rows, sin_rows, cos_rows, sin_rows,
    )

    first_parts, second_pair, query, push = lax.optimization_barrier(
        (first_parts, second_pair, query, push)
    )
    first_own = jnp.concatenate(first_parts, axis=0)
    first_other = lax.ppermute(first_own, "core", PAIR)
    second_parts = chips_of(second_pair)
    count = prompt // 2
    low_block = pl.BlockSpec((count, HEAD_DIM), lambda i, s: (0, kv_width // HEAD_DIM))

    def attend(own, other, at, before):
        first = before is None
        kb = each * HEAD_DIM
        in_specs = [
            pl.BlockSpec(memory_space=pltpu.SMEM),
            head_cols(rows, each * qb, at),
            head_cols(rows, each * qb, at),
            head_cols(count, kb),
            head_cols(count, kb),
            head_cols(count, kb, 1),
            head_cols(count, kb, 1),
            low_block,
            low_block,
            head_cols(rl, kb, at),
            head_cols(rl, kb, heads // each + at),
            pl.BlockSpec((rl, HEAD_DIM), lambda i, s: (0, low_at)),
            whole((3 * RANK, rows)),
            whole((2 * RANK, rows)),
            head_cols(RANK, each * qb, at),
            pl.BlockSpec((2, RANK, kb), lambda i, s: (0, 0, i + at)),
            head_cols(RANK, each * qb, at),
            p_table,
            p_table,
            r_table,
            r_table,
            whole((HALF, prompt + rl)),
            whole((HALF, prompt + rl)),
        ]
        operands = [
            spot, reply_lengths, query, push, own, other, own, other, first_own, first_other,
            reply_kv, reply_kv, reply_kv, low_t, lowered_t, query_up_weight, key_value_up_weight,
            out_down, cos_rows, sin_rows, cos_rows, sin_rows, cos_t, sin_t,
        ]
        aliases = {}
        if not first:
            aliases = {len(operands) + 3: 0, len(operands) + 4: 1}
            in_specs += [
                whole((RANK, rows)),
                whole((RANK, rows)),
                whole((2 * RANK, prompt + rl)),
                pl.BlockSpec(memory_space=pl.ANY),
                pl.BlockSpec(memory_space=pl.ANY),
            ]
            operands += list(before)
        per_head = 2 * share + 2
        return pl.pallas_call(
            functools.partial(attend_kernel, first),
            grid_spec=pltpu.PrefetchScalarGridSpec(
                num_scalar_prefetch=1,
                grid=(1,),
                in_specs=in_specs,
                out_specs=[
                    pl.BlockSpec((1, pr, each * qb), lambda i, s: (0, 0, i + at)),
                    pl.BlockSpec((1, 1, rl, each * qb), lambda i, s: (0, 0, 0, i + at)),
                    whole((each * per_head, RANK, HEAD_DIM)),
                    whole((RANK, rows)),
                    whole((RANK, rows)),
                    whole((2 * RANK, prompt + rl)),
                    whole((group, RANK, 2 * pr)),
                    whole((2 * RANK, rl)),
                ],
                scratch_shapes=[
                    pltpu.VMEM((each, HEAD_DIM, prompt + rl), F32),
                    pltpu.VMEM((each, HEAD_DIM, prompt + rl), F32),
                    pltpu.VMEM((rows, each * qb), BF16),
                    pltpu.VMEM((rows, each * qb), BF16),
                    pltpu.VMEM((each, prompt + rl, HEAD_DIM), BF16),
                    pltpu.VMEM((each, prompt + rl, 2 * HEAD_DIM), BF16),
                    pltpu.VMEM((prompt + rl, HEAD_DIM), BF16),
                    pltpu.VMEM((pr, prompt), F32),
                ],
            ),
            out_shape=[
                jax.ShapeDtypeStruct((1, pr, q_width), BF16),
                jax.ShapeDtypeStruct((1, 1, rl, q_width), BF16),
                jax.ShapeDtypeStruct((each * per_head, RANK, HEAD_DIM), BF16),
                jax.ShapeDtypeStruct((RANK, rows), F32),
                jax.ShapeDtypeStruct((RANK, rows), F32),
                jax.ShapeDtypeStruct((2 * RANK, prompt + rl), F32),
                jax.ShapeDtypeStruct((group, RANK, 2 * pr), BF16),
                jax.ShapeDtypeStruct((2 * RANK, rl), BF16),
            ],
            input_output_aliases=aliases,
            name="attend",
            **params(12 * rows * prompt * q_width // 2, 8_000_000),
        )(*operands)

    p_half, r_half, tiles_a, fold_q, lifted, fold_kv, _, _ = attend(
        first_own, first_other, 0, None
    )
    second_parts, fold_q, lifted, fold_kv = lax.optimization_barrier(
        (second_parts, fold_q, lifted, fold_kv)
    )
    second_own = jnp.concatenate(second_parts, axis=0)
    second_other = lax.ppermute(second_own, "core", PAIR)
    p_context, r_context, tiles_b, fold_q, lifted, _, fold_send, fold_reply = attend(
        second_own, second_other, 1, (fold_q, lifted, fold_kv, p_half, r_half)
    )

    fold_recv = lax.all_to_all(fold_send, RESP, 0, 0, tiled=True)

    slots = 2 * lax.axis_size(CHIPS) * 2
    half = slots // 2
    keep, give = pl.pallas_call(
        grads_kernel,
        grid_spec=pltpu.PrefetchScalarGridSpec(
            num_scalar_prefetch=1,
            grid=(1,),
            in_specs=[
                whole((RANK, rows)),
                whole((RANK, rows)),
                whole((2 * RANK, rl)),
                whole((group, RANK, 2 * pr)),
                whole((1, pr, d)),
                whole((1, 1, rl, d)),
                whole((1, pr, d)),
                whole((1, 1, rl, d)),
                whole(tiles_a.shape),
                whole(tiles_b.shape),
            ],
            out_specs=[whole((half, RANK, HEAD_DIM)), whole((half, RANK, HEAD_DIM))],
            scratch_shapes=[pltpu.VMEM((slots, RANK, HEAD_DIM), BF16)],
        ),
        out_shape=[jax.ShapeDtypeStruct((half, RANK, HEAD_DIM), BF16)] * 2,
        name="grads",
        **params(2 * rows * d * 64, 5_000_000),
    )(
        spot, fold_q, lifted, fold_reply, fold_recv, prompt_hidden, reply_hidden, prompt_grad_out,
        reply_grad_out, tiles_a, tiles_b,
    )

    chips = lax.axis_size(CHIPS)
    got = lax.ppermute(give, "core", PAIR)
    paired = (keep.astype(F32) + got.astype(F32)).astype(BF16)
    spread = lax.all_to_all(
        paired.reshape(chips, -1, HEAD_DIM), CHIPS, 0, 0, tiled=True
    )
    total = jnp.sum(spread.astype(F32), axis=0).astype(BF16)
    mine = lax.all_to_all(
        jnp.broadcast_to(total[None], spread.shape), CHIPS, 0, 0, tiled=True
    ).reshape(half, RANK, HEAD_DIM)
    theirs = lax.ppermute(mine, "core", PAIR)

    shapes = [(3 * RANK, d), (RANK, q_width), (2 * RANK, kv_width), (RANK, q_width), (RANK, d)]
    sum_down, sum_q, sum_kv, sum_od, sum_up = pl.pallas_call(
        unpack_kernel,
        grid_spec=pltpu.PrefetchScalarGridSpec(
            num_scalar_prefetch=1,
            grid=(1,),
            in_specs=[whole((half, RANK, HEAD_DIM))] * 2,
            out_specs=[whole(x) for x in shapes],
            scratch_shapes=[pltpu.VMEM((slots, RANK, HEAD_DIM), BF16)],
        ),
        out_shape=[jax.ShapeDtypeStruct(x, F32) for x in shapes],
        name="unpack",
        **params(0, 3_000_000),
    )(spot, mine, theirs)
    return (
        p_context,
        r_context,
        jnp.transpose(sum_down.reshape(3, RANK, d), (0, 2, 1)),
        sum_q,
        sum_kv.reshape(2, RANK, kv_width),
        jnp.transpose(sum_od),
        sum_up,
    )


def solution(mesh):
    fine = Mesh(mesh.devices.reshape(SIZES), CTX + RESP)
    return jax.shard_map(
        per_device,
        mesh=fine,
        in_specs=(
            P(CTX, RESP, None),
            P(CTX, RESP, None),
            P(CTX, RESP, None, None),
            P(CTX, RESP, None, None),
            P(CTX, RESP),
            P(),
            P(),
            P(),
            P(),
            P(),
            P(CTX, RESP, None),
            P(CTX, RESP, None),
            P(CTX, RESP, None, None),
            P(CTX, RESP, None, None),
        ),
        out_specs=(P(CTX, RESP, None), P(CTX, RESP, None, None), P(), P(), P(), P(), P()),
        check_vma=False,
    )
```

time: 162 us -> 117 us (0.72)
  waiting for transfers between devices: 32.9 us -> 9.62 us
  between operations: 14.8 us -> 1.66 us
  Pallas kernels: 49.9 us -> 40.2 us
  starting transfers between devices: 4.16 us -> 12.6 us
  local copies, waits for them, and re-layouts: 9.13 us -> 4.73 us
  blocking collectives: 49.9 us -> 47.5 us
    all_gather x1 -> x0, waiting for transfers between devices: 29.7 us -> none  [per_device(): all_kv = lax.all_gather(own_kv, 'resp', axis=0, tiled=True)]
    ppermute x0 -> x11, starting transfers between devices: none -> 12.6 us  [the longest x6 5.33 us: shifted(): return lax.ppermute(x, axis, [(i, (i + by) % n) for i in range(n)])]
    pallas_call x3 -> x6, Pallas kernels: 47.3 us -> 37.7 us  [the longest x2 27.7 us: attend(): pl.pallas_call(functools.partial(attend_kernel, first), grid_spec=pltpu.P...]
    ppermute x0 -> x11, waiting for transfers between devices: none -> 9.62 us  [the longest x6 4.76 us: shifted(): return lax.ppermute(x, axis, [(i, (i + by) % n) for i in range(n)])]
    all_to_all x1 -> x0, starting transfers between devices: 4.12 us -> none  [per_device(): fold_recv = lax.all_to_all(fold_send, 'resp', 0, 0, tiled=True)]
    all_to_all x1 -> x0, waiting for transfers between devices: 3.19 us -> none  [per_device(): fold_recv = lax.all_to_all(fold_send, 'resp', 0, 0, tiled=True)]
    all_to_all x2 -> x3, blocking collectives: 49.9 us -> 47.5 us  [the longest x1 20.5 us: per_device(): lax.all_to_all(paired.reshape(chips, -1, HEAD_DIM), CHIPS, 0, 0, tiled=True)]
    transpose x2 -> x0, local copies, waits for them, and re-layouts: 2.2 us -> none  [the longest x1 1.1 us: per_device(): jnp.transpose(sum_down.reshape(3, RANK, d), (0, 2, 1))]
  transfers between devices with their start and end apart: 2 -> 11, of which waited for: 2 -> 5; matrix products, arithmetic and copies ran while one was open for 2% -> 0% of each run, Pallas kernels for 5% -> 19%
where the time goes in v2:
time: 117 us
  blocking collectives  47.5 us (41%)
  Pallas kernels  40.2 us (34%)
  starting transfers between devices  12.6 us (11%)
  waiting for transfers between devices  9.62 us (8%)
  local copies, waits for them, and re-layouts  4.73 us (4%)
  between operations  1.66 us (1%)
    pallas_call x2, Pallas kernels, attend(): pl.pallas_call(functools.partial(attend_kernel, first), grid_spec=pltpu.P...  27.7 us
    all_to_all x1, blocking collectives, per_device(): lax.all_to_all(paired.reshape(chips, -1, HEAD_DIM), CHIPS, 0, 0, tiled=True)  20.5 us
    all_to_all x1, blocking collectives, per_device(): lax.all_to_all(jnp.broadcast_to(total[None], spread.shape), CHIPS, 0, 0,...  15.5 us
    all_to_all x1, blocking collectives, per_device(): fold_recv = lax.all_to_all(fold_send, RESP, 0, 0, tiled=True)  11.4 us
    ppermute x6, starting transfers between devices, shifted(): return lax.ppermute(x, axis, [(i, (i + by) % n) for i in range(n)])  5.33 us
    ppermute x6, waiting for transfers between devices, shifted(): return lax.ppermute(x, axis, [(i, (i + by) % n) for i in range(n)])  4.76 us
    unnamed x52, local copies, waits for them, and re-layouts  4.59 us
    pallas_call x1, Pallas kernels, per_device(): pl.pallas_call(reply_kernel, grid=(1,), in_specs=[pl.BlockSpec(memory_spa...  4.29 us
  transfers between devices with their start and end apart: 11, of which 5 were waited for; matrix products, arithmetic and copies ran while one was open for 0% of the time, Pallas kernels for 19%

profile of v2, /device:TPU:1, one launch (start us, length us, event | category | flops | bytes accessed | tf_op | source)
XLA Modules:
  0.0 116.6 jit_solution(4734591194589645635)
XLA Ops:
  0.6 2.6 %front.1.p_low = bf16[64,1152]{1,0:T(8,128)(2,1)} custom-call(s32[1]{0:T(128)} %bitcast.spot, bf16[1,64,5120]{2,1,0:T(8,128)(2,1)} %p_hidden.1, bf16[1,64,5120]{2,1,0:T(8,128)(2,1)} %p_base.1, bf16[48,5120]{1,0:T(8,128)(2,1)} %bitcast.18, bf16[2,16,512]{2,1,0:T(8,128)(2,1)} %kv_up.7, f32[1152,128]{1,0:T(8,128)} %constant.26.clone.cos.r_cos.p_cos, ...), custom_call_target="tpu_custom_call" | custom-call | flops 31457280 | bytes 2000000 | tf_op jit(solution)/shard_map/front/pallas_call | solution.py:452
  3.2 2.5 %collective-permute-start = (bf16[64,1152]{1,0:T(8,128)(2,1)}, bf16[64,1152]{1,0:T(8,128)(2,1)S(1)}, u32[]{:S(2)}, u32[]{:S(2)}) collective-permute-start(bf16[64,1152]{1,0:T(8,128)(2,1)} %front.1.p_low), channel_id=1, source_target_pairs={{0,8},{8,0},{1,9},{9,1},{2,10},{10,2},{3,11},{11,3},{4,12},{12,4},... | collective-permute-start | bytes 442376 | tf_op jit(solution)/shard_map/ppermute | solution.py:472
  6.4 4.3 %reply.1 = (bf16[128,1152]{1,0:T(8,128)(2,1)}, bf16[192,128]{1,0:T(8,128)(2,1)}, bf16[192,128]{1,0:T(8,128)(2,1)}, bf16[48,192]{1,0:T(8,128)(2,1)}, bf16[32,192]{1,0:T(8,128)(2,1)}) custom-call(s32[1,1]{1,0:T(1,128)S(6)} %copy.35.lengths, bf16[64,1152]{1,0:T(8,128)(2,1)} %front.1.p_low, bf16[1,64,5120]{2,1,0:T(8,128)(2,1)} %p_out.3, ...), custom_call_target="tpu_custom_call" | custom-call | flops 188743680 | bytes 6000000 | tf_op jit(solution)/shard_map/reply/pallas_call | solution.py:474
  10.8 2.8 %collective-permute-start.3 = (bf16[128,640]{1,0:T(8,128)(2,1)S(1)}, bf16[128,640]{1,0:T(8,128)(2,1)S(1)}, u32[]{:S(2)}, u32[]{:S(2)}) collective-permute-start(bf16[128,640]{1,0:T(8,128)(2,1)S(1)} %pad_maximum_fusion), channel_id=1, source_target_pairs={{0,6},{2,0},{4,2},{6,4},{1,7},{3,1},{5,3},{7,5},{8,14},{10,8},{12,... | collective-permute-start | bytes 491528 | tf_op jit(solution)/shard_map/ppermute | solution.py:403
  13.9 0.7 collective-permute-start.1
  14.7 0.8 copy-done.13
  15.5 0.8 copy-done.14
  16.3 3.5 %query.1 = (bf16[192,4096]{1,0:T(8,128)(2,1)}, bf16[192,4096]{1,0:T(8,128)(2,1)}) custom-call(s32[1]{0:T(128)} %bitcast.spot, s32[1,1]{1,0:T(1,128)S(6)} %copy.35.lengths, bf16[192,128]{1,0:T(8,128)(2,1)S(1)} %copy-done.13, bf16[192,128]{1,0:T(8,128)(2,1)S(1)} %copy-done.14, bf16[1,64,5120]{2,1,0:T(8,128)(2,1)S(1)} %copy-done.7, ...), custom_call_target="tpu_custom_call" | custom-call | flops 402653184 | bytes 8000000 | tf_op jit(solution)/shard_map/query/pallas_call | solution.py:528
  19.9 4.7 %collective-permute-done.1 = bf16[128,640]{1,0:T(8,128)(2,1)S(1)} collective-permute-done((bf16[128,640]{1,0:T(8,128)(2,1)S(1)}, bf16[128,640]{1,0:T(8,128)(2,1)S(1)}, u32[]{:S(2)}, u32[]{:S(2)}) %collective-permute-start.1) | collective-permute-done | bytes 163872 | tf_op jit(solution)/shard_map/ppermute | solution.py:403
  24.8 0.6 collective-permute-start.7
  26.0 0.8 collective-permute-start.4
  27.2 1.4 %copy-done.15 = bf16[192,4096]{1,0:T(8,128)(2,1)S(1)} copy-done((bf16[192,4096]{1,0:T(8,128)(2,1)S(1)}, bf16[192,4096]{1,0:T(8,128)(2,1)}, u32[]{:S(2)}) %copy-start.15) | copy-done | bytes 1572888
  28.6 1.4 %copy-done.16 = bf16[192,4096]{1,0:T(8,128)(2,1)S(1)} copy-done((bf16[192,4096]{1,0:T(8,128)(2,1)S(1)}, bf16[192,4096]{1,0:T(8,128)(2,1)}, u32[]{:S(2)}) %copy-start.16) | copy-done | bytes 1572888
  30.0 14.0 %attend.2 = (bf16[1,64,4096]{2,1,0:T(8,128)(2,1)}, bf16[1,1,128,4096]{3,2,1,0:T(8,128)(2,1)}, bf16[36,16,128]{2,1,0:T(8,128)(2,1)S(1)}, f32[16,192]{1,0:T(8,128)...) custom-call(s32[1]{0:T(128)} %bitcast.spot, ...), custom_call_target="tpu_custom_call" | custom-call | flops 4831838208 | bytes 8000000 | tf_op jit(solution)/shard_map/attend/pallas_call | solution.py:615
  44.5 1.5 %collective-permute-done.8.key_b.value_b = bf16[512,512]{1,0:T(8,128)(2,1)S(1)} collective-permute-done((bf16[512,512]{1,0:T(8,128)(2,1)S(1)}, bf16[512,512]{1,0:T(8,128)(2,1)S(1)}, u32[]{:S(2)}, u32[]{:S(2)}) %collective-permute-start.8) | collective-permute-done | bytes 524320 | tf_op jit(solution)/shard_map/ppermute | solution.py:664
  46.1 13.7 %attend.3 = (bf16[1,64,4096]{2,1,0:T(8,128)(2,1)}, bf16[1,1,128,4096]{3,2,1,0:T(8,128)(2,1)}, bf16[36,16,128]{2,1,0:T(8,128)(2,1)S(1)}, f32[16,192]{1,0:T(8,128)...) custom-call(s32[1]{0:T(128)} %bitcast.spot, ...), custom_call_target="tpu_custom_call", output_to_operand_aliasing={{0}: (27, {}), {1}: (28, {})} | custom-call | flops 4831838208 | bytes 8000000 | tf_op jit(solution)/shard_map/attend/pallas_call | solution.py:615
  59.8 11.4 %all_to_all.15.fold_recv = bf16[16,16,128]{2,1,0:T(8,128)(2,1)S(1)} all-to-all(bf16[16,16,128]{2,1,0:T(8,128)(2,1)S(1)} %get-tuple-element.87), channel_id=1, replica_groups=mesh['x'=4,'z_hi'=2,'z_lo'=2,'y'=4,'core'=2] {'z_lo','y','core'}, dimensions={0} | all-to-all | bytes 131072 | tf_op jit(solution)/shard_map/all_to_all | solution.py:669
  71.2 0.9 grads.1
  72.5 1.5 %collective-permute-done.9 = bf16[128,16,128]{2,1,0:T(8,128)(2,1)S(1)} collective-permute-done((bf16[128,16,128]{2,1,0:T(8,128)(2,1)S(1)}, bf16[128,16,128]{2,1,0:T(8,128)(2,1)S(1)}, u32[]{:S(2)}, u32[]{:S(2)}) %collective-permute-start.9) | collective-permute-done | bytes 524320 | tf_op jit(solution)/shard_map/ppermute | solution.py:702
  74.2 20.5 %all_to_all.16 = bf16[64,32,128]{2,1,0:T(8,128)(2,1)S(1)} all-to-all(bf16[64,32,128]{2,1,0:T(8,128)(2,1)S(1)} %bitcast.17), channel_id=1, replica_groups=mesh['x'=4,'z_hi'=2,'z_lo'=2,'y'=4,'core'=2] {'x','z_hi','z_lo','y'}, dimensions={0} | all-to-all | bytes 1048576 | tf_op jit(solution)/shard_map/all_to_all | solution.py:704
  94.9 15.5 %all_to_all.17 = bf16[64,32,128]{2,1,0:T(8,128)(2,1)S(1)} all-to-all(bf16[64,32,128]{2,1,0:T(8,128)(2,1)S(1)} %broadcast_in_dim.10), channel_id=1, replica_groups=mesh['x'=4,'z_hi'=2,'z_lo'=2,'y'=4,'core'=2] {'x','z_hi','z_lo','y'}, dimensions={0} | all-to-all | bytes 1048576 | tf_op jit(solution)/shard_map/all_to_all | solution.py:708
  110.5 3.2 %collective-permute-start.10 = (bf16[128,16,128]{2,1,0:T(8,128)(2,1)S(1)}, bf16[128,16,128]{2,1,0:T(8,128)(2,1)S(1)}, u32[]{:S(2)}, u32[]{:S(2)}) collective-permute-start(bf16[128,16,128]{2,1,0:T(8,128)(2,1)S(1)} %bitcast.12), channel_id=1, source_target_pairs={{0,1},{1,0},{2,3},{3,2},{4,5},{5,4},{6,7},{7,6},{8,9},{9,8},{10,11... | collective-permute-start | bytes 1572872 | tf_op jit(solution)/shard_map/ppermute | solution.py:711
  113.7 1.5 %collective-permute-done.10.theirs = bf16[128,16,128]{2,1,0:T(8,128)(2,1)S(1)} collective-permute-done((bf16[128,16,128]{2,1,0:T(8,128)(2,1)S(1)}, bf16[128,16,128]{2,1,0:T(8,128)(2,1)S(1)}, u32[]{:S(2)}, u32[]{:S(2)}) %collective-permute-start.10) | collective-permute-done | bytes 524320 | tf_op jit(solution)/shard_map/ppermute | solution.py:711
  115.2 1.3 %unpack.1 = (f32[48,5120]{1,0:T(8,128)}, f32[16,4096]{1,0:T(8,128)}, f32[32,512]{1,0:T(8,128)}, f32[16,4096]{1,0:T(8,128)}, f32[16,5120]{1,0:T(8,128)}) custom-call(s32[1]{0:T(128)} %bitcast.spot, bf16[128,16,128]{2,1,0:T(8,128)(2,1)S(1)} %bitcast.13, bf16[128,16,128]{2,1,0:T(8,128)(2,1)S(1)} %collective-permute-done.10.theirs), custom_call_target="tpu_custom_call" | custom-call | bytes 3000000 | tf_op jit(solution)/shard_map/unpack/pallas_call | solution.py:714
  (71 shorter events, 2.8 us)
Async XLA Ops:
  3.2 7.5 %collective-permute-start = (bf16[64,1152]{1,0:T(8,128)(2,1)}, bf16[64,1152]{1,0:T(8,128)(2,1)S(1)}, u32[]{:S(2)}, u32[]{:S(2)}) collective-permute-start(bf16[64,1152]{1,0:T(8,128)(2,1)} %front.1.p_low), channel_id=1, source_target_pairs={{0,8},{8,0},{1,9},{9,1},{2,10},{10,2},{3,11},{11,3},{4,12},{12,4},... | collective-permute-start | bytes 442376 | tf_op jit(solution)/shard_map/ppermute | solution.py:472
  6.3 8.3 %copy-start.1 = (f32[1152,128]{1,0:T(8,128)S(1)}, f32[1152,128]{1,0:T(8,128)}, u32[]{:S(2)}) copy-start(f32[1152,128]{1,0:T(8,128)} %constant.26.clone.cos.r_cos.p_cos) | copy-start | bytes 1769476
  6.3 8.3 %copy-start.4 = (bf16[1,1,128,5120]{3,2,1,0:T(8,128)(2,1)S(1)}, bf16[1,1,128,5120]{3,2,1,0:T(8,128)(2,1)}, u32[]{:S(2)}) copy-start(bf16[1,1,128,5120]{3,2,1,0:T(8,128)(2,1)} %r_base.3) | copy-start | bytes 3932164
  6.3 8.3 %copy-start.7 = (bf16[1,64,5120]{2,1,0:T(8,128)(2,1)S(1)}, bf16[1,64,5120]{2,1,0:T(8,128)(2,1)}, u32[]{:S(2)}) copy-start(bf16[1,64,5120]{2,1,0:T(8,128)(2,1)} %p_base.1) | copy-start | bytes 1966084
  6.4 8.3 %copy-start.8 = (bf16[1,1,128,4096]{3,2,1,0:T(8,128)(2,1)S(1)}, bf16[1,1,128,4096]{3,2,1,0:T(8,128)(2,1)}, u32[]{:S(2)}) copy-start(bf16[1,1,128,4096]{3,2,1,0:T(8,128)(2,1)} %r_gbase.1) | copy-start | bytes 3145732
  6.4 8.3 %copy-start.9 = (bf16[1,64,4096]{2,1,0:T(8,128)(2,1)S(1)}, bf16[1,64,4096]{2,1,0:T(8,128)(2,1)}, u32[]{:S(2)}) copy-start(bf16[1,64,4096]{2,1,0:T(8,128)(2,1)} %p_gbase.1) | copy-start | bytes 1572868
  6.4 8.3 %copy-start.11 = (bf16[16,4096]{1,0:T(8,128)(2,1)S(1)}, bf16[16,4096]{1,0:T(8,128)(2,1)}, u32[]{:S(2)}) copy-start(bf16[16,4096]{1,0:T(8,128)(2,1)} %q_up.5) | copy-start | bytes 393220
  6.4 8.3 %copy-start.12 = (bf16[4096,16]{0,1:T(8,128)(2,1)S(1)}, bf16[4096,16]{0,1:T(8,128)(2,1)}, u32[]{:S(2)}) copy-start(bf16[4096,16]{0,1:T(8,128)(2,1)} %param.26) | copy-start | bytes 393220
  10.8 9.1 %collective-permute-start.3 = (bf16[128,640]{1,0:T(8,128)(2,1)S(1)}, bf16[128,640]{1,0:T(8,128)(2,1)S(1)}, u32[]{:S(2)}, u32[]{:S(2)}) collective-permute-start(bf16[128,640]{1,0:T(8,128)(2,1)S(1)} %pad_maximum_fusion), channel_id=1, source_target_pairs={{0,6},{2,0},{4,2},{6,4},{1,7},{3,1},{5,3},{7,5},{8,14},{10,8},{12,... | collective-permute-start | bytes 491528 | tf_op jit(solution)/shard_map/ppermute | solution.py:403
  13.6 6.3 %collective-permute-start.2 = (bf16[128,640]{1,0:T(8,128)(2,1)S(1)}, bf16[128,640]{1,0:T(8,128)(2,1)S(1)}, u32[]{:S(2)}, u32[]{:S(2)}) collective-permute-start(bf16[128,640]{1,0:T(8,128)(2,1)S(1)} %pad_maximum_fusion), channel_id=1, source_target_pairs={{0,4},{2,6},{4,0},{6,2},{1,5},{3,7},{5,1},{7,3},{8,12},{10,14},{12... | collective-permute-start | bytes 491528 | tf_op jit(solution)/shard_map/ppermute | solution.py:403
  13.9 10.7 %collective-permute-start.1 = (bf16[128,640]{1,0:T(8,128)(2,1)S(1)}, bf16[128,640]{1,0:T(8,128)(2,1)S(1)}, u32[]{:S(2)}, u32[]{:S(2)}) collective-permute-start(bf16[128,640]{1,0:T(8,128)(2,1)S(1)} %pad_maximum_fusion), channel_id=1, source_target_pairs={{0,2},{2,4},{4,6},{6,0},{1,3},{3,5},{5,7},{7,1},{8,10},{10,12},{12... | collective-permute-start | bytes 491528 | tf_op jit(solution)/shard_map/ppermute | solution.py:403
  19.8 7.3 %copy-start.17 = (bf16[128,1152]{1,0:T(8,128)(2,1)S(1)}, bf16[128,1152]{1,0:T(8,128)(2,1)}, u32[]{:S(2)}) copy-start(bf16[128,1152]{1,0:T(8,128)(2,1)} %get-tuple-element.67.r_key.r_value.r_low) | copy-start | bytes 884740
  19.8 7.3 %copy-start.18 = (bf16[48,192]{1,0:T(8,128)(2,1)S(1)}, bf16[48,192]{1,0:T(8,128)(2,1)}, u32[]{:S(2)}) copy-start(bf16[48,192]{1,0:T(8,128)(2,1)} %get-tuple-element.68.low_t) | copy-start | bytes 55300
  24.8 2.3 %collective-permute-start.7 = (bf16[512,640]{1,0:T(8,128)(2,1)S(1)}, bf16[512,640]{1,0:T(8,128)(2,1)S(1)}, u32[]{:S(2)}, u32[]{:S(2)}) collective-permute-start(bf16[512,640]{1,0:T(8,128)(2,1)S(1)} %constant_dynamic-update-slice_fusion.key_a.value_a.low_a), channel_id=1, source_target_pairs={{0,1},{1,0},{2,3},{3,2},{4,5},{5,4},{6,7},{7,6},{8,9},{9,8},{10,11... | collective-permute-start | bytes 1966088 | tf_op jit(solution)/shard_map/ppermute | solution.py:565
  25.4 18.5 %collective-permute-start.6 = (bf16[128,512]{1,0:T(8,128)(2,1)S(1)}, bf16[128,512]{1,0:T(8,128)(2,1)S(1)}, u32[]{:S(2)}, u32[]{:S(2)}) collective-permute-start(bf16[128,512]{1,0:T(8,128)(2,1)S(1)} %pad_maximum_fusion.1), channel_id=1, source_target_pairs={{0,6},{2,0},{4,2},{6,4},{1,7},{3,1},{5,3},{7,5},{8,14},{10,8},{12,... | collective-permute-start | bytes 393224 | tf_op jit(solution)/shard_map/ppermute | solution.py:403
  25.7 18.2 %collective-permute-start.5 = (bf16[128,512]{1,0:T(8,128)(2,1)S(1)}, bf16[128,512]{1,0:T(8,128)(2,1)S(1)}, u32[]{:S(2)}, u32[]{:S(2)}) collective-permute-start(bf16[128,512]{1,0:T(8,128)(2,1)S(1)} %pad_maximum_fusion.1), channel_id=1, source_target_pairs={{0,4},{2,6},{4,0},{6,2},{1,5},{3,7},{5,1},{7,3},{8,12},{10,14},{12... | collective-permute-start | bytes 393224 | tf_op jit(solution)/shard_map/ppermute | solution.py:403
  26.0 17.9 %collective-permute-start.4 = (bf16[128,512]{1,0:T(8,128)(2,1)S(1)}, bf16[128,512]{1,0:T(8,128)(2,1)S(1)}, u32[]{:S(2)}, u32[]{:S(2)}) collective-permute-start(bf16[128,512]{1,0:T(8,128)(2,1)S(1)} %pad_maximum_fusion.1), channel_id=1, source_target_pairs={{0,2},{2,4},{4,6},{6,0},{1,3},{3,5},{5,7},{7,1},{8,10},{10,12},{12... | collective-permute-start | bytes 393224 | tf_op jit(solution)/shard_map/ppermute | solution.py:403
  44.0 2.0 %collective-permute-start.8 = (bf16[512,512]{1,0:T(8,128)(2,1)S(1)}, bf16[512,512]{1,0:T(8,128)(2,1)S(1)}, u32[]{:S(2)}, u32[]{:S(2)}) collective-permute-start(bf16[512,512]{1,0:T(8,128)(2,1)S(1)} %constant_dynamic-update-slice_fusion.4.key_a.value_a), channel_id=1, source_target_pairs={{0,1},{1,0},{2,3},{3,2},{4,5},{5,4},{6,7},{7,6},{8,9},{9,8},{10,11... | collective-permute-start | bytes 1572872 | tf_op jit(solution)/shard_map/ppermute | solution.py:664
  46.1 25.1 %copy-start.2 = (bf16[1,1,128,5120]{3,2,1,0:T(8,128)(2,1)S(1)}, bf16[1,1,128,5120]{3,2,1,0:T(8,128)(2,1)}, u32[]{:S(2)}) copy-start(bf16[1,1,128,5120]{3,2,1,0:T(8,128)(2,1)} %r_hidden.3) | copy-start | bytes 3932164
  46.1 25.1 %copy-start.3 = (bf16[1,1,128,5120]{3,2,1,0:T(8,128)(2,1)S(1)}, bf16[1,1,128,5120]{3,2,1,0:T(8,128)(2,1)}, u32[]{:S(2)}) copy-start(bf16[1,1,128,5120]{3,2,1,0:T(8,128)(2,1)} %r_out.3) | copy-start | bytes 3932164
  46.1 25.1 %copy-start.5 = (bf16[1,64,5120]{2,1,0:T(8,128)(2,1)S(1)}, bf16[1,64,5120]{2,1,0:T(8,128)(2,1)}, u32[]{:S(2)}) copy-start(bf16[1,64,5120]{2,1,0:T(8,128)(2,1)} %p_hidden.1) | copy-start | bytes 1966084
  46.1 25.1 %copy-start.6 = (bf16[1,64,5120]{2,1,0:T(8,128)(2,1)S(1)}, bf16[1,64,5120]{2,1,0:T(8,128)(2,1)}, u32[]{:S(2)}) copy-start(bf16[1,64,5120]{2,1,0:T(8,128)(2,1)} %p_out.3) | copy-start | bytes 1966084
  72.1 2.0 %collective-permute-start.9 = (bf16[128,16,128]{2,1,0:T(8,128)(2,1)S(1)}, bf16[128,16,128]{2,1,0:T(8,128)(2,1)S(1)}, u32[]{:S(2)}, u32[]{:S(2)}) collective-permute-start(bf16[128,16,128]{2,1,0:T(8,128)(2,1)S(1)} %get-tuple-element.91), channel_id=1, source_target_pairs={{0,1},{1,0},{2,3},{3,2},{4,5},{5,4},{6,7},{7,6},{8,9},{9,8},{10,11... | collective-permute-start | bytes 1572872 | tf_op jit(solution)/shard_map/ppermute | solution.py:702
  110.5 4.8 %collective-permute-start.10 = (bf16[128,16,128]{2,1,0:T(8,128)(2,1)S(1)}, bf16[128,16,128]{2,1,0:T(8,128)(2,1)S(1)}, u32[]{:S(2)}, u32[]{:S(2)}) collective-permute-start(bf16[128,16,128]{2,1,0:T(8,128)(2,1)S(1)} %bitcast.12), channel_id=1, source_target_pairs={{0,1},{1,0},{2,3},{3,2},{4,5},{5,4},{6,7},{7,6},{8,9},{9,8},{10,11... | collective-permute-start | bytes 1572872 | tf_op jit(solution)/shard_map/ppermute | solution.py:711
  (10 other events, 42.0 us)

commit v3 on v2

--- a/solution.py
+++ b/solution.py
@@ -106,8 +106,9 @@
 
 def query_kernel(
     spot, lengths, lows, splits, p_base, p_gbase, r_base, r_gbase, q_up, out_down,
-    p_cos, p_sin, r_cos, r_sin, query, push,
+    p_cos, p_sin, r_cos, r_sin, query_a, push_a, query_b, push_b, mark,
 ):
+    mark[...] = splits[: mark.shape[0], :]
     pr = p_base.shape[1]
     rl = r_base.shape[2]
     wide = q_up.shape[1]
@@ -116,19 +117,28 @@
     o_lift = jnp.concatenate(
         [out_down[...], out_down[...], jnp.zeros((HEAD_DIM - 2 * RANK, wide), BF16)], axis=0
     )
-    for base, gbase, cos, sin, at, n in (
-        (p_base[0], p_gbase[0], p_cos, p_sin, 0, pr),
-        (r_base[0, 0], r_gbase[0, 0], r_cos, r_sin, pr, rl),
-    ):
-        q = base.astype(F32) + 2.0 * mm(lows[at : at + n, :], q_lift)
-        for h in range(0, wide, HEAD_DIM):
-            query[at : at + n, h : h + HEAD_DIM] = rope(
-                q[:, h : h + HEAD_DIM], cos[...], sin[...]
-            ).astype(BF16)
-        up = gbase.astype(F32) + 2.0 * mm(splits[at : at + n, :], o_lift)
-        if at:
-            up = jnp.where(live, up, 0.0)
-        push[at : at + n, :] = up.astype(BF16)
+    def fill(query, push):
+        for base, gbase, cos, sin, at, n in (
+            (p_base[0], p_gbase[0], p_cos, p_sin, 0, pr),
+            (r_base[0, 0], r_gbase[0, 0], r_cos, r_sin, pr, rl),
+        ):
+            q = base.astype(F32) + 2.0 * mm(lows[at : at + n, :], q_lift)
+            for h in range(0, wide, HEAD_DIM):
+                query[at : at + n, h : h + HEAD_DIM] = rope(
+                    q[:, h : h + HEAD_DIM], cos[...], sin[...]
+                ).astype(BF16)
+            up = gbase.astype(F32) + 2.0 * mm(splits[at : at + n, :], o_lift)
+            if at:
+                up = jnp.where(live, up, 0.0)
+            push[at : at + n, :] = up.astype(BF16)
+
+    @pl.when(pl.program_id(0) < pl.num_programs(0) // 2)
+    def _():
+        fill(query_a, push_a)
+
+    @pl.when(pl.program_id(0) >= pl.num_programs(0) // 2)
+    def _():
+        fill(query_b, push_b)
 
 
 def attend_kernel(
@@ -304,9 +314,11 @@
             blocks[at][0]()
         if at:
             blocks[at - 1][3]()
+        if at < len(blocks):
+            blocks[at][1]()
+        if at:
             blocks[at - 1][4]()
         if at < len(blocks):
-            blocks[at][1]()
             blocks[at][2]()
         if at and at % each == 0:
             new = finish(at // each - 1)
@@ -525,7 +537,7 @@
     def cols4(shift=0):
         return pl.BlockSpec((1, 1, rl, qb), lambda i, s: (0, 0, 0, i + shift))
 
-    query, push = pl.pallas_call(
+    query_a, push_a, query_b, push_b, mark = pl.pallas_call(
         query_kernel,
         grid_spec=pltpu.PrefetchScalarGridSpec(
             num_scalar_prefetch=1,
@@ -545,11 +557,20 @@
                 r_table,
                 r_table,
             ],
-            out_specs=[head_cols(rows, qb), head_cols(rows, qb)],
+            out_specs=[
+                pl.BlockSpec((rows, qb), lambda i, s: (0, jnp.minimum(i, each - 1))),
+                pl.BlockSpec((rows, qb), lambda i, s: (0, jnp.minimum(i, each - 1))),
+                pl.BlockSpec((rows, qb), lambda i, s: (0, jnp.maximum(i - each, 0))),
+                pl.BlockSpec((rows, qb), lambda i, s: (0, jnp.maximum(i - each, 0))),
+                whole((RANK, HEAD_DIM)),
+            ],
         ),
         out_shape=[
-            jax.ShapeDtypeStruct((rows, q_width), BF16),
-            jax.ShapeDtypeStruct((rows, q_width), BF16),
+            jax.ShapeDtypeStruct((rows, q_width // 2), BF16),
+            jax.ShapeDtypeStruct((rows, q_width // 2), BF16),
+            jax.ShapeDtypeStruct((rows, q_width // 2), BF16),
+            jax.ShapeDtypeStruct((rows, q_width // 2), BF16),
+            jax.ShapeDtypeStruct((RANK, HEAD_DIM), BF16),
         ],
         name="query",
         **params(4 * rows * q_width * 128, 8_000_000, 48),
@@ -558,8 +579,8 @@
         reply_grad_base, query_up_weight, out_down, cos_rows, sin_rows, cos_rows, sin_rows,
     )
 
-    first_parts, second_pair, query, push = lax.optimization_barrier(
-        (first_parts, second_pair, query, push)
+    first_parts, second_pair, query_a, push_a = lax.optimization_barrier(
+        (first_parts, second_pair, query_a, push_a)
     )
     first_own = jnp.concatenate(first_parts, axis=0)
     first_other = lax.ppermute(first_own, "core", PAIR)
@@ -567,13 +588,13 @@
     count = prompt // 2
     low_block = pl.BlockSpec((count, HEAD_DIM), lambda i, s: (0, kv_width // HEAD_DIM))
 
-    def attend(own, other, at, before):
+    def attend(query, push, own, other, at, before):
         first = before is None
         kb = each * HEAD_DIM
         in_specs = [
             pl.BlockSpec(memory_space=pltpu.SMEM),
-            head_cols(rows, each * qb, at),
-            head_cols(rows, each * qb, at),
+            whole((rows, each * qb)),
+            whole((rows, each * qb)),
             head_cols(count, kb),
             head_cols(count, kb),
             head_cols(count, kb, 1),
@@ -655,7 +676,7 @@
         )(*operands)
 
     p_half, r_half, tiles_a, fold_q, lifted, fold_kv, _, _ = attend(
-        first_own, first_other, 0, None
+        query_a, push_a, first_own, first_other, 0, None
     )
     second_parts, fold_q, lifted, fold_kv = lax.optimization_barrier(
         (second_parts, fold_q, lifted, fold_kv)
@@ -663,7 +684,7 @@
     second_own = jnp.concatenate(second_parts, axis=0)
     second_other = lax.ppermute(second_own, "core", PAIR)
     p_context, r_context, tiles_b, fold_q, lifted, _, fold_send, fold_reply = attend(
-        second_own, second_other, 1, (fold_q, lifted, fold_kv, p_half, r_half)
+        query_b, push_b, second_own, second_other, 1, (fold_q, lifted, fold_kv, p_half, r_half)
     )
 
     fold_recv = lax.all_to_all(fold_send, RESP, 0, 0, tiled=True)

time: 117 us -> 114 us (0.974)
  local copies, waits for them, and re-layouts: 4.73 us -> 1.91 us
    unnamed x52 -> x44, local copies, waits for them, and re-layouts: 4.59 us -> 1.77 us
  transfers between devices with their start and end apart: 11 -> 11, of which waited for: 5 -> 5; matrix products, arithmetic and copies ran while one was open for 0% -> 0% of each run, Pallas kernels for 19% -> 20%
where the time goes in v3:
time: 114 us
  blocking collectives  47.5 us (42%)
  Pallas kernels  41 us (36%)
  starting transfers between devices  12.6 us (11%)
  waiting for transfers between devices  8.73 us (8%)
  local copies, waits for them, and re-layouts  1.91 us (2%)
  between operations  1.62 us (1%)
    pallas_call x2, Pallas kernels, attend(): pl.pallas_call(functools.partial(attend_kernel, first), grid_spec=pltpu.P...  27.5 us
    all_to_all x1, blocking collectives, per_device(): lax.all_to_all(paired.reshape(chips, -1, HEAD_DIM), CHIPS, 0, 0, tiled=True)  20.5 us
    all_to_all x1, blocking collectives, per_device(): lax.all_to_all(jnp.broadcast_to(total[None], spread.shape), CHIPS, 0, 0,...  15.5 us
    all_to_all x1, blocking collectives, per_device(): fold_recv = lax.all_to_all(fold_send, RESP, 0, 0, tiled=True)  11.4 us
    ppermute x6, starting transfers between devices, shifted(): return lax.ppermute(x, axis, [(i, (i + by) % n) for i in range(n)])  5.32 us
    pallas_call x1, Pallas kernels, per_device(): pl.pallas_call(query_kernel, grid_spec=pltpu.PrefetchScalarGridSpec(num_s...  4.42 us
    pallas_call x1, Pallas kernels, per_device(): pl.pallas_call(reply_kernel, grid=(1,), in_specs=[pl.BlockSpec(memory_spa...  4.29 us
    ppermute x6, waiting for transfers between devices, shifted(): return lax.ppermute(x, axis, [(i, (i + by) % n) for i in range(n)])  3.88 us
  transfers between devices with their start and end apart: 11, of which 5 were waited for; matrix products, arithmetic and copies ran while one was open for 0% of the time, Pallas kernels for 20%

profile of v3, /device:TPU:1, one launch (start us, length us, event | category | flops | bytes accessed | tf_op | source)
XLA Modules:
  0.0 113.6 jit_solution(7945665392059262037)
XLA Ops:
  0.6 2.6 %front.1.p_low = bf16[64,1152]{1,0:T(8,128)(2,1)} custom-call(s32[1]{0:T(128)} %bitcast.spot, bf16[1,64,5120]{2,1,0:T(8,128)(2,1)} %p_hidden.1, bf16[1,64,5120]{2,1,0:T(8,128)(2,1)} %p_base.1, bf16[48,5120]{1,0:T(8,128)(2,1)} %bitcast.18, bf16[2,16,512]{2,1,0:T(8,128)(2,1)} %kv_up.7, f32[1152,128]{1,0:T(8,128)} %constant.26.clone.cos.r_cos.p_cos, ...), custom_call_target="tpu_custom_call" | custom-call | flops 31457280 | bytes 2000000 | tf_op jit(solution)/shard_map/front/pallas_call | solution.py:464
  3.2 2.5 %collective-permute-start = (bf16[64,1152]{1,0:T(8,128)(2,1)}, bf16[64,1152]{1,0:T(8,128)(2,1)S(1)}, u32[]{:S(2)}, u32[]{:S(2)}) collective-permute-start(bf16[64,1152]{1,0:T(8,128)(2,1)} %front.1.p_low), channel_id=1, source_target_pairs={{0,8},{8,0},{1,9},{9,1},{2,10},{10,2},{3,11},{11,3},{4,12},{12,4},... | collective-permute-start | bytes 442376 | tf_op jit(solution)/shard_map/ppermute | solution.py:484
  6.4 4.3 %reply.1 = (bf16[128,1152]{1,0:T(8,128)(2,1)}, bf16[192,128]{1,0:T(8,128)(2,1)}, bf16[192,128]{1,0:T(8,128)(2,1)}, bf16[48,192]{1,0:T(8,128)(2,1)}, bf16[32,192]{1,0:T(8,128)(2,1)}) custom-call(s32[1,1]{1,0:T(1,128)S(6)} %copy.35.lengths, bf16[64,1152]{1,0:T(8,128)(2,1)} %front.1.p_low, bf16[1,64,5120]{2,1,0:T(8,128)(2,1)} %p_out.3, ...), custom_call_target="tpu_custom_call" | custom-call | flops 188743680 | bytes 6000000 | tf_op jit(solution)/shard_map/reply/pallas_call | solution.py:486
  10.7 2.8 %collective-permute-start.3 = (bf16[128,640]{1,0:T(8,128)(2,1)S(1)}, bf16[128,640]{1,0:T(8,128)(2,1)S(1)}, u32[]{:S(2)}, u32[]{:S(2)}) collective-permute-start(bf16[128,640]{1,0:T(8,128)(2,1)S(1)} %pad_maximum_fusion), channel_id=1, source_target_pairs={{0,6},{2,0},{4,2},{6,4},{1,7},{3,1},{5,3},{7,5},{8,14},{10,8},{12,... | collective-permute-start | bytes 491528 | tf_op jit(solution)/shard_map/ppermute | solution.py:415
  13.9 0.7 collective-permute-start.1
  14.7 0.8 copy-done.11
  15.5 0.8 copy-done.12
  16.3 4.4 %query.1 = (bf16[192,2048]{1,0:T(8,128)(2,1)S(1)}, bf16[192,2048]{1,0:T(8,128)(2,1)S(1)}, bf16[192,2048]{1,0:T(8,128)(2,1)S(1)}, bf16[192,2048]{1,0:T(8,128)(2,1)S(1)}, bf16[16,128]{1,0:T(8,128)(2,1)}) custom-call(s32[1]{0:T(128)} %bitcast.spot, s32[1,1]{1,0:T(1,128)S(6)} %copy.35.lengths, bf16[192,128]{1,0:T(8,128)(2,1)S(1)} %copy-done.11, ...), custom_call_target="tpu_custom_call" | custom-call | flops 402653184 | bytes 8000000 | tf_op jit(solution)/shard_map/query/pallas_call | solution.py:540
  20.8 3.9 %collective-permute-done.1 = bf16[128,640]{1,0:T(8,128)(2,1)S(1)} collective-permute-done((bf16[128,640]{1,0:T(8,128)(2,1)S(1)}, bf16[128,640]{1,0:T(8,128)(2,1)S(1)}, u32[]{:S(2)}, u32[]{:S(2)}) %collective-permute-start.1) | collective-permute-done | bytes 163872 | tf_op jit(solution)/shard_map/ppermute | solution.py:415
  24.7 0.6 collective-permute-start.7
  25.7 0.5 collective-permute-start.5
  26.2 0.7 collective-permute-start.4
  27.1 14.0 %attend.2 = (bf16[1,64,4096]{2,1,0:T(8,128)(2,1)}, bf16[1,1,128,4096]{3,2,1,0:T(8,128)(2,1)}, bf16[36,16,128]{2,1,0:T(8,128)(2,1)S(1)}, f32[16,192]{1,0:T(8,128)...) custom-call(s32[1]{0:T(128)} %bitcast.spot, ...), custom_call_target="tpu_custom_call" | custom-call | flops 4831838208 | bytes 8000000 | tf_op jit(solution)/shard_map/attend/pallas_call | solution.py:636
  41.2 0.5 collective-permute-start.8
  41.7 1.5 %collective-permute-done.8.key_b.value_b = bf16[512,512]{1,0:T(8,128)(2,1)S(1)} collective-permute-done((bf16[512,512]{1,0:T(8,128)(2,1)S(1)}, bf16[512,512]{1,0:T(8,128)(2,1)S(1)}, u32[]{:S(2)}, u32[]{:S(2)}) %collective-permute-start.8) | collective-permute-done | bytes 524320 | tf_op jit(solution)/shard_map/ppermute | solution.py:685
  43.2 13.6 %attend.3 = (bf16[1,64,4096]{2,1,0:T(8,128)(2,1)}, bf16[1,1,128,4096]{3,2,1,0:T(8,128)(2,1)}, bf16[36,16,128]{2,1,0:T(8,128)(2,1)S(1)}, f32[16,192]{1,0:T(8,128)...) custom-call(s32[1]{0:T(128)} %bitcast.spot, ...), custom_call_target="tpu_custom_call", output_to_operand_aliasing={{0}: (27, {}), {1}: (28, {})} | custom-call | flops 4831838208 | bytes 8000000 | tf_op jit(solution)/shard_map/attend/pallas_call | solution.py:636
  56.8 11.4 %all_to_all.15.fold_recv = bf16[16,16,128]{2,1,0:T(8,128)(2,1)S(1)} all-to-all(bf16[16,16,128]{2,1,0:T(8,128)(2,1)S(1)} %get-tuple-element.91), channel_id=1, replica_groups=mesh['x'=4,'z_hi'=2,'z_lo'=2,'y'=4,'core'=2] {'z_lo','y','core'}, dimensions={0} | all-to-all | bytes 131072 | tf_op jit(solution)/shard_map/all_to_all | solution.py:690
  68.2 0.9 grads.1
  69.6 1.5 %collective-permute-done.9 = bf16[128,16,128]{2,1,0:T(8,128)(2,1)S(1)} collective-permute-done((bf16[128,16,128]{2,1,0:T(8,128)(2,1)S(1)}, bf16[128,16,128]{2,1,0:T(8,128)(2,1)S(1)}, u32[]{:S(2)}, u32[]{:S(2)}) %collective-permute-start.9) | collective-permute-done | bytes 524320 | tf_op jit(solution)/shard_map/ppermute | solution.py:723
  71.2 20.5 %all_to_all.16 = bf16[64,32,128]{2,1,0:T(8,128)(2,1)S(1)} all-to-all(bf16[64,32,128]{2,1,0:T(8,128)(2,1)S(1)} %bitcast.17), channel_id=1, replica_groups=mesh['x'=4,'z_hi'=2,'z_lo'=2,'y'=4,'core'=2] {'x','z_hi','z_lo','y'}, dimensions={0} | all-to-all | bytes 1048576 | tf_op jit(solution)/shard_map/all_to_all | solution.py:725
  91.9 15.5 %all_to_all.17 = bf16[64,32,128]{2,1,0:T(8,128)(2,1)S(1)} all-to-all(bf16[64,32,128]{2,1,0:T(8,128)(2,1)S(1)} %broadcast_in_dim.10), channel_id=1, replica_groups=mesh['x'=4,'z_hi'=2,'z_lo'=2,'y'=4,'core'=2] {'x','z_hi','z_lo','y'}, dimensions={0} | all-to-all | bytes 1048576 | tf_op jit(solution)/shard_map/all_to_all | solution.py:729
  107.5 3.2 %collective-permute-start.10 = (bf16[128,16,128]{2,1,0:T(8,128)(2,1)S(1)}, bf16[128,16,128]{2,1,0:T(8,128)(2,1)S(1)}, u32[]{:S(2)}, u32[]{:S(2)}) collective-permute-start(bf16[128,16,128]{2,1,0:T(8,128)(2,1)S(1)} %bitcast.12), channel_id=1, source_target_pairs={{0,1},{1,0},{2,3},{3,2},{4,5},{5,4},{6,7},{7,6},{8,9},{9,8},{10,11... | collective-permute-start | bytes 1572872 | tf_op jit(solution)/shard_map/ppermute | solution.py:732
  110.7 1.5 %collective-permute-done.10.theirs = bf16[128,16,128]{2,1,0:T(8,128)(2,1)S(1)} collective-permute-done((bf16[128,16,128]{2,1,0:T(8,128)(2,1)S(1)}, bf16[128,16,128]{2,1,0:T(8,128)(2,1)S(1)}, u32[]{:S(2)}, u32[]{:S(2)}) %collective-permute-start.10) | collective-permute-done | bytes 524320 | tf_op jit(solution)/shard_map/ppermute | solution.py:732
  112.3 1.3 %unpack.1 = (f32[48,5120]{1,0:T(8,128)}, f32[16,4096]{1,0:T(8,128)}, f32[32,512]{1,0:T(8,128)}, f32[16,4096]{1,0:T(8,128)}, f32[16,5120]{1,0:T(8,128)}) custom-call(s32[1]{0:T(128)} %bitcast.spot, bf16[128,16,128]{2,1,0:T(8,128)(2,1)S(1)} %bitcast.13, bf16[128,16,128]{2,1,0:T(8,128)(2,1)S(1)} %collective-permute-done.10.theirs), custom_call_target="tpu_custom_call" | custom-call | bytes 3000000 | tf_op jit(solution)/shard_map/unpack/pallas_call | solution.py:735
  (63 shorter events, 2.0 us)
Async XLA Ops:
  3.2 7.5 %collective-permute-start = (bf16[64,1152]{1,0:T(8,128)(2,1)}, bf16[64,1152]{1,0:T(8,128)(2,1)S(1)}, u32[]{:S(2)}, u32[]{:S(2)}) collective-permute-start(bf16[64,1152]{1,0:T(8,128)(2,1)} %front.1.p_low), channel_id=1, source_target_pairs={{0,8},{8,0},{1,9},{9,1},{2,10},{10,2},{3,11},{11,3},{4,12},{12,4},... | collective-permute-start | bytes 442376 | tf_op jit(solution)/shard_map/ppermute | solution.py:484
  6.3 8.3 %copy-start.1 = (f32[1152,128]{1,0:T(8,128)S(1)}, f32[1152,128]{1,0:T(8,128)}, u32[]{:S(2)}) copy-start(f32[1152,128]{1,0:T(8,128)} %constant.26.clone.cos.r_cos.p_cos) | copy-start | bytes 1769476
  6.3 8.3 %copy-start.6 = (bf16[1,64,5120]{2,1,0:T(8,128)(2,1)S(1)}, bf16[1,64,5120]{2,1,0:T(8,128)(2,1)}, u32[]{:S(2)}) copy-start(bf16[1,64,5120]{2,1,0:T(8,128)(2,1)} %p_base.1) | copy-start | bytes 1966084
  6.3 8.3 %copy-start.7 = (bf16[1,64,4096]{2,1,0:T(8,128)(2,1)S(1)}, bf16[1,64,4096]{2,1,0:T(8,128)(2,1)}, u32[]{:S(2)}) copy-start(bf16[1,64,4096]{2,1,0:T(8,128)(2,1)} %p_gbase.1) | copy-start | bytes 1572868
  6.4 8.3 %copy-start.9 = (bf16[16,4096]{1,0:T(8,128)(2,1)S(1)}, bf16[16,4096]{1,0:T(8,128)(2,1)}, u32[]{:S(2)}) copy-start(bf16[16,4096]{1,0:T(8,128)(2,1)} %q_up.5) | copy-start | bytes 393220
  6.4 8.3 %copy-start.10 = (bf16[4096,16]{0,1:T(8,128)(2,1)S(1)}, bf16[4096,16]{0,1:T(8,128)(2,1)}, u32[]{:S(2)}) copy-start(bf16[4096,16]{0,1:T(8,128)(2,1)} %param.26) | copy-start | bytes 393220
  10.7 10.0 %collective-permute-start.3 = (bf16[128,640]{1,0:T(8,128)(2,1)S(1)}, bf16[128,640]{1,0:T(8,128)(2,1)S(1)}, u32[]{:S(2)}, u32[]{:S(2)}) collective-permute-start(bf16[128,640]{1,0:T(8,128)(2,1)S(1)} %pad_maximum_fusion), channel_id=1, source_target_pairs={{0,6},{2,0},{4,2},{6,4},{1,7},{3,1},{5,3},{7,5},{8,14},{10,8},{12,... | collective-permute-start | bytes 491528 | tf_op jit(solution)/shard_map/ppermute | solution.py:415
  13.5 7.2 %collective-permute-start.2 = (bf16[128,640]{1,0:T(8,128)(2,1)S(1)}, bf16[128,640]{1,0:T(8,128)(2,1)S(1)}, u32[]{:S(2)}, u32[]{:S(2)}) collective-permute-start(bf16[128,640]{1,0:T(8,128)(2,1)S(1)} %pad_maximum_fusion), channel_id=1, source_target_pairs={{0,4},{2,6},{4,0},{6,2},{1,5},{3,7},{5,1},{7,3},{8,12},{10,14},{12... | collective-permute-start | bytes 491528 | tf_op jit(solution)/shard_map/ppermute | solution.py:415
  13.9 10.7 %collective-permute-start.1 = (bf16[128,640]{1,0:T(8,128)(2,1)S(1)}, bf16[128,640]{1,0:T(8,128)(2,1)S(1)}, u32[]{:S(2)}, u32[]{:S(2)}) collective-permute-start(bf16[128,640]{1,0:T(8,128)(2,1)S(1)} %pad_maximum_fusion), channel_id=1, source_target_pairs={{0,2},{2,4},{4,6},{6,0},{1,3},{3,5},{5,7},{7,1},{8,10},{10,12},{12... | collective-permute-start | bytes 491528 | tf_op jit(solution)/shard_map/ppermute | solution.py:415
  20.7 6.4 %copy-start.8 = (bf16[2,16,512]{2,1,0:T(8,128)(2,1)S(1)}, bf16[2,16,512]{2,1,0:T(8,128)(2,1)}, u32[]{:S(2)}) copy-start(bf16[2,16,512]{2,1,0:T(8,128)(2,1)} %kv_up.7) | copy-start | bytes 98308
  20.7 6.4 %copy-start.13 = (bf16[128,1152]{1,0:T(8,128)(2,1)S(1)}, bf16[128,1152]{1,0:T(8,128)(2,1)}, u32[]{:S(2)}) copy-start(bf16[128,1152]{1,0:T(8,128)(2,1)} %get-tuple-element.71.r_key.r_value.r_low) | copy-start | bytes 884740
  20.7 6.4 %copy-start.14 = (bf16[48,192]{1,0:T(8,128)(2,1)S(1)}, bf16[48,192]{1,0:T(8,128)(2,1)}, u32[]{:S(2)}) copy-start(bf16[48,192]{1,0:T(8,128)(2,1)} %get-tuple-element.72.low_t) | copy-start | bytes 55300
  20.7 6.4 %copy-start.15 = (bf16[32,192]{1,0:T(8,128)(2,1)S(1)}, bf16[32,192]{1,0:T(8,128)(2,1)}, u32[]{:S(2)}) copy-start(bf16[32,192]{1,0:T(8,128)(2,1)} %get-tuple-element.73.lowered_t) | copy-start | bytes 36868
  24.7 2.3 %collective-permute-start.7 = (bf16[512,640]{1,0:T(8,128)(2,1)S(1)}, bf16[512,640]{1,0:T(8,128)(2,1)S(1)}, u32[]{:S(2)}, u32[]{:S(2)}) collective-permute-start(bf16[512,640]{1,0:T(8,128)(2,1)S(1)} %constant_dynamic-update-slice_fusion.key_a.value_a.low_a), channel_id=1, source_target_pairs={{0,1},{1,0},{2,3},{3,2},{4,5},{5,4},{6,7},{7,6},{8,9},{9,8},{10,11... | collective-permute-start | bytes 1966088 | tf_op jit(solution)/shard_map/ppermute | solution.py:586
  25.4 15.7 %collective-permute-start.6 = (bf16[128,512]{1,0:T(8,128)(2,1)S(1)}, bf16[128,512]{1,0:T(8,128)(2,1)S(1)}, u32[]{:S(2)}, u32[]{:S(2)}) collective-permute-start(bf16[128,512]{1,0:T(8,128)(2,1)S(1)} %pad_maximum_fusion.1), channel_id=1, source_target_pairs={{0,6},{2,0},{4,2},{6,4},{1,7},{3,1},{5,3},{7,5},{8,14},{10,8},{12,... | collective-permute-start | bytes 393224 | tf_op jit(solution)/shard_map/ppermute | solution.py:415
  25.7 15.4 %collective-permute-start.5 = (bf16[128,512]{1,0:T(8,128)(2,1)S(1)}, bf16[128,512]{1,0:T(8,128)(2,1)S(1)}, u32[]{:S(2)}, u32[]{:S(2)}) collective-permute-start(bf16[128,512]{1,0:T(8,128)(2,1)S(1)} %pad_maximum_fusion.1), channel_id=1, source_target_pairs={{0,4},{2,6},{4,0},{6,2},{1,5},{3,7},{5,1},{7,3},{8,12},{10,14},{12... | collective-permute-start | bytes 393224 | tf_op jit(solution)/shard_map/ppermute | solution.py:415
  26.2 14.9 %collective-permute-start.4 = (bf16[128,512]{1,0:T(8,128)(2,1)S(1)}, bf16[128,512]{1,0:T(8,128)(2,1)S(1)}, u32[]{:S(2)}, u32[]{:S(2)}) collective-permute-start(bf16[128,512]{1,0:T(8,128)(2,1)S(1)} %pad_maximum_fusion.1), channel_id=1, source_target_pairs={{0,2},{2,4},{4,6},{6,0},{1,3},{3,5},{5,7},{7,1},{8,10},{10,12},{12... | collective-permute-start | bytes 393224 | tf_op jit(solution)/shard_map/ppermute | solution.py:415
  41.2 2.0 %collective-permute-start.8 = (bf16[512,512]{1,0:T(8,128)(2,1)S(1)}, bf16[512,512]{1,0:T(8,128)(2,1)S(1)}, u32[]{:S(2)}, u32[]{:S(2)}) collective-permute-start(bf16[512,512]{1,0:T(8,128)(2,1)S(1)} %constant_dynamic-update-slice_fusion.4.key_a.value_a), channel_id=1, source_target_pairs={{0,1},{1,0},{2,3},{3,2},{4,5},{5,4},{6,7},{7,6},{8,9},{9,8},{10,11... | collective-permute-start | bytes 1572872 | tf_op jit(solution)/shard_map/ppermute | solution.py:685
  43.2 25.0 %copy-start.2 = (bf16[1,1,128,5120]{3,2,1,0:T(8,128)(2,1)S(1)}, bf16[1,1,128,5120]{3,2,1,0:T(8,128)(2,1)}, u32[]{:S(2)}) copy-start(bf16[1,1,128,5120]{3,2,1,0:T(8,128)(2,1)} %r_hidden.3) | copy-start | bytes 3932164
  43.2 25.0 %copy-start.3 = (bf16[1,1,128,5120]{3,2,1,0:T(8,128)(2,1)S(1)}, bf16[1,1,128,5120]{3,2,1,0:T(8,128)(2,1)}, u32[]{:S(2)}) copy-start(bf16[1,1,128,5120]{3,2,1,0:T(8,128)(2,1)} %r_out.3) | copy-start | bytes 3932164
  43.2 25.0 %copy-start.4 = (bf16[1,64,5120]{2,1,0:T(8,128)(2,1)S(1)}, bf16[1,64,5120]{2,1,0:T(8,128)(2,1)}, u32[]{:S(2)}) copy-start(bf16[1,64,5120]{2,1,0:T(8,128)(2,1)} %p_hidden.1) | copy-start | bytes 1966084
  43.2 25.0 %copy-start.5 = (bf16[1,64,5120]{2,1,0:T(8,128)(2,1)S(1)}, bf16[1,64,5120]{2,1,0:T(8,128)(2,1)}, u32[]{:S(2)}) copy-start(bf16[1,64,5120]{2,1,0:T(8,128)(2,1)} %p_out.3) | copy-start | bytes 1966084
  69.1 2.0 %collective-permute-start.9 = (bf16[128,16,128]{2,1,0:T(8,128)(2,1)S(1)}, bf16[128,16,128]{2,1,0:T(8,128)(2,1)S(1)}, u32[]{:S(2)}, u32[]{:S(2)}) collective-permute-start(bf16[128,16,128]{2,1,0:T(8,128)(2,1)S(1)} %get-tuple-element.95), channel_id=1, source_target_pairs={{0,1},{1,0},{2,3},{3,2},{4,5},{5,4},{6,7},{7,6},{8,9},{9,8},{10,11... | collective-permute-start | bytes 1572872 | tf_op jit(solution)/shard_map/ppermute | solution.py:723
  107.5 4.8 %collective-permute-start.10 = (bf16[128,16,128]{2,1,0:T(8,128)(2,1)S(1)}, bf16[128,16,128]{2,1,0:T(8,128)(2,1)S(1)}, u32[]{:S(2)}, u32[]{:S(2)}) collective-permute-start(bf16[128,16,128]{2,1,0:T(8,128)(2,1)S(1)} %bitcast.12), channel_id=1, source_target_pairs={{0,1},{1,0},{2,3},{3,2},{4,5},{5,4},{6,7},{7,6},{8,9},{9,8},{10,11... | collective-permute-start | bytes 1572872 | tf_op jit(solution)/shard_map/ppermute | solution.py:732
  (6 other events, 22.7 us)

commit v4 on v3

--- a/solution.py
+++ b/solution.py
@@ -415,8 +415,9 @@
     return lax.ppermute(x, axis, [(i, (i + by) % n) for i in range(n)])
 
 
-def chips_of(pair):
-    return [pair] + [shifted(pair, "y", k) for k in (1, 2, 3)]
+def chips_of(pair, two):
+    one, three = shifted(pair, "y", 1), shifted(pair, "y", 3)
+    return [pair, one, two, lax.ppermute(two, "z_lo", PAIR), three]
 
 
 def per_device(
@@ -482,6 +483,7 @@
     )(spot, prompt_hidden, prompt_base, down, key_value_up_weight, cos_rows, sin_rows)
 
     far_kv = lax.ppermute(own_kv, "z_lo", PAIR)
+    two_kv = shifted(own_kv, "y", 2)
 
     reply_kv, lows, splits, low_t, lowered_t = pl.pallas_call(
         reply_kernel,
@@ -522,11 +524,11 @@
         key_value_up_weight, output_up, cos_rows, sin_rows,
     )
 
-    own_kv, far_kv, lows, splits = lax.optimization_barrier((own_kv, far_kv, lows, splits))
+    own_kv, far_kv, two_kv, lows, splits = lax.optimization_barrier(
+        (own_kv, far_kv, two_kv, lows, splits)
+    )
     cut = kv_width + HEAD_DIM
-    first_pair = jnp.concatenate([own_kv[:, :cut], far_kv[:, :cut]], axis=0)
-    second_pair = jnp.concatenate([own_kv[:, cut:], far_kv[:, cut:]], axis=0)
-    first_parts = chips_of(first_pair)
+    parts = chips_of(jnp.concatenate([own_kv, far_kv], axis=0), two_kv)
 
     def head_cols(n, width, shift=0):
         return pl.BlockSpec((n, width), lambda i, s: (0, i + shift))
@@ -579,12 +581,11 @@
         reply_grad_base, query_up_weight, out_down, cos_rows, sin_rows, cos_rows, sin_rows,
     )
 
-    first_parts, second_pair, query_a, push_a = lax.optimization_barrier(
-        (first_parts, second_pair, query_a, push_a)
-    )
-    first_own = jnp.concatenate(first_parts, axis=0)
+    parts, query_a, push_a = lax.optimization_barrier((parts, query_a, push_a))
+    first_own = jnp.concatenate([x[:, :cut] for x in parts], axis=0)
+    second_own = jnp.concatenate([x[:, cut:] for x in parts], axis=0)
     first_other = lax.ppermute(first_own, "core", PAIR)
-    second_parts = chips_of(second_pair)
+    second_other = lax.ppermute(second_own, "core", PAIR)
     count = prompt // 2
     low_block = pl.BlockSpec((count, HEAD_DIM), lambda i, s: (0, kv_width // HEAD_DIM))
 
@@ -678,11 +679,6 @@
     p_half, r_half, tiles_a, fold_q, lifted, fold_kv, _, _ = attend(
         query_a, push_a, first_own, first_other, 0, None
     )
-    second_parts, fold_q, lifted, fold_kv = lax.optimization_barrier(
-        (second_parts, fold_q, lifted, fold_kv)
-    )
-    second_own = jnp.concatenate(second_parts, axis=0)
-    second_other = lax.ppermute(second_own, "core", PAIR)
     p_context, r_context, tiles_b, fold_q, lifted, _, fold_send, fold_reply = attend(
         query_b, push_b, second_own, second_other, 1, (fold_q, lifted, fold_kv, p_half, r_half)
     )

time: 114 us -> 110 us (0.965)
  waiting for transfers between devices: 8.73 us -> 6.04 us
  blocking collectives: 47.5 us -> 45.1 us
    ppermute x6 -> x3, waiting for transfers between devices: 3.88 us -> 1.37 us  [shifted(): return lax.ppermute(x, axis, [(i, (i + by) % n) for i in range(n)])]
    all_to_all x1, blocking collectives: 11.4 us -> 9.01 us  [per_device(): fold_recv = lax.all_to_all(fold_send, RESP, 0, 0, tiled=True)]
    ppermute x1, starting transfers between devices: 0.62 us -> 2.52 us  [per_device(): first_other = lax.ppermute(first_own, 'core', PAIR)]
    ppermute x1, waiting for transfers between devices: 1.54 us -> 0.01 us  [per_device(): second_other = lax.ppermute(second_own, 'core', PAIR)]
    ppermute x1, waiting for transfers between devices: 0.24 us -> 1.58 us  [per_device(): first_other = lax.ppermute(first_own, 'core', PAIR)]
    ppermute x6 -> x3, starting transfers between devices: 5.32 us -> 5.28 us  [shifted(): return lax.ppermute(x, axis, [(i, (i + by) % n) for i in range(n)])]
  transfers between devices with their start and end apart: 11 -> 9, of which waited for: 5 -> 4; matrix products, arithmetic and copies ran while one was open for 0% -> 0% of each run, Pallas kernels for 20% -> 21%
where the time goes in v4:
time: 110 us; the launch traced here: 109 us
  blocking collectives  45.1 us (41%)
  Pallas kernels  41 us (37%)
  starting transfers between devices  13.2 us (12%)
  waiting for transfers between devices  6.04 us (5%)
  local copies, waits for them, and re-layouts  1.93 us (2%)
  between operations  1.6 us (1%)
    pallas_call x2, Pallas kernels, attend(): pl.pallas_call(functools.partial(attend_kernel, first), grid_spec=pltpu.P...  27.6 us
    all_to_all x1, blocking collectives, per_device(): lax.all_to_all(paired.reshape(chips, -1, HEAD_DIM), CHIPS, 0, 0, tiled=True)  20.5 us
    all_to_all x1, blocking collectives, per_device(): lax.all_to_all(jnp.broadcast_to(total[None], spread.shape), CHIPS, 0, 0,...  15.5 us
    all_to_all x1, blocking collectives, per_device(): fold_recv = lax.all_to_all(fold_send, RESP, 0, 0, tiled=True)  9.01 us
    ppermute x3, starting transfers between devices, shifted(): return lax.ppermute(x, axis, [(i, (i + by) % n) for i in range(n)])  5.28 us
    pallas_call x1, Pallas kernels, per_device(): pl.pallas_call(query_kernel, grid_spec=pltpu.PrefetchScalarGridSpec(num_s...  4.41 us
    pallas_call x1, Pallas kernels, per_device(): pl.pallas_call(reply_kernel, grid=(1,), in_specs=[pl.BlockSpec(memory_spa...  4.29 us
    ppermute x1, starting transfers between devices, per_device(): theirs = lax.ppermute(mine, 'core', PAIR)  3.24 us
  transfers between devices with their start and end apart: 9, of which 4 were waited for; matrix products, arithmetic and copies ran while one was open for 0% of the time, Pallas kernels for 21%

profile of v4, /device:TPU:1, one launch (start us, length us, event | category | flops | bytes accessed | tf_op | source)
XLA Modules:
  0.0 109.1 jit_solution(17443154200140795211)
XLA Ops:
  0.6 2.6 %front.1.p_low = bf16[64,1152]{1,0:T(8,128)(2,1)} custom-call(s32[1]{0:T(128)} %bitcast.spot, bf16[1,64,5120]{2,1,0:T(8,128)(2,1)} %p_hidden.1, bf16[1,64,5120]{2,1,0:T(8,128)(2,1)} %p_base.1, bf16[48,5120]{1,0:T(8,128)(2,1)} %bitcast.18, bf16[2,16,512]{2,1,0:T(8,128)(2,1)} %kv_up.7, f32[1152,128]{1,0:T(8,128)} %constant.26.clone.cos.r_cos.p_cos, ...), custom_call_target="tpu_custom_call" | custom-call | flops 31457280 | bytes 2000000 | tf_op jit(solution)/shard_map/front/pallas_call | solution.py:465
  3.2 3.7 %collective-permute-start.1 = (bf16[64,1152]{1,0:T(8,128)(2,1)}, bf16[64,1152]{1,0:T(8,128)(2,1)S(1)}, u32[]{:S(2)}, u32[]{:S(2)}) collective-permute-start(bf16[64,1152]{1,0:T(8,128)(2,1)} %front.1.p_low), channel_id=1, source_target_pairs={{0,4},{2,6},{4,0},{6,2},{1,5},{3,7},{5,1},{7,3},{8,12},{10,14},{12... | collective-permute-start | bytes 442376 | tf_op jit(solution)/shard_map/ppermute | solution.py:415
  6.9 1.6 %collective-permute-start = (bf16[64,1152]{1,0:T(8,128)(2,1)}, bf16[64,1152]{1,0:T(8,128)(2,1)S(1)}, u32[]{:S(2)}, u32[]{:S(2)}) collective-permute-start(bf16[64,1152]{1,0:T(8,128)(2,1)} %front.1.p_low), channel_id=1, source_target_pairs={{0,8},{8,0},{1,9},{9,1},{2,10},{10,2},{3,11},{11,3},{4,12},{12,4},... | collective-permute-start | bytes 442376 | tf_op jit(solution)/shard_map/ppermute | solution.py:485
  9.3 4.3 %reply.1 = (bf16[128,1152]{1,0:T(8,128)(2,1)}, bf16[192,128]{1,0:T(8,128)(2,1)}, bf16[192,128]{1,0:T(8,128)(2,1)}, bf16[48,192]{1,0:T(8,128)(2,1)}, bf16[32,192]{1,0:T(8,128)(2,1)}) custom-call(s32[1,1]{1,0:T(1,128)S(6)} %copy.38.lengths, bf16[64,1152]{1,0:T(8,128)(2,1)} %front.1.p_low, bf16[1,64,5120]{2,1,0:T(8,128)(2,1)} %p_out.3, ...), custom_call_target="tpu_custom_call" | custom-call | flops 188743680 | bytes 6000000 | tf_op jit(solution)/shard_map/reply/pallas_call | solution.py:488
  13.7 0.8 collective-permute-start.4
  14.5 0.7 collective-permute-start.2
  15.3 0.8 copy-done.11
  16.1 0.8 copy-done.12
  16.9 4.4 %query.1 = (bf16[192,2048]{1,0:T(8,128)(2,1)S(1)}, bf16[192,2048]{1,0:T(8,128)(2,1)S(1)}, bf16[192,2048]{1,0:T(8,128)(2,1)S(1)}, bf16[192,2048]{1,0:T(8,128)(2,1)S(1)}, bf16[16,128]{1,0:T(8,128)(2,1)}) custom-call(s32[1]{0:T(128)} %bitcast.spot, s32[1,1]{1,0:T(1,128)S(6)} %copy.38.lengths, bf16[192,128]{1,0:T(8,128)(2,1)S(1)} %copy-done.11, ...), custom_call_target="tpu_custom_call" | custom-call | flops 402653184 | bytes 8000000 | tf_op jit(solution)/shard_map/query/pallas_call | solution.py:542
  21.3 1.4 %collective-permute-done.2 = bf16[128,1152]{1,0:T(8,128)(2,1)S(1)} collective-permute-done((bf16[128,1152]{1,0:T(8,128)(2,1)S(1)}, bf16[128,1152]{1,0:T(8,128)(2,1)S(1)}, u32[]{:S(2)}, u32[]{:S(2)}) %collective-permute-start.2) | collective-permute-done | bytes 294944 | tf_op jit(solution)/shard_map/ppermute | solution.py:415
  22.9 2.5 %collective-permute-start.6 = (bf16[512,640]{1,0:T(8,128)(2,1)S(1)}, bf16[512,640]{1,0:T(8,128)(2,1)S(1)}, u32[]{:S(2)}, u32[]{:S(2)}) collective-permute-start(bf16[512,640]{1,0:T(8,128)(2,1)S(1)} %slice_dynamic-update-slice_fusion.key_a.value_a.low_a), channel_id=1, source_target_pairs={{0,1},{1,0},{2,3},{3,2},{4,5},{5,4},{6,7},{7,6},{8,9},{9,8},{10,11... | collective-permute-start | bytes 1966088 | tf_op jit(solution)/shard_map/ppermute | solution.py:587
  25.5 1.6 %collective-permute-done.6.key_b.value_b.low_b = bf16[512,640]{1,0:T(8,128)(2,1)S(1)} collective-permute-done((bf16[512,640]{1,0:T(8,128)(2,1)S(1)}, bf16[512,640]{1,0:T(8,128)(2,1)S(1)}, u32[]{:S(2)}, u32[]{:S(2)}) %collective-permute-start.6) | collective-permute-done | bytes 655392 | tf_op jit(solution)/shard_map/ppermute | solution.py:587
  27.1 14.0 %attend.2 = (bf16[1,64,4096]{2,1,0:T(8,128)(2,1)}, bf16[1,1,128,4096]{3,2,1,0:T(8,128)(2,1)}, bf16[36,16,128]{2,1,0:T(8,128)(2,1)S(1)}, f32[16,192]{1,0:T(8,128)...) custom-call(s32[1]{0:T(128)} %bitcast.spot, ...), custom_call_target="tpu_custom_call" | custom-call | flops 4831838208 | bytes 8000000 | tf_op jit(solution)/shard_map/attend/pallas_call | solution.py:637
  41.1 13.6 %attend.3 = (bf16[1,64,4096]{2,1,0:T(8,128)(2,1)}, bf16[1,1,128,4096]{3,2,1,0:T(8,128)(2,1)}, bf16[36,16,128]{2,1,0:T(8,128)(2,1)S(1)}, f32[16,192]{1,0:T(8,128)...) custom-call(s32[1]{0:T(128)} %bitcast.spot, ...), custom_call_target="tpu_custom_call", output_to_operand_aliasing={{0}: (27, {}), {1}: (28, {})} | custom-call | flops 4831838208 | bytes 8000000 | tf_op jit(solution)/shard_map/attend/pallas_call | solution.py:637
  54.7 9.0 %all_to_all.15.fold_recv = bf16[16,16,128]{2,1,0:T(8,128)(2,1)S(1)} all-to-all(bf16[16,16,128]{2,1,0:T(8,128)(2,1)S(1)} %get-tuple-element.79), channel_id=1, replica_groups=mesh['x'=4,'z_hi'=2,'z_lo'=2,'y'=4,'core'=2] {'z_lo','y','core'}, dimensions={0} | all-to-all | bytes 131072 | tf_op jit(solution)/shard_map/all_to_all | solution.py:686
  63.8 0.9 grads.1
  64.6 0.5 collective-permute-start.7
  65.1 1.5 %collective-permute-done.7 = bf16[128,16,128]{2,1,0:T(8,128)(2,1)S(1)} collective-permute-done((bf16[128,16,128]{2,1,0:T(8,128)(2,1)S(1)}, bf16[128,16,128]{2,1,0:T(8,128)(2,1)S(1)}, u32[]{:S(2)}, u32[]{:S(2)}) %collective-permute-start.7) | collective-permute-done | bytes 524320 | tf_op jit(solution)/shard_map/ppermute | solution.py:719
  66.6 0.1 add_convert_fusion
  66.8 20.5 %all_to_all.16 = bf16[64,32,128]{2,1,0:T(8,128)(2,1)S(1)} all-to-all(bf16[64,32,128]{2,1,0:T(8,128)(2,1)S(1)} %bitcast.17), channel_id=1, replica_groups=mesh['x'=4,'z_hi'=2,'z_lo'=2,'y'=4,'core'=2] {'x','z_hi','z_lo','y'}, dimensions={0} | all-to-all | bytes 1048576 | tf_op jit(solution)/shard_map/all_to_all | solution.py:721
  87.5 15.5 %all_to_all.17 = bf16[64,32,128]{2,1,0:T(8,128)(2,1)S(1)} all-to-all(bf16[64,32,128]{2,1,0:T(8,128)(2,1)S(1)} %broadcast_in_dim.10), channel_id=1, replica_groups=mesh['x'=4,'z_hi'=2,'z_lo'=2,'y'=4,'core'=2] {'x','z_hi','z_lo','y'}, dimensions={0} | all-to-all | bytes 1048576 | tf_op jit(solution)/shard_map/all_to_all | solution.py:725
  103.0 3.2 %collective-permute-start.8 = (bf16[128,16,128]{2,1,0:T(8,128)(2,1)S(1)}, bf16[128,16,128]{2,1,0:T(8,128)(2,1)S(1)}, u32[]{:S(2)}, u32[]{:S(2)}) collective-permute-start(bf16[128,16,128]{2,1,0:T(8,128)(2,1)S(1)} %bitcast.12), channel_id=1, source_target_pairs={{0,1},{1,0},{2,3},{3,2},{4,5},{5,4},{6,7},{7,6},{8,9},{9,8},{10,11... | collective-permute-start | bytes 1572872 | tf_op jit(solution)/shard_map/ppermute | solution.py:728
  106.3 1.5 %collective-permute-done.8.theirs = bf16[128,16,128]{2,1,0:T(8,128)(2,1)S(1)} collective-permute-done((bf16[128,16,128]{2,1,0:T(8,128)(2,1)S(1)}, bf16[128,16,128]{2,1,0:T(8,128)(2,1)S(1)}, u32[]{:S(2)}, u32[]{:S(2)}) %collective-permute-start.8) | collective-permute-done | bytes 524320 | tf_op jit(solution)/shard_map/ppermute | solution.py:728
  107.8 1.3 %unpack.1 = (f32[48,5120]{1,0:T(8,128)}, f32[16,4096]{1,0:T(8,128)}, f32[32,512]{1,0:T(8,128)}, f32[16,4096]{1,0:T(8,128)}, f32[16,5120]{1,0:T(8,128)}) custom-call(s32[1]{0:T(128)} %bitcast.spot, bf16[128,16,128]{2,1,0:T(8,128)(2,1)S(1)} %bitcast.13, bf16[128,16,128]{2,1,0:T(8,128)(2,1)S(1)} %collective-permute-done.8.theirs), custom_call_target="tpu_custom_call" | custom-call | bytes 3000000 | tf_op jit(solution)/shard_map/unpack/pallas_call | solution.py:731
  (57 shorter events, 0.6 us)
Async XLA Ops:
  3.2 10.4 %collective-permute-start.1 = (bf16[64,1152]{1,0:T(8,128)(2,1)}, bf16[64,1152]{1,0:T(8,128)(2,1)S(1)}, u32[]{:S(2)}, u32[]{:S(2)}) collective-permute-start(bf16[64,1152]{1,0:T(8,128)(2,1)} %front.1.p_low), channel_id=1, source_target_pairs={{0,4},{2,6},{4,0},{6,2},{1,5},{3,7},{5,1},{7,3},{8,12},{10,14},{12... | collective-permute-start | bytes 442376 | tf_op jit(solution)/shard_map/ppermute | solution.py:415
  6.9 6.7 %collective-permute-start = (bf16[64,1152]{1,0:T(8,128)(2,1)}, bf16[64,1152]{1,0:T(8,128)(2,1)S(1)}, u32[]{:S(2)}, u32[]{:S(2)}) collective-permute-start(bf16[64,1152]{1,0:T(8,128)(2,1)} %front.1.p_low), channel_id=1, source_target_pairs={{0,8},{8,0},{1,9},{9,1},{2,10},{10,2},{3,11},{11,3},{4,12},{12,4},... | collective-permute-start | bytes 442376 | tf_op jit(solution)/shard_map/ppermute | solution.py:485
  9.2 6.0 %copy-start = (f32[1152,128]{1,0:T(8,128)S(1)}, f32[1152,128]{1,0:T(8,128)}, u32[]{:S(2)}) copy-start(f32[1152,128]{1,0:T(8,128)} %constant.27.clone.sin.r_sin.p_sin) | copy-start | bytes 1769476
  9.2 6.0 %copy-start.1 = (f32[1152,128]{1,0:T(8,128)S(1)}, f32[1152,128]{1,0:T(8,128)}, u32[]{:S(2)}) copy-start(f32[1152,128]{1,0:T(8,128)} %constant.26.clone.cos.r_cos.p_cos) | copy-start | bytes 1769476
  9.3 6.0 %copy-start.6 = (bf16[1,64,5120]{2,1,0:T(8,128)(2,1)S(1)}, bf16[1,64,5120]{2,1,0:T(8,128)(2,1)}, u32[]{:S(2)}) copy-start(bf16[1,64,5120]{2,1,0:T(8,128)(2,1)} %p_base.1) | copy-start | bytes 1966084
  9.3 6.0 %copy-start.7 = (bf16[1,64,4096]{2,1,0:T(8,128)(2,1)S(1)}, bf16[1,64,4096]{2,1,0:T(8,128)(2,1)}, u32[]{:S(2)}) copy-start(bf16[1,64,4096]{2,1,0:T(8,128)(2,1)} %p_gbase.1) | copy-start | bytes 1572868
  9.3 6.0 %copy-start.9 = (bf16[16,4096]{1,0:T(8,128)(2,1)S(1)}, bf16[16,4096]{1,0:T(8,128)(2,1)}, u32[]{:S(2)}) copy-start(bf16[16,4096]{1,0:T(8,128)(2,1)} %q_up.5) | copy-start | bytes 393220
  9.3 5.9 %copy-start.10 = (bf16[4096,16]{0,1:T(8,128)(2,1)S(1)}, bf16[4096,16]{0,1:T(8,128)(2,1)}, u32[]{:S(2)}) copy-start(bf16[4096,16]{0,1:T(8,128)(2,1)} %param.26) | copy-start | bytes 393220
  13.7 7.7 %collective-permute-start.4 = (bf16[128,1152]{1,0:T(8,128)(2,1)S(1)}, bf16[128,1152]{1,0:T(8,128)(2,1)S(1)}, u32[]{:S(2)}, u32[]{:S(2)}) collective-permute-start(bf16[128,1152]{1,0:T(8,128)(2,1)S(1)} %constant_dynamic-update-slice_fusion), channel_id=1, source_target_pairs={{0,6},{2,0},{4,2},{6,4},{1,7},{3,1},{5,3},{7,5},{8,14},{10,8},{12,... | collective-permute-start | bytes 884744 | tf_op jit(solution)/shard_map/ppermute | solution.py:415
  14.5 8.2 %collective-permute-start.2 = (bf16[128,1152]{1,0:T(8,128)(2,1)S(1)}, bf16[128,1152]{1,0:T(8,128)(2,1)S(1)}, u32[]{:S(2)}, u32[]{:S(2)}) collective-permute-start(bf16[128,1152]{1,0:T(8,128)(2,1)S(1)} %constant_dynamic-update-slice_fusion), channel_id=1, source_target_pairs={{0,2},{2,4},{4,6},{6,0},{1,3},{3,5},{5,7},{7,1},{8,10},{10,12},{12... | collective-permute-start | bytes 884744 | tf_op jit(solution)/shard_map/ppermute | solution.py:415
  15.2 6.1 %collective-permute-start.3 = (bf16[64,1152]{1,0:T(8,128)(2,1)S(1)}, bf16[64,1152]{1,0:T(8,128)(2,1)S(1)}, u32[]{:S(2)}, u32[]{:S(2)}) collective-permute-start(bf16[64,1152]{1,0:T(8,128)(2,1)S(1)} %collective-permute-done.1), channel_id=1, source_target_pairs={{0,8},{8,0},{1,9},{9,1},{2,10},{10,2},{3,11},{11,3},{4,12},{12,4},... | collective-permute-start | bytes 442376 | tf_op jit(solution)/shard_map/ppermute | solution.py:420
  21.3 5.8 %copy-start.8 = (bf16[2,16,512]{2,1,0:T(8,128)(2,1)S(1)}, bf16[2,16,512]{2,1,0:T(8,128)(2,1)}, u32[]{:S(2)}) copy-start(bf16[2,16,512]{2,1,0:T(8,128)(2,1)} %kv_up.7) | copy-start | bytes 98308
  21.3 5.8 %copy-start.13 = (bf16[128,1152]{1,0:T(8,128)(2,1)S(1)}, bf16[128,1152]{1,0:T(8,128)(2,1)}, u32[]{:S(2)}) copy-start(bf16[128,1152]{1,0:T(8,128)(2,1)} %get-tuple-element.64.r_key.r_value.r_low) | copy-start | bytes 884740
  21.3 5.8 %copy-start.14 = (bf16[48,192]{1,0:T(8,128)(2,1)S(1)}, bf16[48,192]{1,0:T(8,128)(2,1)}, u32[]{:S(2)}) copy-start(bf16[48,192]{1,0:T(8,128)(2,1)} %get-tuple-element.65.low_t) | copy-start | bytes 55300
  21.3 5.8 %copy-start.15 = (bf16[32,192]{1,0:T(8,128)(2,1)S(1)}, bf16[32,192]{1,0:T(8,128)(2,1)}, u32[]{:S(2)}) copy-start(bf16[32,192]{1,0:T(8,128)(2,1)} %get-tuple-element.66.lowered_t) | copy-start | bytes 36868
  21.3 5.8 %copy-start.16 = (f32[64,1152]{1,0:T(8,128)S(1)}, f32[64,1152]{1,0:T(8,128)}, u32[]{:S(2)}) copy-start(f32[64,1152]{1,0:T(8,128)} %constant.29.clone.sin_t) | copy-start | bytes 884740
  22.9 4.2 %collective-permute-start.6 = (bf16[512,640]{1,0:T(8,128)(2,1)S(1)}, bf16[512,640]{1,0:T(8,128)(2,1)S(1)}, u32[]{:S(2)}, u32[]{:S(2)}) collective-permute-start(bf16[512,640]{1,0:T(8,128)(2,1)S(1)} %slice_dynamic-update-slice_fusion.key_a.value_a.low_a), channel_id=1, source_target_pairs={{0,1},{1,0},{2,3},{3,2},{4,5},{5,4},{6,7},{7,6},{8,9},{9,8},{10,11... | collective-permute-start | bytes 1966088 | tf_op jit(solution)/shard_map/ppermute | solution.py:587
  25.4 15.7 %collective-permute-start.5 = (bf16[512,512]{1,0:T(8,128)(2,1)S(1)}, bf16[512,512]{1,0:T(8,128)(2,1)S(1)}, u32[]{:S(2)}, u32[]{:S(2)}) collective-permute-start(bf16[512,512]{1,0:T(8,128)(2,1)S(1)} %slice_dynamic-update-slice_fusion.3.key_a.value_a), channel_id=1, source_target_pairs={{0,1},{1,0},{2,3},{3,2},{4,5},{5,4},{6,7},{7,6},{8,9},{9,8},{10,11... | collective-permute-start | bytes 1572872 | tf_op jit(solution)/shard_map/ppermute | solution.py:588
  41.1 22.6 %copy-start.2 = (bf16[1,1,128,5120]{3,2,1,0:T(8,128)(2,1)S(1)}, bf16[1,1,128,5120]{3,2,1,0:T(8,128)(2,1)}, u32[]{:S(2)}) copy-start(bf16[1,1,128,5120]{3,2,1,0:T(8,128)(2,1)} %r_hidden.3) | copy-start | bytes 3932164
  41.1 22.6 %copy-start.3 = (bf16[1,1,128,5120]{3,2,1,0:T(8,128)(2,1)S(1)}, bf16[1,1,128,5120]{3,2,1,0:T(8,128)(2,1)}, u32[]{:S(2)}) copy-start(bf16[1,1,128,5120]{3,2,1,0:T(8,128)(2,1)} %r_out.3) | copy-start | bytes 3932164
  41.1 22.6 %copy-start.4 = (bf16[1,64,5120]{2,1,0:T(8,128)(2,1)S(1)}, bf16[1,64,5120]{2,1,0:T(8,128)(2,1)}, u32[]{:S(2)}) copy-start(bf16[1,64,5120]{2,1,0:T(8,128)(2,1)} %p_hidden.1) | copy-start | bytes 1966084
  41.1 22.6 %copy-start.5 = (bf16[1,64,5120]{2,1,0:T(8,128)(2,1)S(1)}, bf16[1,64,5120]{2,1,0:T(8,128)(2,1)}, u32[]{:S(2)}) copy-start(bf16[1,64,5120]{2,1,0:T(8,128)(2,1)} %p_out.3) | copy-start | bytes 1966084
  64.6 2.0 %collective-permute-start.7 = (bf16[128,16,128]{2,1,0:T(8,128)(2,1)S(1)}, bf16[128,16,128]{2,1,0:T(8,128)(2,1)S(1)}, u32[]{:S(2)}, u32[]{:S(2)}) collective-permute-start(bf16[128,16,128]{2,1,0:T(8,128)(2,1)S(1)} %get-tuple-element.83), channel_id=1, source_target_pairs={{0,1},{1,0},{2,3},{3,2},{4,5},{5,4},{6,7},{7,6},{8,9},{9,8},{10,11... | collective-permute-start | bytes 1572872 | tf_op jit(solution)/shard_map/ppermute | solution.py:719
  103.0 4.8 %collective-permute-start.8 = (bf16[128,16,128]{2,1,0:T(8,128)(2,1)S(1)}, bf16[128,16,128]{2,1,0:T(8,128)(2,1)S(1)}, u32[]{:S(2)}, u32[]{:S(2)}) collective-permute-start(bf16[128,16,128]{2,1,0:T(8,128)(2,1)S(1)} %bitcast.12), channel_id=1, source_target_pairs={{0,1},{1,0},{2,3},{3,2},{4,5},{5,4},{6,7},{7,6},{8,9},{9,8},{10,11... | collective-permute-start | bytes 1572872 | tf_op jit(solution)/shard_map/ppermute | solution.py:728
  (4 other events, 11.8 us)

commit v5 on v4

--- a/solution.py
+++ b/solution.py
@@ -326,8 +326,10 @@
     fold_q[...] = folds[0]
     lifted[...] = folds[1]
     fk, fv = folds[2], folds[3]
-    fold_kv[:RANK, :] = fk
-    fold_kv[RANK:, :] = fv
+    if first:
+        fold_kv[:RANK, :] = fk
+        fold_kv[RANK:, :] = fv
+        return
     for r in range(prompt // pr):
         cols = slice(r * pr, (r + 1) * pr)
         fold_send[r] = jnp.concatenate([fk[:, cols], fv[:, cols]], axis=1).astype(BF16)

time: 110 us -> 108 us (0.982)
  Pallas kernels: 41 us -> 39.7 us
    pallas_call x2, Pallas kernels: 27.6 us -> 26.3 us  [attend(): pl.pallas_call(functools.partial(attend_kernel, first), grid_spec=pltpu.P...]
  transfers between devices with their start and end apart: 9 -> 9, of which waited for: 4 -> 4; matrix products, arithmetic and copies ran while one was open for 0% -> 0% of each run, Pallas kernels for 21% -> 20%
where the time goes in v5:
time: 108 us
  blocking collectives  45.1 us (42%)
  Pallas kernels  39.7 us (37%)
  starting transfers between devices  13.2 us (12%)
  waiting for transfers between devices  6.04 us (6%)
  local copies, waits for them, and re-layouts  1.93 us (2%)
  between operations  1.62 us (2%)
    pallas_call x2, Pallas kernels, attend(): pl.pallas_call(functools.partial(attend_kernel, first), grid_spec=pltpu.P...  26.3 us
    all_to_all x1, blocking collectives, per_device(): lax.all_to_all(paired.reshape(chips, -1, HEAD_DIM), CHIPS, 0, 0, tiled=True)  20.5 us
    all_to_all x1, blocking collectives, per_device(): lax.all_to_all(jnp.broadcast_to(total[None], spread.shape), CHIPS, 0, 0,...  15.5 us
    all_to_all x1, blocking collectives, per_device(): fold_recv = lax.all_to_all(fold_send, RESP, 0, 0, tiled=True)  9.02 us
    ppermute x3, starting transfers between devices, shifted(): return lax.ppermute(x, axis, [(i, (i + by) % n) for i in range(n)])  5.28 us
    pallas_call x1, Pallas kernels, per_device(): pl.pallas_call(query_kernel, grid_spec=pltpu.PrefetchScalarGridSpec(num_s...  4.41 us
    pallas_call x1, Pallas kernels, per_device(): pl.pallas_call(reply_kernel, grid=(1,), in_specs=[pl.BlockSpec(memory_spa...  4.29 us
    ppermute x1, starting transfers between devices, per_device(): theirs = lax.ppermute(mine, 'core', PAIR)  3.24 us
  transfers between devices with their start and end apart: 9, of which 4 were waited for; matrix products, arithmetic and copies ran while one was open for 0% of the time, Pallas kernels for 20%

profile of v5, /device:TPU:1, one launch (start us, length us, event | category | flops | bytes accessed | tf_op | source)
XLA Modules:
  0.0 107.9 jit_solution(13281189094815598107)
XLA Ops:
  0.6 2.6 %front.1.p_low = bf16[64,1152]{1,0:T(8,128)(2,1)} custom-call(s32[1]{0:T(128)} %bitcast.spot, bf16[1,64,5120]{2,1,0:T(8,128)(2,1)} %p_hidden.1, bf16[1,64,5120]{2,1,0:T(8,128)(2,1)} %p_base.1, bf16[48,5120]{1,0:T(8,128)(2,1)} %bitcast.18, bf16[2,16,512]{2,1,0:T(8,128)(2,1)} %kv_up.7, f32[1152,128]{1,0:T(8,128)} %constant.26.clone.cos.r_cos.p_cos, ...), custom_call_target="tpu_custom_call" | custom-call | flops 31457280 | bytes 2000000 | tf_op jit(solution)/shard_map/front/pallas_call | solution.py:467
  3.2 3.7 %collective-permute-start.1 = (bf16[64,1152]{1,0:T(8,128)(2,1)}, bf16[64,1152]{1,0:T(8,128)(2,1)S(1)}, u32[]{:S(2)}, u32[]{:S(2)}) collective-permute-start(bf16[64,1152]{1,0:T(8,128)(2,1)} %front.1.p_low), channel_id=1, source_target_pairs={{0,4},{2,6},{4,0},{6,2},{1,5},{3,7},{5,1},{7,3},{8,12},{10,14},{12... | collective-permute-start | bytes 442376 | tf_op jit(solution)/shard_map/ppermute | solution.py:417
  6.9 1.6 %collective-permute-start = (bf16[64,1152]{1,0:T(8,128)(2,1)}, bf16[64,1152]{1,0:T(8,128)(2,1)S(1)}, u32[]{:S(2)}, u32[]{:S(2)}) collective-permute-start(bf16[64,1152]{1,0:T(8,128)(2,1)} %front.1.p_low), channel_id=1, source_target_pairs={{0,8},{8,0},{1,9},{9,1},{2,10},{10,2},{3,11},{11,3},{4,12},{12,4},... | collective-permute-start | bytes 442376 | tf_op jit(solution)/shard_map/ppermute | solution.py:487
  9.3 4.3 %reply.1 = (bf16[128,1152]{1,0:T(8,128)(2,1)}, bf16[192,128]{1,0:T(8,128)(2,1)}, bf16[192,128]{1,0:T(8,128)(2,1)}, bf16[48,192]{1,0:T(8,128)(2,1)}, bf16[32,192]{1,0:T(8,128)(2,1)}) custom-call(s32[1,1]{1,0:T(1,128)S(6)} %copy.38.lengths, bf16[64,1152]{1,0:T(8,128)(2,1)} %front.1.p_low, bf16[1,64,5120]{2,1,0:T(8,128)(2,1)} %p_out.3, ...), custom_call_target="tpu_custom_call" | custom-call | flops 188743680 | bytes 6000000 | tf_op jit(solution)/shard_map/reply/pallas_call | solution.py:490
  13.7 0.8 collective-permute-start.4
  14.5 0.7 collective-permute-start.2
  15.3 0.8 copy-done.11
  16.1 0.8 copy-done.12
  16.9 4.4 %query.1 = (bf16[192,2048]{1,0:T(8,128)(2,1)S(1)}, bf16[192,2048]{1,0:T(8,128)(2,1)S(1)}, bf16[192,2048]{1,0:T(8,128)(2,1)S(1)}, bf16[192,2048]{1,0:T(8,128)(2,1)S(1)}, bf16[16,128]{1,0:T(8,128)(2,1)}) custom-call(s32[1]{0:T(128)} %bitcast.spot, s32[1,1]{1,0:T(1,128)S(6)} %copy.38.lengths, bf16[192,128]{1,0:T(8,128)(2,1)S(1)} %copy-done.11, ...), custom_call_target="tpu_custom_call" | custom-call | flops 402653184 | bytes 8000000 | tf_op jit(solution)/shard_map/query/pallas_call | solution.py:544
  21.3 1.4 %collective-permute-done.2 = bf16[128,1152]{1,0:T(8,128)(2,1)S(1)} collective-permute-done((bf16[128,1152]{1,0:T(8,128)(2,1)S(1)}, bf16[128,1152]{1,0:T(8,128)(2,1)S(1)}, u32[]{:S(2)}, u32[]{:S(2)}) %collective-permute-start.2) | collective-permute-done | bytes 294944 | tf_op jit(solution)/shard_map/ppermute | solution.py:417
  22.9 2.5 %collective-permute-start.6 = (bf16[512,640]{1,0:T(8,128)(2,1)S(1)}, bf16[512,640]{1,0:T(8,128)(2,1)S(1)}, u32[]{:S(2)}, u32[]{:S(2)}) collective-permute-start(bf16[512,640]{1,0:T(8,128)(2,1)S(1)} %slice_dynamic-update-slice_fusion.key_a.value_a.low_a), channel_id=1, source_target_pairs={{0,1},{1,0},{2,3},{3,2},{4,5},{5,4},{6,7},{7,6},{8,9},{9,8},{10,11... | collective-permute-start | bytes 1966088 | tf_op jit(solution)/shard_map/ppermute | solution.py:589
  25.5 1.6 %collective-permute-done.6.key_b.value_b.low_b = bf16[512,640]{1,0:T(8,128)(2,1)S(1)} collective-permute-done((bf16[512,640]{1,0:T(8,128)(2,1)S(1)}, bf16[512,640]{1,0:T(8,128)(2,1)S(1)}, u32[]{:S(2)}, u32[]{:S(2)}) %collective-permute-start.6) | collective-permute-done | bytes 655392 | tf_op jit(solution)/shard_map/ppermute | solution.py:589
  27.1 13.3 %attend.2 = (bf16[1,64,4096]{2,1,0:T(8,128)(2,1)}, bf16[1,1,128,4096]{3,2,1,0:T(8,128)(2,1)}, bf16[36,16,128]{2,1,0:T(8,128)(2,1)S(1)}, f32[16,192]{1,0:T(8,128)...) custom-call(s32[1]{0:T(128)} %bitcast.spot, ...), custom_call_target="tpu_custom_call" | custom-call | flops 4831838208 | bytes 8000000 | tf_op jit(solution)/shard_map/attend/pallas_call | solution.py:639
  40.5 13.0 %attend.3 = (bf16[1,64,4096]{2,1,0:T(8,128)(2,1)}, bf16[1,1,128,4096]{3,2,1,0:T(8,128)(2,1)}, bf16[36,16,128]{2,1,0:T(8,128)(2,1)S(1)}, f32[16,192]{1,0:T(8,128)...) custom-call(s32[1]{0:T(128)} %bitcast.spot, ...), custom_call_target="tpu_custom_call", output_to_operand_aliasing={{0}: (27, {}), {1}: (28, {})} | custom-call | flops 4831838208 | bytes 8000000 | tf_op jit(solution)/shard_map/attend/pallas_call | solution.py:639
  53.5 9.0 %all_to_all.15.fold_recv = bf16[16,16,128]{2,1,0:T(8,128)(2,1)S(1)} all-to-all(bf16[16,16,128]{2,1,0:T(8,128)(2,1)S(1)} %get-tuple-element.79), channel_id=1, replica_groups=mesh['x'=4,'z_hi'=2,'z_lo'=2,'y'=4,'core'=2] {'z_lo','y','core'}, dimensions={0} | all-to-all | bytes 131072 | tf_op jit(solution)/shard_map/all_to_all | solution.py:688
  62.5 0.9 grads.1
  63.4 0.5 collective-permute-start.7
  63.9 1.5 %collective-permute-done.7 = bf16[128,16,128]{2,1,0:T(8,128)(2,1)S(1)} collective-permute-done((bf16[128,16,128]{2,1,0:T(8,128)(2,1)S(1)}, bf16[128,16,128]{2,1,0:T(8,128)(2,1)S(1)}, u32[]{:S(2)}, u32[]{:S(2)}) %collective-permute-start.7) | collective-permute-done | bytes 524320 | tf_op jit(solution)/shard_map/ppermute | solution.py:721
  65.4 0.1 add_convert_fusion
  65.5 20.5 %all_to_all.16 = bf16[64,32,128]{2,1,0:T(8,128)(2,1)S(1)} all-to-all(bf16[64,32,128]{2,1,0:T(8,128)(2,1)S(1)} %bitcast.17), channel_id=1, replica_groups=mesh['x'=4,'z_hi'=2,'z_lo'=2,'y'=4,'core'=2] {'x','z_hi','z_lo','y'}, dimensions={0} | all-to-all | bytes 1048576 | tf_op jit(solution)/shard_map/all_to_all | solution.py:723
  86.2 15.5 %all_to_all.17 = bf16[64,32,128]{2,1,0:T(8,128)(2,1)S(1)} all-to-all(bf16[64,32,128]{2,1,0:T(8,128)(2,1)S(1)} %broadcast_in_dim.10), channel_id=1, replica_groups=mesh['x'=4,'z_hi'=2,'z_lo'=2,'y'=4,'core'=2] {'x','z_hi','z_lo','y'}, dimensions={0} | all-to-all | bytes 1048576 | tf_op jit(solution)/shard_map/all_to_all | solution.py:727
  101.8 3.2 %collective-permute-start.8 = (bf16[128,16,128]{2,1,0:T(8,128)(2,1)S(1)}, bf16[128,16,128]{2,1,0:T(8,128)(2,1)S(1)}, u32[]{:S(2)}, u32[]{:S(2)}) collective-permute-start(bf16[128,16,128]{2,1,0:T(8,128)(2,1)S(1)} %bitcast.12), channel_id=1, source_target_pairs={{0,1},{1,0},{2,3},{3,2},{4,5},{5,4},{6,7},{7,6},{8,9},{9,8},{10,11... | collective-permute-start | bytes 1572872 | tf_op jit(solution)/shard_map/ppermute | solution.py:730
  105.0 1.5 %collective-permute-done.8.theirs = bf16[128,16,128]{2,1,0:T(8,128)(2,1)S(1)} collective-permute-done((bf16[128,16,128]{2,1,0:T(8,128)(2,1)S(1)}, bf16[128,16,128]{2,1,0:T(8,128)(2,1)S(1)}, u32[]{:S(2)}, u32[]{:S(2)}) %collective-permute-start.8) | collective-permute-done | bytes 524320 | tf_op jit(solution)/shard_map/ppermute | solution.py:730
  106.6 1.3 %unpack.1 = (f32[48,5120]{1,0:T(8,128)}, f32[16,4096]{1,0:T(8,128)}, f32[32,512]{1,0:T(8,128)}, f32[16,4096]{1,0:T(8,128)}, f32[16,5120]{1,0:T(8,128)}) custom-call(s32[1]{0:T(128)} %bitcast.spot, bf16[128,16,128]{2,1,0:T(8,128)(2,1)S(1)} %bitcast.13, bf16[128,16,128]{2,1,0:T(8,128)(2,1)S(1)} %collective-permute-done.8.theirs), custom_call_target="tpu_custom_call" | custom-call | bytes 3000000 | tf_op jit(solution)/shard_map/unpack/pallas_call | solution.py:733
  (57 shorter events, 0.6 us)
Async XLA Ops:
  3.2 10.4 %collective-permute-start.1 = (bf16[64,1152]{1,0:T(8,128)(2,1)}, bf16[64,1152]{1,0:T(8,128)(2,1)S(1)}, u32[]{:S(2)}, u32[]{:S(2)}) collective-permute-start(bf16[64,1152]{1,0:T(8,128)(2,1)} %front.1.p_low), channel_id=1, source_target_pairs={{0,4},{2,6},{4,0},{6,2},{1,5},{3,7},{5,1},{7,3},{8,12},{10,14},{12... | collective-permute-start | bytes 442376 | tf_op jit(solution)/shard_map/ppermute | solution.py:417
  6.9 6.7 %collective-permute-start = (bf16[64,1152]{1,0:T(8,128)(2,1)}, bf16[64,1152]{1,0:T(8,128)(2,1)S(1)}, u32[]{:S(2)}, u32[]{:S(2)}) collective-permute-start(bf16[64,1152]{1,0:T(8,128)(2,1)} %front.1.p_low), channel_id=1, source_target_pairs={{0,8},{8,0},{1,9},{9,1},{2,10},{10,2},{3,11},{11,3},{4,12},{12,4},... | collective-permute-start | bytes 442376 | tf_op jit(solution)/shard_map/ppermute | solution.py:487
  9.2 6.0 %copy-start = (f32[1152,128]{1,0:T(8,128)S(1)}, f32[1152,128]{1,0:T(8,128)}, u32[]{:S(2)}) copy-start(f32[1152,128]{1,0:T(8,128)} %constant.27.clone.sin.r_sin.p_sin) | copy-start | bytes 1769476
  9.2 6.0 %copy-start.1 = (f32[1152,128]{1,0:T(8,128)S(1)}, f32[1152,128]{1,0:T(8,128)}, u32[]{:S(2)}) copy-start(f32[1152,128]{1,0:T(8,128)} %constant.26.clone.cos.r_cos.p_cos) | copy-start | bytes 1769476
  9.3 6.0 %copy-start.6 = (bf16[1,64,5120]{2,1,0:T(8,128)(2,1)S(1)}, bf16[1,64,5120]{2,1,0:T(8,128)(2,1)}, u32[]{:S(2)}) copy-start(bf16[1,64,5120]{2,1,0:T(8,128)(2,1)} %p_base.1) | copy-start | bytes 1966084
  9.3 6.0 %copy-start.7 = (bf16[1,64,4096]{2,1,0:T(8,128)(2,1)S(1)}, bf16[1,64,4096]{2,1,0:T(8,128)(2,1)}, u32[]{:S(2)}) copy-start(bf16[1,64,4096]{2,1,0:T(8,128)(2,1)} %p_gbase.1) | copy-start | bytes 1572868
  9.3 6.0 %copy-start.9 = (bf16[16,4096]{1,0:T(8,128)(2,1)S(1)}, bf16[16,4096]{1,0:T(8,128)(2,1)}, u32[]{:S(2)}) copy-start(bf16[16,4096]{1,0:T(8,128)(2,1)} %q_up.5) | copy-start | bytes 393220
  9.3 5.9 %copy-start.10 = (bf16[4096,16]{0,1:T(8,128)(2,1)S(1)}, bf16[4096,16]{0,1:T(8,128)(2,1)}, u32[]{:S(2)}) copy-start(bf16[4096,16]{0,1:T(8,128)(2,1)} %param.26) | copy-start | bytes 393220
  13.7 7.7 %collective-permute-start.4 = (bf16[128,1152]{1,0:T(8,128)(2,1)S(1)}, bf16[128,1152]{1,0:T(8,128)(2,1)S(1)}, u32[]{:S(2)}, u32[]{:S(2)}) collective-permute-start(bf16[128,1152]{1,0:T(8,128)(2,1)S(1)} %constant_dynamic-update-slice_fusion), channel_id=1, source_target_pairs={{0,6},{2,0},{4,2},{6,4},{1,7},{3,1},{5,3},{7,5},{8,14},{10,8},{12,... | collective-permute-start | bytes 884744 | tf_op jit(solution)/shard_map/ppermute | solution.py:417
  14.5 8.2 %collective-permute-start.2 = (bf16[128,1152]{1,0:T(8,128)(2,1)S(1)}, bf16[128,1152]{1,0:T(8,128)(2,1)S(1)}, u32[]{:S(2)}, u32[]{:S(2)}) collective-permute-start(bf16[128,1152]{1,0:T(8,128)(2,1)S(1)} %constant_dynamic-update-slice_fusion), channel_id=1, source_target_pairs={{0,2},{2,4},{4,6},{6,0},{1,3},{3,5},{5,7},{7,1},{8,10},{10,12},{12... | collective-permute-start | bytes 884744 | tf_op jit(solution)/shard_map/ppermute | solution.py:417
  15.2 6.1 %collective-permute-start.3 = (bf16[64,1152]{1,0:T(8,128)(2,1)S(1)}, bf16[64,1152]{1,0:T(8,128)(2,1)S(1)}, u32[]{:S(2)}, u32[]{:S(2)}) collective-permute-start(bf16[64,1152]{1,0:T(8,128)(2,1)S(1)} %collective-permute-done.1), channel_id=1, source_target_pairs={{0,8},{8,0},{1,9},{9,1},{2,10},{10,2},{3,11},{11,3},{4,12},{12,4},... | collective-permute-start | bytes 442376 | tf_op jit(solution)/shard_map/ppermute | solution.py:422
  21.3 5.8 %copy-start.8 = (bf16[2,16,512]{2,1,0:T(8,128)(2,1)S(1)}, bf16[2,16,512]{2,1,0:T(8,128)(2,1)}, u32[]{:S(2)}) copy-start(bf16[2,16,512]{2,1,0:T(8,128)(2,1)} %kv_up.7) | copy-start | bytes 98308
  21.3 5.8 %copy-start.13 = (bf16[128,1152]{1,0:T(8,128)(2,1)S(1)}, bf16[128,1152]{1,0:T(8,128)(2,1)}, u32[]{:S(2)}) copy-start(bf16[128,1152]{1,0:T(8,128)(2,1)} %get-tuple-element.64.r_key.r_value.r_low) | copy-start | bytes 884740
  21.3 5.8 %copy-start.14 = (bf16[48,192]{1,0:T(8,128)(2,1)S(1)}, bf16[48,192]{1,0:T(8,128)(2,1)}, u32[]{:S(2)}) copy-start(bf16[48,192]{1,0:T(8,128)(2,1)} %get-tuple-element.65.low_t) | copy-start | bytes 55300
  21.3 5.8 %copy-start.15 = (bf16[32,192]{1,0:T(8,128)(2,1)S(1)}, bf16[32,192]{1,0:T(8,128)(2,1)}, u32[]{:S(2)}) copy-start(bf16[32,192]{1,0:T(8,128)(2,1)} %get-tuple-element.66.lowered_t) | copy-start | bytes 36868
  21.3 5.8 %copy-start.16 = (f32[64,1152]{1,0:T(8,128)S(1)}, f32[64,1152]{1,0:T(8,128)}, u32[]{:S(2)}) copy-start(f32[64,1152]{1,0:T(8,128)} %constant.29.clone.sin_t) | copy-start | bytes 884740
  22.9 4.2 %collective-permute-start.6 = (bf16[512,640]{1,0:T(8,128)(2,1)S(1)}, bf16[512,640]{1,0:T(8,128)(2,1)S(1)}, u32[]{:S(2)}, u32[]{:S(2)}) collective-permute-start(bf16[512,640]{1,0:T(8,128)(2,1)S(1)} %slice_dynamic-update-slice_fusion.key_a.value_a.low_a), channel_id=1, source_target_pairs={{0,1},{1,0},{2,3},{3,2},{4,5},{5,4},{6,7},{7,6},{8,9},{9,8},{10,11... | collective-permute-start | bytes 1966088 | tf_op jit(solution)/shard_map/ppermute | solution.py:589
  25.4 15.0 %collective-permute-start.5 = (bf16[512,512]{1,0:T(8,128)(2,1)S(1)}, bf16[512,512]{1,0:T(8,128)(2,1)S(1)}, u32[]{:S(2)}, u32[]{:S(2)}) collective-permute-start(bf16[512,512]{1,0:T(8,128)(2,1)S(1)} %slice_dynamic-update-slice_fusion.3.key_a.value_a), channel_id=1, source_target_pairs={{0,1},{1,0},{2,3},{3,2},{4,5},{5,4},{6,7},{7,6},{8,9},{9,8},{10,11... | collective-permute-start | bytes 1572872 | tf_op jit(solution)/shard_map/ppermute | solution.py:590
  40.4 22.1 %copy-start.2 = (bf16[1,1,128,5120]{3,2,1,0:T(8,128)(2,1)S(1)}, bf16[1,1,128,5120]{3,2,1,0:T(8,128)(2,1)}, u32[]{:S(2)}) copy-start(bf16[1,1,128,5120]{3,2,1,0:T(8,128)(2,1)} %r_hidden.3) | copy-start | bytes 3932164
  40.4 22.1 %copy-start.3 = (bf16[1,1,128,5120]{3,2,1,0:T(8,128)(2,1)S(1)}, bf16[1,1,128,5120]{3,2,1,0:T(8,128)(2,1)}, u32[]{:S(2)}) copy-start(bf16[1,1,128,5120]{3,2,1,0:T(8,128)(2,1)} %r_out.3) | copy-start | bytes 3932164
  40.4 22.1 %copy-start.4 = (bf16[1,64,5120]{2,1,0:T(8,128)(2,1)S(1)}, bf16[1,64,5120]{2,1,0:T(8,128)(2,1)}, u32[]{:S(2)}) copy-start(bf16[1,64,5120]{2,1,0:T(8,128)(2,1)} %p_hidden.1) | copy-start | bytes 1966084
  40.5 22.1 %copy-start.5 = (bf16[1,64,5120]{2,1,0:T(8,128)(2,1)S(1)}, bf16[1,64,5120]{2,1,0:T(8,128)(2,1)}, u32[]{:S(2)}) copy-start(bf16[1,64,5120]{2,1,0:T(8,128)(2,1)} %p_out.3) | copy-start | bytes 1966084
  63.4 2.0 %collective-permute-start.7 = (bf16[128,16,128]{2,1,0:T(8,128)(2,1)S(1)}, bf16[128,16,128]{2,1,0:T(8,128)(2,1)S(1)}, u32[]{:S(2)}, u32[]{:S(2)}) collective-permute-start(bf16[128,16,128]{2,1,0:T(8,128)(2,1)S(1)} %get-tuple-element.83), channel_id=1, source_target_pairs={{0,1},{1,0},{2,3},{3,2},{4,5},{5,4},{6,7},{7,6},{8,9},{9,8},{10,11... | collective-permute-start | bytes 1572872 | tf_op jit(solution)/shard_map/ppermute | solution.py:721
  101.8 4.8 %collective-permute-start.8 = (bf16[128,16,128]{2,1,0:T(8,128)(2,1)S(1)}, bf16[128,16,128]{2,1,0:T(8,128)(2,1)S(1)}, u32[]{:S(2)}, u32[]{:S(2)}) collective-permute-start(bf16[128,16,128]{2,1,0:T(8,128)(2,1)S(1)} %bitcast.12), channel_id=1, source_target_pairs={{0,1},{1,0},{2,3},{3,2},{4,5},{5,4},{6,7},{7,6},{8,9},{9,8},{10,11... | collective-permute-start | bytes 1572872 | tf_op jit(solution)/shard_map/ppermute | solution.py:730
  (4 other events, 11.8 us)
